TPU v7x, 32 devices: a whole 2x2x4 slice. The times are simulated.
32 devices in a mesh: expert: 16 (over z, y, core), edata: 2 (over x).
Axes of the slice: x: 2, y: 2, z: 4, core: 2. Of those that a mesh axis runs over, the one named last changes fastest.
Arguments:
- tokens: bfloat16 [1024, 2048], P(('expert', 'edata')), may hold values from -6 to 6
- out_grad: bfloat16 [1024, 2048], P(('expert', 'edata')), may hold values from -6 to 6
- routes: int32 [1024, 8], P(('expert', 'edata')), may hold values from 0 to 15, as said below
- gate_codes: int32 [1024, 8], P(('expert', 'edata')), may hold values from 1 to 4095
- w_gate: bfloat16 [16, 2048, 768], P('expert'), may hold values from -0.125 to 0.125
- w_up: bfloat16 [16, 2048, 768], P('expert'), may hold values from -0.125 to 0.125
- w_down: bfloat16 [16, 768, 2048], P('expert'), may hold values from -0.21875 to 0.21875
Outputs:
- mixed: bfloat16 [1024, 2048], P(('expert', 'edata'))
- input_grad: bfloat16 [1024, 2048], P(('expert', 'edata'))
- grad_down: float32 [2048, 16, 768], P('edata', 'expert')
Inputs may be any that keep to these rules, and one draw needn't show every extreme that they name: `routes`: each token names 8 different experts. For each index of edata one expert, drawn anew in each draw, is named by exactly 32 of the 32 tokens of every device of that index of edata; any other expert is named by at most (15) tokens of one device.
All inputs are finite; a program needn't handle non-finite values.
Results may differ from a plain program's by a relative error of at most 0.017.
Values may be sent and summed in bfloat16 or wider, within the bound.
No kernel may reach another device: no remote copies, remote signals or barrier semaphores. Data moves between devices by JAX's collectives and lax.ppermute only.
A program may use at most 128 MiB of HBM per device.

v0:
```python
import jax
import jax.numpy as jnp
from jax import lax
from jax.sharding import PartitionSpec as P

BLOCK = 128


def take_rows(source, row_ids, row_limit):
    is_valid = row_ids < row_limit
    safe_rows = jnp.minimum(row_ids, row_limit - 1)
    return jnp.where(
        is_valid[:, None], jnp.take(source, safe_rows, axis=0), jnp.zeros((), source.dtype)
    )


def expert_block(rows_in, grads_in, gate_mat, up_mat, down_mat):
    gate_pre = jnp.dot(rows_in, gate_mat, preferred_element_type=jnp.float32)
    up_pre = jnp.dot(rows_in, up_mat, preferred_element_type=jnp.float32)
    sig_gate = jax.nn.sigmoid(gate_pre)
    act_gate = gate_pre * sig_gate
    hidden_act = (act_gate * up_pre).astype(jnp.bfloat16)
    expert_out = jnp.dot(hidden_act, down_mat, preferred_element_type=jnp.float32).astype(
        jnp.bfloat16
    )
    grad_hidden = jnp.einsum("rd,fd->rf", grads_in, down_mat, preferred_element_type=jnp.float32)
    grad_gate_pre = (grad_hidden * up_pre * sig_gate * (1.0 + gate_pre * (1.0 - sig_gate))).astype(
        jnp.bfloat16
    )
    grad_up_pre = (grad_hidden * act_gate).astype(jnp.bfloat16)
    grad_rows = (
        jnp.einsum("rf,df->rd", grad_gate_pre, gate_mat, preferred_element_type=jnp.float32)
        + jnp.einsum("rf,df->rd", grad_up_pre, up_mat, preferred_element_type=jnp.float32)
    ).astype(jnp.bfloat16)
    return (expert_out, grad_rows, hidden_act)


def expert_sums(rows_do, rows_hidden, rows_owner):
    keep_mask = (rows_owner == 0).astype(jnp.bfloat16)
    terms = [
        jnp.einsum(
            "rd,rf->df", rows_do, rows_hidden * keep_mask, preferred_element_type=jnp.float32
        )
    ]
    return jnp.stack(terms, axis=1)


def shards(tokens, out_grad, routes, gate_codes, w_gate, w_up, w_down):
    tok_rows, model_width = tokens.shape
    top_count = routes.shape[1]
    local_experts = w_gate.shape[0]
    hidden_units = w_gate.shape[2]
    n_expert = lax.axis_size("expert")
    all_experts = local_experts * n_expert
    capacity = 2 * tok_rows * top_count // all_experts
    routed = tok_rows * top_count
    buffer_rows = all_experts * capacity
    gate_float = gate_codes.astype(jnp.float32)
    gate_values = gate_float / jnp.sum(gate_float, axis=1, keepdims=True)
    scaled = (
        (gate_values[:, :, None] * out_grad[:, None, :].astype(jnp.float32))
        .astype(jnp.bfloat16)
        .reshape(routed, model_width)
    )
    flat_expert = routes.reshape(routed)
    onehot = (flat_expert[:, None] == jnp.arange(all_experts, dtype=jnp.int32)[None, :]).astype(
        jnp.int32
    )
    before = jnp.cumsum(onehot, axis=0) - onehot
    slot_of = jnp.sum(before * onehot, axis=1)
    counts = jnp.sum(onehot, axis=0)
    target = flat_expert * capacity + slot_of
    owner_row = (
        jnp.full((buffer_rows,), routed, jnp.int32)
        .at[target]
        .set(jnp.arange(routed, dtype=jnp.int32))
    )
    token_of = jnp.where(owner_row < routed, owner_row // top_count, tok_rows)
    send_x = take_rows(tokens, token_of, tok_rows).reshape(all_experts, capacity, model_width)
    send_do = take_rows(scaled, owner_row, routed).reshape(all_experts, capacity, model_width)
    send_count = counts.astype(jnp.bfloat16).reshape(all_experts, 1)
    recv_x, recv_do, recv_count = (
        lax.all_to_all(send_x, "expert", split_axis=0, concat_axis=0, tiled=True),
        lax.all_to_all(send_do, "expert", split_axis=0, concat_axis=0, tiled=True),
        lax.all_to_all(send_count, "expert", split_axis=0, concat_axis=0, tiled=True),
    )
    work_x, work_do, work_count = (recv_x, recv_do, recv_count)
    count_grid = work_count.astype(jnp.int32)
    slot_ids = jnp.arange(capacity, dtype=jnp.int32)
    is_valid = slot_ids[None, None, :] < count_grid[:, :, None]
    per_expert = jnp.sum(count_grid, axis=0)
    padded = (per_expert + BLOCK - 1) // BLOCK * BLOCK
    begins = jnp.cumsum(padded) - padded
    earlier = jnp.cumsum(count_grid, axis=0) - count_grid
    block_count = buffer_rows // BLOCK + local_experts
    slot_total = block_count * BLOCK
    position = jnp.where(
        is_valid, begins[None, :, None] + earlier[:, :, None] + slot_ids[None, None, :], slot_total
    ).reshape(buffer_rows)
    source_of = (
        jnp.full((slot_total,), buffer_rows, jnp.int32)
        .at[position]
        .set(jnp.arange(buffer_rows, dtype=jnp.int32), mode="drop")
    )
    used_blocks = jnp.sum(padded) // BLOCK
    block_starts = jnp.arange(block_count, dtype=jnp.int32) * BLOCK
    block_expert = jnp.clip(
        jnp.sum((begins[None, :] <= block_starts[:, None]).astype(jnp.int32), axis=1) - 1,
        0,
        local_experts - 1,
    )
    comp_x = take_rows(work_x.reshape(buffer_rows, model_width), source_of, buffer_rows)
    comp_do = take_rows(work_do.reshape(buffer_rows, model_width), source_of, buffer_rows)
    zero_rows = jnp.zeros((slot_total, model_width), jnp.bfloat16)
    zero_hidden = jnp.zeros((slot_total, hidden_units), jnp.bfloat16)

    def block_step(block_id, loop_state):
        out_rows, grad_out, comp_hidden = loop_state
        offset = block_id * BLOCK
        rows_in = lax.dynamic_slice_in_dim(comp_x, offset, BLOCK, 0)
        grads_in = lax.dynamic_slice_in_dim(comp_do, offset, BLOCK, 0)
        expert_id = lax.dynamic_index_in_dim(block_expert, block_id, 0, keepdims=False)
        gate_mat = lax.dynamic_index_in_dim(w_gate, expert_id, 0, keepdims=False)
        up_mat = lax.dynamic_index_in_dim(w_up, expert_id, 0, keepdims=False)
        down_mat = lax.dynamic_index_in_dim(w_down, expert_id, 0, keepdims=False)
        expert_out, grad_rows, hidden_act = expert_block(
            rows_in, grads_in, gate_mat, up_mat, down_mat
        )
        out_rows = lax.dynamic_update_slice_in_dim(out_rows, expert_out, offset, 0)
        grad_out = lax.dynamic_update_slice_in_dim(grad_out, grad_rows, offset, 0)
        comp_hidden = lax.dynamic_update_slice_in_dim(comp_hidden, hidden_act, offset, 0)
        return (out_rows, grad_out, comp_hidden)

    out_rows, grad_out, comp_hidden = lax.fori_loop(
        0, used_blocks, block_step, (zero_rows, zero_rows, zero_hidden)
    )
    slot_owner = jnp.repeat(block_expert, BLOCK)
    partial_down = expert_sums(comp_do, comp_hidden, slot_owner[:, None])
    grad_down = lax.psum_scatter(
        partial_down.astype(jnp.bfloat16), "edata", scatter_dimension=0, tiled=True
    ).astype(jnp.float32)
    ret_o = take_rows(out_rows, position, slot_total).reshape(all_experts, capacity, model_width)
    ret_dx = take_rows(grad_out, position, slot_total).reshape(all_experts, capacity, model_width)
    home_o, home_dx = (
        lax.all_to_all(ret_o, "expert", split_axis=0, concat_axis=0, tiled=True),
        lax.all_to_all(ret_dx, "expert", split_axis=0, concat_axis=0, tiled=True),
    )
    rows_out = jnp.take(home_o.reshape(buffer_rows, model_width), target, axis=0).reshape(
        tok_rows, top_count, model_width
    )
    rows_grad = jnp.take(home_dx.reshape(buffer_rows, model_width), target, axis=0).reshape(
        tok_rows, top_count, model_width
    )
    mixed = jnp.sum(gate_values[:, :, None] * rows_out.astype(jnp.float32), axis=1).astype(
        jnp.bfloat16
    )
    input_grad = jnp.sum(rows_grad.astype(jnp.float32), axis=1).astype(jnp.bfloat16)
    return (mixed, input_grad, grad_down)


def solution(mesh):
    placed = (
        P(("expert", "edata"), None),
        P(("expert", "edata"), None),
        P(("expert", "edata"), None),
        P(("expert", "edata"), None),
        P("expert", None, None),
        P("expert", None, None),
        P("expert", None, None),
    )
    return jax.shard_map(
        shards,
        mesh=mesh,
        in_specs=placed,
        out_specs=(
            P(("expert", "edata"), None),
            P(("expert", "edata"), None),
            P("edata", "expert", None),
        ),
        check_vma=False,
    )
```

profile of v0, /device:TPU:15, one launch (start us, length us, event | category | flops | bytes accessed | tf_op | source)
XLA Modules:
  0.0 331.4 jit_solution(18023786229771164762)
XLA Ops:
  7.2 0.8 copy.14
  8.2 0.6 reduce-window.9
  9.1 0.7 copy.17
  9.8 6.6 %all-to-all-start = ((bf16[16,1,1]{2,1,0:T(2,128)(2,1)}), bf16[16,1,1]{2,1,0:T(2,128)(2,1)S(1)}, u32[]{:S(2)}, u32[]{:S(2)}) async-start(bf16[16,1,1]{2,1,0:T(2,128)(2,1)} %copy.17), calls=%async_computation | async-start | bytes 16384 | tf_op jit(solution)/shard_map/all_to_all | solution.py:85
  16.4 0.7 broadcast_multiply_fusion
  17.3 1.4 scatter_custom_fusion.1
  18.9 2.5 gather_fusion
  21.4 1.7 select_select_fusion.5
  23.1 6.2 %all-to-all-start.1 = ((bf16[16,32,2048]{2,1,0:T(8,128)(2,1)}), bf16[16,32,2048]{2,1,0:T(8,128)(2,1)S(1)}, u32[]{:S(2)}, u32[]{:S(2)}) async-start(bf16[16,32,2048]{2,1,0:T(8,128)(2,1)} %select_select_fusion.5), calls=%async_computation.1 | async-start | bytes 4194304 | tf_op jit(solution)/shard_map/all_to_all | solution.py:83
  29.9 3.3 gather_fusion.1
  33.1 3.2 select_select_fusion.4
  36.4 40.3 %all-to-all-done.1 = bf16[16,32,2048]{2,1,0:T(8,128)(2,1)S(1)} async-done(((bf16[16,32,2048]{2,1,0:T(8,128)(2,1)}), bf16[16,32,2048]{2,1,0:T(8,128)(2,1)S(1)}, u32[]{:S(2)}, u32[]{:S(2)}) %all-to-all-start.1) | async-done | bytes 2097184 | tf_op jit(solution)/shard_map/all_to_all | solution.py:83
  76.6 4.9 %all-to-all-start.2 = ((bf16[16,32,2048]{2,1,0:T(8,128)(2,1)}), bf16[16,32,2048]{2,1,0:T(8,128)(2,1)}, u32[]{:S(2)}, u32[]{:S(2)}) async-start(bf16[16,32,2048]{2,1,0:T(8,128)(2,1)} %select_select_fusion.4), calls=%async_computation.2 | async-start | bytes 4194304 | tf_op jit(solution)/shard_map/all_to_all | solution.py:84
  81.6 0.9 convert_reduce_fusion.2
  84.0 2.4 scatter_custom_fusion
  86.5 4.1 %gather_fusion.2 = bf16[640,2048]{1,0:T(8,128)(2,1)} fusion(bf16[512,2048]{1,0:T(8,128)(2,1)S(1)} %bitcast.94, s32[1024]{0:T(1024)S(1)} %pad_clamp_fusion.3), kind=kCustom, calls=%fused_computation.clone | custom fusion | bytes 5245440 | tf_op jit(solution)/shard_map/jit(_take)/gather | solution.py:13
  90.6 38.5 %all-to-all-done.2 = bf16[16,32,2048]{2,1,0:T(8,128)(2,1)} async-done(((bf16[16,32,2048]{2,1,0:T(8,128)(2,1)}), bf16[16,32,2048]{2,1,0:T(8,128)(2,1)}, u32[]{:S(2)}, u32[]{:S(2)}) %all-to-all-start.2) | async-done | bytes 2097184 | tf_op jit(solution)/shard_map/all_to_all | solution.py:84
  129.1 8.9 %gather_fusion.3 = bf16[640,2048]{1,0:T(8,128)(2,1)} fusion(bf16[512,2048]{1,0:T(8,128)(2,1)} %bitcast.14, s32[1024]{0:T(1024)S(1)} %pad_clamp_fusion.3), kind=kCustom, calls=%fused_computation.3.clone | custom fusion | bytes 5245440 | tf_op jit(solution)/shard_map/jit(_take)/gather | solution.py:13
  138.0 4.2 %select_select_fusion = (bf16[640,2048]{1,0:T(8,128)(2,1)}, bf16[640,2048]{1,0:T(8,128)(2,1)}) fusion(bf16[640,2048]{1,0:T(8,128)(2,1)} %gather_fusion.3, pred[640]{0:T(1024)(128)(4,1)S(1)} %get-tuple-element.127, pred[640]{0:T(1024)(128)(4,1)S(1)} %get-tuple-element.126, bf16[640,2048]{1,0:T(8,128)(2,1)S(1)} %copy-done.5), kind=kLoop, calls=%fused_computation.44 | loop fusion | flops 5242880 | bytes 10487040 | tf_op jit(solution)/shard_map/jit(_where)/select_n | solution.py:12
  142.2 1.8 broadcast_in_dim.142
  144.0 1.8 broadcast_in_dim.142.clone
  145.9 1.0 broadcast_in_dim.143
  146.9 22.5 %while.15 = (s32[]{:T(128)}, bf16[640,2048]{1,0:T(8,128)(2,1)}, bf16[640,2048]{1,0:T(8,128)(2,1)}, bf16[640,768]{1,0:T(8,128)(2,1)}, s32[]{:T(128)}, /*index=5*/...) while((s32[]{:T(128)}, bf16[640,2048]{1,0:T(8,128)(2,1)}, ...), condition=%wide.region_10.12_spmd, body=%wide.region_9.11_spmd.sunk | while | flops 2418868224 | bytes 52888828 | solution.py:134
  146.9 1.8 fusion.84
  149.0 2.5 constant_dynamic-update-slice_fusion.2
  151.4 2.2 fusion.86
  153.7 1.1 fusion.87
  154.8 2.0 fusion.88
  156.8 1.4 fusion.85
  158.2 1.8 fusion.84
  160.2 2.5 constant_dynamic-update-slice_fusion.2
  162.7 2.2 fusion.86
  164.9 1.1 fusion.87
  166.1 2.0 fusion.88
  168.0 1.4 fusion.85
  169.4 7.4 %gather_fusion.4 = bf16[512,2048]{1,0:T(8,128)(2,1)} fusion(bf16[640,2048]{1,0:T(8,128)(2,1)} %get-tuple-element.86, s32[1024]{0:T(1024)S(1)} %pad_clamp_fusion.1), kind=kCustom, calls=%fused_computation.1.clone | custom fusion | bytes 4196352 | tf_op jit(solution)/shard_map/jit(_take)/gather | solution.py:13
  176.8 3.3 gather_fusion.6
  180.1 3.9 %select_select_fusion.2 = (bf16[512,2048]{1,0:T(8,128)(2,1)}, bf16[512,2048]{1,0:T(8,128)(2,1)}) fusion(bf16[512,2048]{1,0:T(8,128)(2,1)} %gather_fusion.6, pred[512]{0:T(512)(128)(4,1)S(1)} %compare_and_fusion.2, pred[512]{0:T(512)(128)(4,1)S(1)} %lt.133, bf16[512,2048]{1,0:T(8,128)(2,1)} %gather_fusion.4), kind=kLoop, calls=%fused_computation.50 | loop fusion | flops 4194304 | bytes 8389632 | tf_op jit(solution)/shard_map/jit(_where)/select_n | solution.py:12
  184.1 27.5 %all-to-all-start.4 = ((bf16[16,32,2048]{2,1,0:T(8,128)(2,1)}), bf16[16,32,2048]{2,1,0:T(8,128)(2,1)S(1)}, u32[]{:S(2)}, u32[]{:S(2)}) async-start(bf16[16,32,2048]{2,1,0:T(8,128)(2,1)} %bitcast.99), calls=%async_computation.4 | async-start | bytes 4194304 | tf_op jit(solution)/shard_map/all_to_all | solution.py:146
  211.8 6.1 %fusion.38 = bf16[2048,1,768]{2,0,1:T(8,128)(2,1)} fusion(bf16[640,2048]{1,0:T(8,128)(2,1)} %get-tuple-element.251, bf16[640,768]{1,0:T(8,128)(2,1)S(1)} %copy-done.6, bf16[640]{0:T(1024)(128)(2,1)S(1)} %broadcast_bitcast_fusion), kind=kOutput, calls=%fused_computation.43 | convolution fusion | flops 2015330304 | bytes 6751488 | tf_op jit(solution)/shard_map/rd,rf->df/dot_general | solution.py:41
  217.9 41.5 %all-to-all-done.4 = bf16[16,32,2048]{2,1,0:T(8,128)(2,1)S(1)} async-done(((bf16[16,32,2048]{2,1,0:T(8,128)(2,1)}), bf16[16,32,2048]{2,1,0:T(8,128)(2,1)S(1)}, u32[]{:S(2)}, u32[]{:S(2)}) %all-to-all-start.4) | async-done | bytes 2097184 | tf_op jit(solution)/shard_map/all_to_all | solution.py:146
  259.4 4.6 %all-to-all-start.3 = ((bf16[16,32,2048]{2,1,0:T(8,128)(2,1)}), bf16[16,32,2048]{2,1,0:T(8,128)(2,1)}, u32[]{:S(2)}, u32[]{:S(2)}) async-start(bf16[16,32,2048]{2,1,0:T(8,128)(2,1)} %bitcast.98), calls=%async_computation.3 | async-start | bytes 4194304 | tf_op jit(solution)/shard_map/all_to_all | solution.py:145
  264.0 1.4 gather_fusion.7
  265.4 46.1 %all-to-all-done.3 = bf16[16,32,2048]{2,1,0:T(8,128)(2,1)} async-done(((bf16[16,32,2048]{2,1,0:T(8,128)(2,1)}), bf16[16,32,2048]{2,1,0:T(8,128)(2,1)}, u32[]{:S(2)}, u32[]{:S(2)}) %all-to-all-start.3) | async-done | bytes 2097184 | tf_op jit(solution)/shard_map/all_to_all | solution.py:145
  311.5 4.2 %gather_fusion.5 = bf16[256,2048]{1,0:T(8,128)(2,1)S(1)} fusion(bf16[512,2048]{1,0:T(8,128)(2,1)} %bitcast.16, s32[1024]{0:T(1024)S(1)} %pad_clamp_fusion), kind=kCustom, calls=%fused_computation.2.clone | custom fusion | bytes 2098176 | tf_op jit(solution)/shard_map/jit(_take)/gather | solution.py:148
  315.7 1.2 bitcast_reduce_fusion
  316.9 2.1 fusion.39
  319.1 5.5 %copy.20 = f32[1024,1,768]{2,1,0:T(1,128)} copy(bf16[1024,1,768]{2,0,1:T(8,128)(2,1)} %reduce-scatter.2.cloned.1.call-done) | data formatting | bytes 4718592
  (72 shorter events, 3.1 us)
Async XLA Ops:
  7.2 11.8 %copy-start = (bf16[32,2048]{1,0:T(8,128)(2,1)S(1)}, bf16[32,2048]{1,0:T(8,128)(2,1)}, u32[]{:S(2)}) copy-start(bf16[32,2048]{1,0:T(8,128)(2,1)} %param.15) | copy-start | bytes 393220
  9.8 13.2 %all-to-all-start = ((bf16[16,1,1]{2,1,0:T(2,128)(2,1)}), bf16[16,1,1]{2,1,0:T(2,128)(2,1)S(1)}, u32[]{:S(2)}, u32[]{:S(2)}) async-start(bf16[16,1,1]{2,1,0:T(2,128)(2,1)} %copy.17), calls=%async_computation | async-start | bytes 16384 | tf_op jit(solution)/shard_map/all_to_all | solution.py:85
  23.1 6.3 %copy-start.8 = (s32[32,8]{0,1:T(8,128)S(1)}, s32[32,8]{0,1:T(8,128)}, u32[]{:S(2)}) copy-start(s32[32,8]{0,1:T(8,128)} %param.18) | copy-start | bytes 3076
  23.1 6.5 %copy-start.7 = (bf16[32,2048]{1,0:T(8,128)(2,1)S(1)}, bf16[32,2048]{1,0:T(8,128)(2,1)}, u32[]{:S(2)}) copy-start(bf16[32,2048]{1,0:T(8,128)(2,1)} %param.16) | copy-start | bytes 393220
  23.1 53.6 %all-to-all-start.1 = ((bf16[16,32,2048]{2,1,0:T(8,128)(2,1)}), bf16[16,32,2048]{2,1,0:T(8,128)(2,1)S(1)}, u32[]{:S(2)}, u32[]{:S(2)}) async-start(bf16[16,32,2048]{2,1,0:T(8,128)(2,1)} %select_select_fusion.5), calls=%async_computation.1 | async-start | bytes 4194304 | tf_op jit(solution)/shard_map/all_to_all | solution.py:83
  76.6 52.4 %all-to-all-start.2 = ((bf16[16,32,2048]{2,1,0:T(8,128)(2,1)}), bf16[16,32,2048]{2,1,0:T(8,128)(2,1)}, u32[]{:S(2)}, u32[]{:S(2)}) async-start(bf16[16,32,2048]{2,1,0:T(8,128)(2,1)} %select_select_fusion.4), calls=%async_computation.2 | async-start | bytes 4194304 | tf_op jit(solution)/shard_map/all_to_all | solution.py:84
  129.1 8.9 %copy-start.5 = (bf16[640,2048]{1,0:T(8,128)(2,1)S(1)}, bf16[640,2048]{1,0:T(8,128)(2,1)}, u32[]{:S(2)}) copy-start(bf16[640,2048]{1,0:T(8,128)(2,1)} %gather_fusion.2) | copy-start | bytes 7864324
  142.2 4.7 %copy-start.1 = (bf16[1,2048,768]{2,1,0:T(8,128)(2,1)S(1)}, bf16[1,2048,768]{2,1,0:T(8,128)(2,1)}, u32[]{:S(2)}) copy-start(bf16[1,2048,768]{2,1,0:T(8,128)(2,1)} %param.19) | copy-start | bytes 9437188
  146.9 2.0 copy-start.4
  148.7 2.8 copy-start.2
  158.2 2.0 copy-start.4
  159.9 2.8 copy-start.2
  169.4 7.5 %copy-start.3 = (bf16[640,2048]{1,0:T(8,128)(2,1)S(1)}, bf16[640,2048]{1,0:T(8,128)(2,1)}, u32[]{:S(2)}) copy-start(bf16[640,2048]{1,0:T(8,128)(2,1)} %get-tuple-element.87) | copy-start | bytes 7864324
  184.1 27.7 %copy-start.6 = (bf16[640,768]{1,0:T(8,128)(2,1)S(1)}, bf16[640,768]{1,0:T(8,128)(2,1)}, u32[]{:S(2)}) copy-start(bf16[640,768]{1,0:T(8,128)(2,1)} %get-tuple-element.88) | copy-start | bytes 2949124
  184.1 75.4 %all-to-all-start.4 = ((bf16[16,32,2048]{2,1,0:T(8,128)(2,1)}), bf16[16,32,2048]{2,1,0:T(8,128)(2,1)S(1)}, u32[]{:S(2)}, u32[]{:S(2)}) async-start(bf16[16,32,2048]{2,1,0:T(8,128)(2,1)} %bitcast.99), calls=%async_computation.4 | async-start | bytes 4194304 | tf_op jit(solution)/shard_map/all_to_all | solution.py:146
  211.6 107.4 %reduce-scatter.2.cloned.1.call-start = ((), (), s32[]{:S(2)}) async-start(), calls=%async_computation.6 | async-start | bytes 4718592 | tf_op jit(solution)/shard_map/reduce_scatter | solution.py:139
  259.4 52.0 %all-to-all-start.3 = ((bf16[16,32,2048]{2,1,0:T(8,128)(2,1)}), bf16[16,32,2048]{2,1,0:T(8,128)(2,1)}, u32[]{:S(2)}, u32[]{:S(2)}) async-start(bf16[16,32,2048]{2,1,0:T(8,128)(2,1)} %bitcast.98), calls=%async_computation.3 | async-start | bytes 4194304 | tf_op jit(solution)/shard_map/all_to_all | solution.py:145
Sparse Core Ops, SparseCore 0:
  218.0 42.9 reduce-scatter.1
where the time goes:
time: 332 us; the launch traced here: 331 us
  waiting for transfers between devices  166 us (50%)
  local copies, waits for them, and re-layouts  52.5 us (16%)
  starting transfers between devices  49.8 us (15%)
  matrix products  28 us (8%)
  other arithmetic  19.7 us (6%)
  between operations  15 us (5%)
    all_to_all x1, waiting for transfers between devices, shards(): lax.all_to_all(ret_o, 'expert', split_axis=0, concat_axis=0, tiled=True)  46.1 us
    all_to_all x1, waiting for transfers between devices, shards(): lax.all_to_all(ret_dx, 'expert', split_axis=0, concat_axis=0, tiled=True)  41.5 us
    all_to_all x1, waiting for transfers between devices, shards(): lax.all_to_all(send_x, 'expert', split_axis=0, concat_axis=0, tiled=True)  40.3 us
    all_to_all x1, waiting for transfers between devices, shards(): lax.all_to_all(send_do, 'expert', split_axis=0, concat_axis=0, tiled=True)  38.5 us
    gather x6, local copies, waits for them, and re-layouts, take_rows(): jnp.take(source, safe_rows, axis=0)  29.5 us
    all_to_all x1, starting transfers between devices, shards(): lax.all_to_all(ret_dx, 'expert', split_axis=0, concat_axis=0, tiled=True)  27.5 us
    select_n x4, other arithmetic, take_rows(): jnp.where(is_valid[:, None], jnp.take(source, safe_rows, axis=0), jnp.zer...  13.1 us
  transfers between devices with their start and end apart: 6, of which 4 were waited for; matrix products, arithmetic and copies ran while one was open for 11% of the time, Pallas kernels for 0%

commit v1 on v0

v1 whole, which is shorter than its diff:
```python
import jax
import jax.numpy as jnp
from jax import lax
from jax.sharding import PartitionSpec as P

LANES = 128


def swap(value, axis, distance):
    size = lax.axis_size(axis)
    return lax.ppermute(value, axis, [(i, i ^ distance) for i in range(size)])


def far_steps(n_expert):
    return list(range(8, n_expert, 4))


def gather_near(block):
    beside = swap(block, "expert", 2)
    own = jnp.concatenate([block, beside], axis=0)
    near = swap(own, "expert", 4)
    return jnp.concatenate([own, near], axis=0)


def gather_far(block, n_expert):
    straight = [swap(block, "expert", step) for step in far_steps(n_expert)]
    straight = jnp.concatenate(straight, axis=0)
    across = swap(straight, "expert", 2)
    return jnp.concatenate([straight, across], axis=0)


def gather_even(block, n_expert):
    return [gather_near(block), gather_far(block, n_expert)]


def gather_odd(parts):
    return [swap(part, "expert", 1) for part in parts]


def scatter_sum(partial, n_expert):
    total_rows, width = partial.shape
    rows = total_rows // n_expert
    half = total_rows // 2
    kept, sent = partial[:half], partial[half:]
    even = (kept + swap(sent, "expert", 1)).reshape(n_expert // 2, rows, width)
    near, far = even[:4], even[4:]
    n_far = far.shape[0] // 2
    from_near = swap(near[2:].reshape(2 * rows, width), "expert", 4).reshape(2, rows, width)
    across = swap(far[n_far:].reshape(n_far * rows, width), "expert", 2).reshape(n_far, rows, width)
    straight = far[:n_far] + across
    beside = swap(near[1] + from_near[1], "expert", 2)
    total = near[0].astype(jnp.float32) + from_near[0].astype(jnp.float32)
    for index, step in enumerate(far_steps(n_expert)):
        total = total + swap(straight[index], "expert", step).astype(jnp.float32)
    total = total + beside.astype(jnp.float32)
    return total.astype(jnp.bfloat16)


def gate_lanes(routes, gate_codes, n_expert):
    experts = jnp.arange(n_expert, dtype=jnp.int32)
    chosen = routes[:, :, None] == experts[None, None, :]
    codes = jnp.sum(jnp.where(chosen, gate_codes[:, :, None], 0), axis=1)
    total = jnp.sum(gate_codes, axis=1, keepdims=True)
    digits = jnp.concatenate([codes // 64, codes % 64, total // 256, total % 256], axis=1)
    return jnp.pad(digits, ((0, 0), (0, LANES - digits.shape[1]))).astype(jnp.bfloat16)


def gate_of_expert(lanes, expert, n_expert):
    values = lanes.astype(jnp.float32)
    index = lax.broadcasted_iota(jnp.int32, values.shape, 1)
    pick = lambda at: jnp.sum(jnp.where(index == at, values, 0.0), axis=1, keepdims=True)
    code = pick(expert) * 64.0 + pick(expert + n_expert)
    total = pick(2 * n_expert) * 256.0 + pick(2 * n_expert + 1)
    return code / total


def dot(left, right, contract):
    return lax.dot_general(left, right, (contract, ((), ())), preferred_element_type=jnp.float32)


def shards(tokens, out_grad, routes, gate_codes, w_gate, w_up, w_down):
    rows, width = tokens.shape
    n_expert = lax.axis_size("expert")
    n_edata = lax.axis_size("edata")
    expert = lax.axis_index("expert")
    gate_mat, up_mat, down_mat = w_gate[0], w_up[0], w_down[0]

    lanes = gate_lanes(routes, gate_codes, n_expert)
    even = gather_even(jnp.concatenate([tokens, lanes], axis=1), n_expert)
    odd = gather_odd(even)
    grads_even = gather_even(out_grad, n_expert)
    grads_odd = gather_odd(grads_even)

    gathered = jnp.concatenate(even + odd, axis=0)
    rows_in, lanes_in = gathered[:, :width], gathered[:, width:]
    gate = gate_of_expert(lanes_in, expert, n_expert)
    gate_pre = dot(rows_in, gate_mat, ((1,), (0,)))
    up_pre = dot(rows_in, up_mat, ((1,), (0,)))
    sig_gate = jax.nn.sigmoid(gate_pre)
    act_gate = gate_pre * sig_gate * gate
    hidden = (act_gate * up_pre).astype(jnp.bfloat16)
    slope = gate * up_pre * sig_gate * (1.0 + gate_pre * (1.0 - sig_gate))
    mixed = scatter_sum(dot(hidden, down_mat, ((1,), (0,))).astype(jnp.bfloat16), n_expert)

    grads_in = jnp.concatenate(grads_even + grads_odd, axis=0)
    grad_hidden = dot(grads_in, down_mat, ((1,), (1,)))
    grad_gate_pre = (grad_hidden * slope).astype(jnp.bfloat16)
    grad_up_pre = (grad_hidden * act_gate).astype(jnp.bfloat16)
    grad_rows = dot(grad_gate_pre, gate_mat, ((1,), (1,))) + dot(grad_up_pre, up_mat, ((1,), (1,)))
    input_grad = scatter_sum(grad_rows.astype(jnp.bfloat16), n_expert)

    place = lax.axis_index("edata")
    share = width // n_edata
    half = grads_in.shape[0] // 2
    grad_down = dot(lax.dynamic_slice_in_dim(grads_in, place * share, share, 1), hidden, ((0,), (0,)))
    for step in range(1, n_edata):
        hidden_other = swap(hidden, "edata", step)
        wanted = lax.dynamic_slice_in_dim(grads_in[:half], (place ^ step) * share, share, 1)
        other_even = swap(wanted, "edata", step)
        other_odd = swap(other_even, "expert", 1)
        grads_other = jnp.concatenate([other_even, other_odd], axis=0)
        grad_down = grad_down + dot(grads_other, hidden_other, ((0,), (0,)))
    return mixed, input_grad, grad_down[:, None, :]


def solution(mesh):
    by_token = P(("expert", "edata"), None)
    by_expert = P("expert", None, None)
    return jax.shard_map(
        shards,
        mesh=mesh,
        in_specs=(by_token,) * 4 + (by_expert,) * 3,
        out_specs=(by_token, by_token, P("edata", "expert", None)),
        check_vma=False,
    )
```

time: 332 us -> 127 us (0.38)
  the two profiles are of different devices: /device:TPU:15 before, /device:TPU:0 now
where the time goes in v1:
time: 127 us
  waiting for transfers between devices  53.1 us (42%)
  starting transfers between devices  35.3 us (28%)
  matrix products  14.2 us (11%)
  local copies, waits for them, and re-layouts  12.8 us (10%)
  other arithmetic  10.6 us (8%)
    ppermute x29, waiting for transfers between devices, swap(): return lax.ppermute(value, axis, [(i, i ^ distance) for i in range(size)])  53.1 us
    ppermute x29, starting transfers between devices, swap(): return lax.ppermute(value, axis, [(i, i ^ distance) for i in range(size)])  35.3 us
    dot_general x8, matrix products, dot(): lax.dot_general(left, right, (contract, ((), ())), preferred_element_type...  14.2 us
    unnamed x38, local copies, waits for them, and re-layouts  12.4 us
  transfers between devices with their start and end apart: 29, of which 10 were waited for; matrix products, arithmetic and copies ran while one was open for 28% of the time, Pallas kernels for 0%

profile of v1, /device:TPU:0, one launch (start us, length us, event | category | flops | bytes accessed | tf_op | source)
XLA Modules:
  0.0 127.1 jit_solution(3362668042776804978)
XLA Ops:
  0.7 5.1 %collective-permute-start.16 = (bf16[32,2048]{1,0:T(8,128)(2,1)}, bf16[32,2048]{1,0:T(8,128)(2,1)}, u32[]{:S(2)}, u32[]{:S(2)}) collective-permute-start(bf16[32,2048]{1,0:T(8,128)(2,1)} %param.8), channel_id=1, source_target_pairs={{0,24},{2,26},{4,28},{6,30},{8,16},{10,18},{12,20},{14,22},{16,8},... | collective-permute-start | bytes 393224 | tf_op jit(solution)/shard_map/ppermute | solution.py:11
  5.8 1.5 %collective-permute-start.13 = (bf16[32,2048]{1,0:T(8,128)(2,1)}, bf16[32,2048]{1,0:T(8,128)(2,1)}, u32[]{:S(2)}, u32[]{:S(2)}) collective-permute-start(bf16[32,2048]{1,0:T(8,128)(2,1)} %param.8), channel_id=1, source_target_pairs={{0,4},{2,6},{4,0},{6,2},{8,12},{10,14},{12,8},{14,10},{16,20},{18,... | collective-permute-start | bytes 393224 | tf_op jit(solution)/shard_map/ppermute | solution.py:11
  8.0 0.7 select_reduce_fusion
  8.9 1.6 %pad_maximum_fusion.8 = (bf16[32,2176]{1,0:T(8,128)(2,1)}, bf16[512,2176]{1,0:T(8,128)(2,1)}) fusion(bf16[32,128]{1,0:T(8,128)(2,1)S(1)} %pad.5.clone, bf16[32,2048]{1,0:T(8,128)(2,1)} %param.7), kind=kLoop, calls=%fused_computation.51 | loop fusion | flops 278527 | bytes 417792 | tf_op jit(solution)/shard_map/concatenate | solution.py:89
  10.5 1.9 %collective-permute-start.3 = (bf16[32,2176]{1,0:T(8,128)(2,1)}, bf16[32,2176]{1,0:T(8,128)(2,1)S(1)}, u32[]{:S(2)}, u32[]{:S(2)}) collective-permute-start(bf16[32,2176]{1,0:T(8,128)(2,1)} %get-tuple-element.25), channel_id=1, source_target_pairs={{0,24},{2,26},{4,28},{6,30},{8,16},{10,18},{12,20},{14,22},{16,8},... | collective-permute-start | bytes 417800 | tf_op jit(solution)/shard_map/ppermute | solution.py:11
  12.9 1.6 %constant_dynamic-update-slice_fusion.21 = (bf16[256,2048]{1,0:T(8,128)(2,1)}, bf16[512,2048]{1,0:T(8,128)(2,1)}) fusion(bf16[32,2048]{1,0:T(8,128)(2,1)} %param.8), kind=kLoop, calls=%fused_computation.77 | loop fusion | bytes 393216
  15.1 6.5 %collective-permute-start.2 = (bf16[32,2176]{1,0:T(8,128)(2,1)}, bf16[32,2176]{1,0:T(8,128)(2,1)S(1)}, u32[]{:S(2)}, u32[]{:S(2)}) collective-permute-start(bf16[32,2176]{1,0:T(8,128)(2,1)} %get-tuple-element.25), channel_id=1, source_target_pairs={{0,16},{2,18},{4,20},{6,22},{8,24},{10,26},{12,28},{14,30},{16,0},... | collective-permute-start | bytes 417800 | tf_op jit(solution)/shard_map/ppermute | solution.py:11
  21.6 1.1 collective-permute-done.15
  22.6 1.0 pad_maximum_fusion.7
  23.6 1.6 %collective-permute-start.17 = (bf16[64,2048]{1,0:T(8,128)(2,1)S(1)}, bf16[64,2048]{1,0:T(8,128)(2,1)S(1)}, u32[]{:S(2)}, u32[]{:S(2)}) collective-permute-start(bf16[64,2048]{1,0:T(8,128)(2,1)S(1)} %pad_maximum_fusion.7), channel_id=1, source_target_pairs={{0,4},{2,6},{4,0},{6,2},{8,12},{10,14},{12,8},{14,10},{16,20},{18,... | collective-permute-start | bytes 786440 | tf_op jit(solution)/shard_map/ppermute | solution.py:11
  25.2 1.0 pad_maximum_fusion.6
  26.2 1.7 %constant_dynamic-update-slice_fusion.20 = (bf16[256,2048]{1,0:T(8,128)(2,1)}, bf16[512,2048]{1,0:T(8,128)(2,1)}) fusion(bf16[256,2048]{1,0:T(8,128)(2,1)} %get-tuple-element.33, bf16[32,2048]{1,0:T(8,128)(2,1)} %collective-permute-done.13, bf16[512,2048]{1,0:T(8,128)(2,1)} %get-tuple-element.34), kind=kLoop, calls=%fused_computation.76 | loop fusion | bytes 393216
  27.9 0.9 pad_maximum_fusion.4
  28.8 2.1 %collective-permute-start.1 = (bf16[64,2176]{1,0:T(8,128)(2,1)S(1)}, bf16[64,2176]{1,0:T(8,128)(2,1)S(1)}, u32[]{:S(2)}, u32[]{:S(2)}) collective-permute-start(bf16[64,2176]{1,0:T(8,128)(2,1)S(1)} %pad_maximum_fusion.4), channel_id=1, source_target_pairs={{0,8},{2,10},{4,12},{6,14},{8,0},{10,2},{12,4},{14,6},{16,24},{18,... | collective-permute-start | bytes 835592 | tf_op jit(solution)/shard_map/ppermute | solution.py:11
  32.1 1.0 pad_maximum_fusion.3
  33.2 2.2 %collective-permute-done.14 = bf16[64,2048]{1,0:T(8,128)(2,1)S(1)} collective-permute-done((bf16[64,2048]{1,0:T(8,128)(2,1)S(1)}, bf16[64,2048]{1,0:T(8,128)(2,1)S(1)}, u32[]{:S(2)}, u32[]{:S(2)}) %collective-permute-start.14) | collective-permute-done | bytes 262176 | tf_op jit(solution)/shard_map/ppermute | solution.py:11
  35.5 0.9 pad_maximum_fusion.2
  36.6 0.9 constant_dynamic-update-slice_fusion.18
  37.5 0.9 constant_dynamic-update-slice_fusion.17
  38.5 1.6 %collective-permute-start.26 = (bf16[256,1024]{1,0:T(8,128)(2,1)S(1)}, bf16[256,1024]{1,0:T(8,128)(2,1)S(1)}, u32[]{:S(2)}, u32[]{:S(2)}) collective-permute-start(bf16[256,1024]{1,0:T(8,128)(2,1)S(1)} %constant_dynamic-slice_fusion), channel_id=1, source_target_pairs={{0,1},{1,0},{2,3},{3,2},{4,5},{5,4},{6,7},{7,6},{8,9},{9,8},{10,11... | collective-permute-start | bytes 1572872 | tf_op jit(solution)/shard_map/ppermute | solution.py:11
  41.1 1.3 %copy-done.10 = bf16[1,768,2048]{2,1,0:T(8,128)(2,1)S(1)} copy-done((bf16[1,768,2048]{2,1,0:T(8,128)(2,1)S(1)}, bf16[1,768,2048]{2,1,0:T(8,128)(2,1)}, u32[]{:S(2)}) %copy-start.10) | copy-done | bytes 3145752
  42.4 1.9 %fusion = f32[512,768]{1,0:T(8,128)S(1)} fusion(bf16[512,2048]{1,0:T(8,128)(2,1)S(1)} %constant_dynamic-update-slice_fusion.8, bf16[1,768,2048]{2,1,0:T(8,128)(2,1)S(1)} %copy-done.10), kind=kOutput, calls=%fused_computation.1 | convolution fusion | flops 1610612736 | bytes 6815744 | tf_op jit(solution)/shard_map/dot_general | solution.py:78
  44.3 8.6 %collective-permute-done.26 = bf16[256,1024]{1,0:T(8,128)(2,1)S(1)} collective-permute-done((bf16[256,1024]{1,0:T(8,128)(2,1)S(1)}, bf16[256,1024]{1,0:T(8,128)(2,1)S(1)}, u32[]{:S(2)}, u32[]{:S(2)}) %collective-permute-start.26) | collective-permute-done | bytes 524320 | tf_op jit(solution)/shard_map/ppermute | solution.py:11
  53.1 1.8 %fusion.10 = f32[512,768]{1,0:T(8,128)S(1)} fusion(bf16[1,2048,768]{2,1,0:T(8,128)(2,1)S(1)} %copy-done.11, bf16[512,2176]{1,0:T(8,128)(2,1)S(1)} %constant_dynamic-update-slice_fusion), kind=kOutput, calls=%fused_computation.11 | convolution fusion | flops 1610612736 | bytes 6815744 | tf_op jit(solution)/shard_map/dot_general | solution.py:78
  55.2 1.9 %multiply_convert_fusion.2 = (bf16[512,768]{1,0:T(8,128)(2,1)S(1)}, f32[512,768]{1,0:T(8,128)S(1)}) fusion(f32[512]{0:T(512)S(1)} %add_divide_fusion.1, f32[512,768]{1,0:T(8,128)S(1)} %fusion.10, bf16[1,2048,768]{2,1,0:T(8,128)(2,1)S(1)} %copy-done, bf16[512,2176]{1,0:T(8,128)(2,1)S(1)} %constant_dynamic-update-slice_fusion), kind=kOutput, calls=%fused_computation.19 | convolution fusion | flops 1613365248 | bytes 9177088 | tf_op jit(solution)/shard_map/dot_general | solution.py:78
  57.1 1.6 %collective-permute-start.28 = (bf16[512,768]{1,0:T(8,128)(2,1)S(1)}, bf16[512,768]{1,0:T(8,128)(2,1)S(1)}, u32[]{:S(2)}, u32[]{:S(2)}) collective-permute-start(bf16[512,768]{1,0:T(8,128)(2,1)S(1)} %get-tuple-element.39), channel_id=1, source_target_pairs={{0,1},{1,0},{2,3},{3,2},{4,5},{5,4},{6,7},{7,6},{8,9},{9,8},{10,11... | collective-permute-start | bytes 2359304 | tf_op jit(solution)/shard_map/ppermute | solution.py:11
  58.7 1.8 %fusion.12 = bf16[512,2048]{1,0:T(8,128)(2,1)S(1)} fusion(bf16[512,768]{1,0:T(8,128)(2,1)S(1)} %get-tuple-element.39, bf16[1,768,2048]{2,1,0:T(8,128)(2,1)S(1)} %copy-done.10), kind=kOutput, calls=%fused_computation.14 | convolution fusion | flops 1611661312 | bytes 6029312 | tf_op jit(solution)/shard_map/dot_general | solution.py:78
  60.9 2.1 %fusion.4 = f32[512,2048]{1,0:T(8,128)S(1)} fusion(bf16[1,2048,768]{2,1,0:T(8,128)(2,1)S(1)} %copy-done, f32[512,768]{1,0:T(8,128)S(1)} %fusion, f32[512,768]{1,0:T(8,128)S(1)} %fusion.10, f32[512]{0:T(512)S(1)} %add_divide_fusion.1), kind=kOutput, calls=%fused_computation.5 | convolution fusion | flops 1613365248 | bytes 10487808 | tf_op jit(solution)/shard_map/dot_general | solution.py:78
  63.0 2.4 %add_convert_fusion = bf16[512,2048]{1,0:T(8,128)(2,1)S(1)} fusion(f32[512,2048]{1,0:T(8,128)S(1)} %fusion.4, bf16[1,2048,768]{2,1,0:T(8,128)(2,1)S(1)} %copy-done.11, f32[512,768]{1,0:T(8,128)S(1)} %fusion, f32[512,768]{1,0:T(8,128)S(1)} %fusion.10, f32[512,768]{1,0:T(8,128)S(1)} %get-tuple-element.40, f32[512]{0:T(512)S(1)} %add_divide_fusion.1), kind=kOutput, calls=%fused_computation | convolution fusion | flops 1617035264 | bytes 14157824 | tf_op jit(solution)/shard_map/dot_general | solution.py:78
  65.8 11.3 %collective-permute-done.28 = bf16[512,768]{1,0:T(8,128)(2,1)S(1)} collective-permute-done((bf16[512,768]{1,0:T(8,128)(2,1)S(1)}, bf16[512,768]{1,0:T(8,128)(2,1)S(1)}, u32[]{:S(2)}, u32[]{:S(2)}) %collective-permute-start.28) | collective-permute-done | bytes 786464 | tf_op jit(solution)/shard_map/ppermute | solution.py:11
  77.1 1.2 fusion.19
  78.4 1.1 add_bitcast_fusion
  79.4 4.9 %copy.16 = f32[1024,1,768]{2,1,0:T(1,128)} copy(f32[1024,1,768]{2,0,1:T(8,128)S(1)} %add_bitcast_fusion) | data formatting | bytes 6291456
  84.5 0.9 collective-permute-start.9
  85.5 1.3 %collective-permute-start.22 = (bf16[64,2048]{1,0:T(8,128)(2,1)S(1)}, bf16[64,2048]{1,0:T(8,128)(2,1)S(1)}, u32[]{:S(2)}, u32[]{:S(2)}) collective-permute-start(bf16[64,2048]{1,0:T(8,128)(2,1)S(1)} %slice.153), channel_id=1, source_target_pairs={{0,4},{2,6},{4,0},{6,2},{8,12},{10,14},{12,8},{14,10},{16,20},{18,... | collective-permute-start | bytes 786440 | tf_op jit(solution)/shard_map/ppermute | solution.py:11
  86.8 7.0 %collective-permute-done.9 = bf16[64,2048]{1,0:T(8,128)(2,1)S(1)} collective-permute-done((bf16[64,2048]{1,0:T(8,128)(2,1)S(1)}, bf16[64,2048]{1,0:T(8,128)(2,1)S(1)}, u32[]{:S(2)}, u32[]{:S(2)}) %collective-permute-start.9) | collective-permute-done | bytes 262176 | tf_op jit(solution)/shard_map/ppermute | solution.py:11
  93.8 0.8 collective-permute-start.10
  94.6 2.0 %collective-permute-start.11 = (bf16[32,2048]{1,0:T(8,128)(2,1)S(1)}, bf16[32,2048]{1,0:T(8,128)(2,1)S(1)}, u32[]{:S(2)}, u32[]{:S(2)}) collective-permute-start(bf16[32,2048]{1,0:T(8,128)(2,1)S(1)} %get-tuple-element.24), channel_id=1, source_target_pairs={{0,24},{2,26},{4,28},{6,30},{8,16},{10,18},{12,20},{14,22},{16,8},... | collective-permute-start | bytes 393224 | tf_op jit(solution)/shard_map/ppermute | solution.py:11
  96.7 0.7 collective-permute-start.8
  97.4 0.7 collective-permute-done.22
  98.2 1.0 collective-permute-start.23
  99.2 2.0 %collective-permute-start.24 = (bf16[32,2048]{1,0:T(8,128)(2,1)S(1)}, bf16[32,2048]{1,0:T(8,128)(2,1)S(1)}, u32[]{:S(2)}, u32[]{:S(2)}) collective-permute-start(bf16[32,2048]{1,0:T(8,128)(2,1)S(1)} %get-tuple-element.22), channel_id=1, source_target_pairs={{0,24},{2,26},{4,28},{6,30},{8,16},{10,18},{12,20},{14,22},{16,8},... | collective-permute-start | bytes 393224 | tf_op jit(solution)/shard_map/ppermute | solution.py:11
  101.2 8.1 %collective-permute-done.8 = bf16[64,2048]{1,0:T(8,128)(2,1)S(1)} collective-permute-done((bf16[64,2048]{1,0:T(8,128)(2,1)S(1)}, bf16[64,2048]{1,0:T(8,128)(2,1)S(1)}, u32[]{:S(2)}, u32[]{:S(2)}) %collective-permute-start.8) | collective-permute-done | bytes 262176 | tf_op jit(solution)/shard_map/ppermute | solution.py:11
  109.5 9.7 %collective-permute-done.21 = bf16[64,2048]{1,0:T(8,128)(2,1)S(1)} collective-permute-done((bf16[64,2048]{1,0:T(8,128)(2,1)S(1)}, bf16[64,2048]{1,0:T(8,128)(2,1)S(1)}, u32[]{:S(2)}, u32[]{:S(2)}) %collective-permute-start.21) | collective-permute-done | bytes 262176 | tf_op jit(solution)/shard_map/ppermute | solution.py:11
  119.9 1.5 %collective-permute-start.25 = (bf16[32,2048]{1,0:T(8,128)(2,1)S(1)}, bf16[32,2048]{1,0:T(8,128)(2,1)S(1)}, u32[]{:S(2)}, u32[]{:S(2)}) collective-permute-start(bf16[32,2048]{1,0:T(8,128)(2,1)S(1)} %slice_add_fusion.4), channel_id=1, source_target_pairs={{0,4},{2,6},{4,0},{6,2},{8,12},{10,14},{12,8},{14,10},{16,20},{18,... | collective-permute-start | bytes 393224 | tf_op jit(solution)/shard_map/ppermute | solution.py:11
  121.3 3.6 %collective-permute-done.12 = bf16[32,2048]{1,0:T(8,128)(2,1)S(1)} collective-permute-done((bf16[32,2048]{1,0:T(8,128)(2,1)S(1)}, bf16[32,2048]{1,0:T(8,128)(2,1)S(1)}, u32[]{:S(2)}, u32[]{:S(2)}) %collective-permute-start.12) | collective-permute-done | bytes 131104 | tf_op jit(solution)/shard_map/ppermute | solution.py:11
  124.9 0.7 add_convert_fusion.2
  126.3 0.7 add_convert_fusion.1
  (93 shorter events, 7.5 us)
Async XLA Ops:
  0.6 54.5 %copy-start = (bf16[1,2048,768]{2,1,0:T(8,128)(2,1)S(1)}, bf16[1,2048,768]{2,1,0:T(8,128)(2,1)}, u32[]{:S(2)}) copy-start(bf16[1,2048,768]{2,1,0:T(8,128)(2,1)} %param.12) | copy-start | bytes 9437188
  0.6 27.3 %copy-start.1 = (bf16[32,2048]{1,0:T(8,128)(2,1)S(1)}, bf16[32,2048]{1,0:T(8,128)(2,1)}, u32[]{:S(2)}) copy-start(bf16[32,2048]{1,0:T(8,128)(2,1)} %param.7) | copy-start | bytes 393220
  0.7 14.4 %collective-permute-start.16 = (bf16[32,2048]{1,0:T(8,128)(2,1)}, bf16[32,2048]{1,0:T(8,128)(2,1)}, u32[]{:S(2)}, u32[]{:S(2)}) collective-permute-start(bf16[32,2048]{1,0:T(8,128)(2,1)} %param.8), channel_id=1, source_target_pairs={{0,24},{2,26},{4,28},{6,30},{8,16},{10,18},{12,20},{14,22},{16,8},... | collective-permute-start | bytes 393224 | tf_op jit(solution)/shard_map/ppermute | solution.py:11
  5.8 16.8 %collective-permute-start.15 = (bf16[32,2048]{1,0:T(8,128)(2,1)}, bf16[32,2048]{1,0:T(8,128)(2,1)}, u32[]{:S(2)}, u32[]{:S(2)}) collective-permute-start(bf16[32,2048]{1,0:T(8,128)(2,1)} %param.8), channel_id=1, source_target_pairs={{0,16},{2,18},{4,20},{6,22},{8,24},{10,26},{12,28},{14,30},{16,0},... | collective-permute-start | bytes 393224 | tf_op jit(solution)/shard_map/ppermute | solution.py:11
  5.8 19.4 %collective-permute-start.13 = (bf16[32,2048]{1,0:T(8,128)(2,1)}, bf16[32,2048]{1,0:T(8,128)(2,1)}, u32[]{:S(2)}, u32[]{:S(2)}) collective-permute-start(bf16[32,2048]{1,0:T(8,128)(2,1)} %param.8), channel_id=1, source_target_pairs={{0,4},{2,6},{4,0},{6,2},{8,12},{10,14},{12,8},{14,10},{16,20},{18,... | collective-permute-start | bytes 393224 | tf_op jit(solution)/shard_map/ppermute | solution.py:11
  8.9 1.6 %copy-start.5 = (bf16[32,128]{1,0:T(8,128)(2,1)}, bf16[32,128]{1,0:T(8,128)(2,1)S(1)}, u32[]{:S(2)}) copy-start(bf16[32,128]{1,0:T(8,128)(2,1)S(1)} %pad.5.clone) | copy-start | bytes 24580
  10.5 20.4 %collective-permute-start.3 = (bf16[32,2176]{1,0:T(8,128)(2,1)}, bf16[32,2176]{1,0:T(8,128)(2,1)S(1)}, u32[]{:S(2)}, u32[]{:S(2)}) collective-permute-start(bf16[32,2176]{1,0:T(8,128)(2,1)} %get-tuple-element.25), channel_id=1, source_target_pairs={{0,24},{2,26},{4,28},{6,30},{8,16},{10,18},{12,20},{14,22},{16,8},... | collective-permute-start | bytes 417800 | tf_op jit(solution)/shard_map/ppermute | solution.py:11
  12.4 15.5 %collective-permute-start = (bf16[32,2176]{1,0:T(8,128)(2,1)}, bf16[32,2176]{1,0:T(8,128)(2,1)S(1)}, u32[]{:S(2)}, u32[]{:S(2)}) collective-permute-start(bf16[32,2176]{1,0:T(8,128)(2,1)} %get-tuple-element.25), channel_id=1, source_target_pairs={{0,4},{2,6},{4,0},{6,2},{8,12},{10,14},{12,8},{14,10},{16,20},{18,... | collective-permute-start | bytes 417800 | tf_op jit(solution)/shard_map/ppermute | solution.py:11
  15.1 20.4 %copy-start.2 = (bf16[32,2048]{1,0:T(8,128)(2,1)S(1)}, bf16[32,2048]{1,0:T(8,128)(2,1)}, u32[]{:S(2)}) copy-start(bf16[32,2048]{1,0:T(8,128)(2,1)} %param.8) | copy-start | bytes 393220
  15.1 15.8 %collective-permute-start.2 = (bf16[32,2176]{1,0:T(8,128)(2,1)}, bf16[32,2176]{1,0:T(8,128)(2,1)S(1)}, u32[]{:S(2)}, u32[]{:S(2)}) collective-permute-start(bf16[32,2176]{1,0:T(8,128)(2,1)} %get-tuple-element.25), channel_id=1, source_target_pairs={{0,16},{2,18},{4,20},{6,22},{8,24},{10,26},{12,28},{14,30},{16,0},... | collective-permute-start | bytes 417800 | tf_op jit(solution)/shard_map/ppermute | solution.py:11
  23.6 8.6 %collective-permute-start.17 = (bf16[64,2048]{1,0:T(8,128)(2,1)S(1)}, bf16[64,2048]{1,0:T(8,128)(2,1)S(1)}, u32[]{:S(2)}, u32[]{:S(2)}) collective-permute-start(bf16[64,2048]{1,0:T(8,128)(2,1)S(1)} %pad_maximum_fusion.7), channel_id=1, source_target_pairs={{0,4},{2,6},{4,0},{6,2},{8,12},{10,14},{12,8},{14,10},{16,20},{18,... | collective-permute-start | bytes 786440 | tf_op jit(solution)/shard_map/ppermute | solution.py:11
  26.2 9.3 %collective-permute-start.14 = (bf16[64,2048]{1,0:T(8,128)(2,1)S(1)}, bf16[64,2048]{1,0:T(8,128)(2,1)S(1)}, u32[]{:S(2)}, u32[]{:S(2)}) collective-permute-start(bf16[64,2048]{1,0:T(8,128)(2,1)S(1)} %pad_maximum_fusion.6), channel_id=1, source_target_pairs={{0,8},{2,10},{4,12},{6,14},{8,0},{10,2},{12,4},{14,6},{16,24},{18,... | collective-permute-start | bytes 786440 | tf_op jit(solution)/shard_map/ppermute | solution.py:11
  27.9 8.6 %copy-start.3 = (bf16[512,2048]{1,0:T(8,128)(2,1)S(1)}, bf16[512,2048]{1,0:T(8,128)(2,1)}, u32[]{:S(2)}) copy-start(bf16[512,2048]{1,0:T(8,128)(2,1)} %get-tuple-element.32) | copy-start | bytes 6291460
  27.9 8.6 %copy-start.4 = (bf16[256,2048]{1,0:T(8,128)(2,1)S(1)}, bf16[256,2048]{1,0:T(8,128)(2,1)}, u32[]{:S(2)}) copy-start(bf16[256,2048]{1,0:T(8,128)(2,1)} %get-tuple-element.31) | copy-start | bytes 3145732
  28.8 11.7 %collective-permute-start.1 = (bf16[64,2176]{1,0:T(8,128)(2,1)S(1)}, bf16[64,2176]{1,0:T(8,128)(2,1)S(1)}, u32[]{:S(2)}, u32[]{:S(2)}) collective-permute-start(bf16[64,2176]{1,0:T(8,128)(2,1)S(1)} %pad_maximum_fusion.4), channel_id=1, source_target_pairs={{0,8},{2,10},{4,12},{6,14},{8,0},{10,2},{12,4},{14,6},{16,24},{18,... | collective-permute-start | bytes 835592 | tf_op jit(solution)/shard_map/ppermute | solution.py:11
  30.9 9.2 %collective-permute-start.4 = (bf16[64,2176]{1,0:T(8,128)(2,1)S(1)}, bf16[64,2176]{1,0:T(8,128)(2,1)S(1)}, u32[]{:S(2)}, u32[]{:S(2)}) collective-permute-start(bf16[64,2176]{1,0:T(8,128)(2,1)S(1)} %pad_maximum_fusion.5), channel_id=1, source_target_pairs={{0,4},{2,6},{4,0},{6,2},{8,12},{10,14},{12,8},{14,10},{16,20},{18,... | collective-permute-start | bytes 835592 | tf_op jit(solution)/shard_map/ppermute | solution.py:11
  33.2 7.9 %collective-permute-start.19 = (bf16[128,2048]{1,0:T(8,128)(2,1)S(1)}, bf16[128,2048]{1,0:T(8,128)(2,1)S(1)}, u32[]{:S(2)}, u32[]{:S(2)}) collective-permute-start(bf16[128,2048]{1,0:T(8,128)(2,1)S(1)} %pad_maximum_fusion.3), channel_id=1, source_target_pairs={{0,2},{2,0},{4,6},{6,4},{8,10},{10,8},{12,14},{14,12},{16,18},{18,... | collective-permute-start | bytes 1572872 | tf_op jit(solution)/shard_map/ppermute | solution.py:11
  36.4 4.6 %collective-permute-start.18 = (bf16[128,2048]{1,0:T(8,128)(2,1)S(1)}, bf16[128,2048]{1,0:T(8,128)(2,1)S(1)}, u32[]{:S(2)}, u32[]{:S(2)}) collective-permute-start(bf16[128,2048]{1,0:T(8,128)(2,1)S(1)} %pad_maximum_fusion.2), channel_id=1, source_target_pairs={{0,2},{2,0},{4,6},{6,4},{8,10},{10,8},{12,14},{14,12},{16,18},{18,... | collective-permute-start | bytes 1572872 | tf_op jit(solution)/shard_map/ppermute | solution.py:11
  36.5 3.9 %copy-start.6 = (bf16[32,128]{1,0:T(8,128)(2,1)S(1)}, bf16[32,128]{1,0:T(8,128)(2,1)}, u32[]{:S(2)}) copy-start(bf16[32,128]{1,0:T(8,128)(2,1)} %copy-done.5) | copy-start | bytes 24580
  38.4 2.4 %copy-start.7 = (bf16[512,2176]{1,0:T(8,128)(2,1)S(1)}, bf16[512,2176]{1,0:T(8,128)(2,1)}, u32[]{:S(2)}) copy-start(bf16[512,2176]{1,0:T(8,128)(2,1)} %constant_dynamic-update-slice_fusion.6) | copy-start | bytes 6684676
  38.5 14.4 %collective-permute-start.26 = (bf16[256,1024]{1,0:T(8,128)(2,1)S(1)}, bf16[256,1024]{1,0:T(8,128)(2,1)S(1)}, u32[]{:S(2)}, u32[]{:S(2)}) collective-permute-start(bf16[256,1024]{1,0:T(8,128)(2,1)S(1)} %constant_dynamic-slice_fusion), channel_id=1, source_target_pairs={{0,1},{1,0},{2,3},{3,2},{4,5},{5,4},{6,7},{7,6},{8,9},{9,8},{10,11... | collective-permute-start | bytes 1572872 | tf_op jit(solution)/shard_map/ppermute | solution.py:11
  40.2 12.8 %collective-permute-start.6 = (bf16[128,2176]{1,0:T(8,128)(2,1)S(1)}, bf16[128,2176]{1,0:T(8,128)(2,1)S(1)}, u32[]{:S(2)}, u32[]{:S(2)}) collective-permute-start(bf16[128,2176]{1,0:T(8,128)(2,1)S(1)} %pad_maximum_fusion.1), channel_id=1, source_target_pairs={{0,2},{2,0},{4,6},{6,4},{8,10},{10,8},{12,14},{14,12},{16,18},{18,... | collective-permute-start | bytes 1671176 | tf_op jit(solution)/shard_map/ppermute | solution.py:11
  40.5 1.9 %copy-start.10 = (bf16[1,768,2048]{2,1,0:T(8,128)(2,1)S(1)}, bf16[1,768,2048]{2,1,0:T(8,128)(2,1)}, u32[]{:S(2)}) copy-start(bf16[1,768,2048]{2,1,0:T(8,128)(2,1)} %param.13) | copy-start | bytes 9437188
  40.5 12.4 %collective-permute-start.5 = (bf16[128,2176]{1,0:T(8,128)(2,1)S(1)}, bf16[128,2176]{1,0:T(8,128)(2,1)S(1)}, u32[]{:S(2)}, u32[]{:S(2)}) collective-permute-start(bf16[128,2176]{1,0:T(8,128)(2,1)S(1)} %pad_maximum_fusion), channel_id=1, source_target_pairs={{0,2},{2,0},{4,6},{6,4},{8,10},{10,8},{12,14},{14,12},{16,18},{18,... | collective-permute-start | bytes 1671176 | tf_op jit(solution)/shard_map/ppermute | solution.py:11
  42.4 10.7 %copy-start.11 = (bf16[1,2048,768]{2,1,0:T(8,128)(2,1)S(1)}, bf16[1,2048,768]{2,1,0:T(8,128)(2,1)}, u32[]{:S(2)}) copy-start(bf16[1,2048,768]{2,1,0:T(8,128)(2,1)} %param.11) | copy-start | bytes 9437188
  52.9 12.9 %collective-permute-start.27 = (bf16[256,1024]{1,0:T(8,128)(2,1)S(1)}, bf16[256,1024]{1,0:T(8,128)(2,1)S(1)}, u32[]{:S(2)}, u32[]{:S(2)}) collective-permute-start(bf16[256,1024]{1,0:T(8,128)(2,1)S(1)} %collective-permute-done.26), channel_id=1, source_target_pairs={{0,2},{2,0},{4,6},{6,4},{8,10},{10,8},{12,14},{14,12},{16,18},{18,... | collective-permute-start | bytes 1572872 | tf_op jit(solution)/shard_map/ppermute | solution.py:11
  53.1 1.8 %copy-start.8 = (pred[128]{0:T(512)(128)(4,1)S(1)}, pred[128]{0:T(512)(128)(4,1)}, u32[]{:S(2)}) copy-start(pred[128]{0:T(512)(128)(4,1)} %get-tuple-element.41) | copy-start | bytes 388
  53.1 1.8 %copy-start.9 = (pred[128]{0:T(512)(128)(4,1)S(1)}, pred[128]{0:T(512)(128)(4,1)}, u32[]{:S(2)}) copy-start(pred[128]{0:T(512)(128)(4,1)} %get-tuple-element.42) | copy-start | bytes 388
  57.1 20.0 %collective-permute-start.28 = (bf16[512,768]{1,0:T(8,128)(2,1)S(1)}, bf16[512,768]{1,0:T(8,128)(2,1)S(1)}, u32[]{:S(2)}, u32[]{:S(2)}) collective-permute-start(bf16[512,768]{1,0:T(8,128)(2,1)S(1)} %get-tuple-element.39), channel_id=1, source_target_pairs={{0,1},{1,0},{2,3},{3,2},{4,5},{5,4},{6,7},{7,6},{8,9},{9,8},{10,11... | collective-permute-start | bytes 2359304 | tf_op jit(solution)/shard_map/ppermute | solution.py:11
  60.6 23.7 %collective-permute-start.7 = (bf16[256,2048]{1,0:T(8,128)(2,1)S(1)}, bf16[256,2048]{1,0:T(8,128)(2,1)S(1)}, u32[]{:S(2)}, u32[]{:S(2)}) collective-permute-start(bf16[256,2048]{1,0:T(8,128)(2,1)S(1)} %slice.137), channel_id=1, source_target_pairs={{0,2},{2,0},{4,6},{6,4},{8,10},{10,8},{12,14},{14,12},{16,18},{18,... | collective-permute-start | bytes 3145736 | tf_op jit(solution)/shard_map/ppermute | solution.py:11
  65.5 19.9 %collective-permute-start.20 = (bf16[256,2048]{1,0:T(8,128)(2,1)S(1)}, bf16[256,2048]{1,0:T(8,128)(2,1)S(1)}, u32[]{:S(2)}, u32[]{:S(2)}) collective-permute-start(bf16[256,2048]{1,0:T(8,128)(2,1)S(1)} %slice.148), channel_id=1, source_target_pairs={{0,2},{2,0},{4,6},{6,4},{8,10},{10,8},{12,14},{14,12},{16,18},{18,... | collective-permute-start | bytes 3145736 | tf_op jit(solution)/shard_map/ppermute | solution.py:11
  84.5 9.3 %collective-permute-start.9 = (bf16[64,2048]{1,0:T(8,128)(2,1)S(1)}, bf16[64,2048]{1,0:T(8,128)(2,1)S(1)}, u32[]{:S(2)}, u32[]{:S(2)}) collective-permute-start(bf16[64,2048]{1,0:T(8,128)(2,1)S(1)} %slice.142), channel_id=1, source_target_pairs={{0,4},{2,6},{4,0},{6,2},{8,12},{10,14},{12,8},{14,10},{16,20},{18,... | collective-permute-start | bytes 786440 | tf_op jit(solution)/shard_map/ppermute | solution.py:11
  85.5 12.6 %collective-permute-start.22 = (bf16[64,2048]{1,0:T(8,128)(2,1)S(1)}, bf16[64,2048]{1,0:T(8,128)(2,1)S(1)}, u32[]{:S(2)}, u32[]{:S(2)}) collective-permute-start(bf16[64,2048]{1,0:T(8,128)(2,1)S(1)} %slice.153), channel_id=1, source_target_pairs={{0,4},{2,6},{4,0},{6,2},{8,12},{10,14},{12,8},{14,10},{16,20},{18,... | collective-permute-start | bytes 786440 | tf_op jit(solution)/shard_map/ppermute | solution.py:11
  93.8 26.0 %collective-permute-start.10 = (bf16[32,2048]{1,0:T(8,128)(2,1)S(1)}, bf16[32,2048]{1,0:T(8,128)(2,1)S(1)}, u32[]{:S(2)}, u32[]{:S(2)}) collective-permute-start(bf16[32,2048]{1,0:T(8,128)(2,1)S(1)} %get-tuple-element.23), channel_id=1, source_target_pairs={{0,16},{2,18},{4,20},{6,22},{8,24},{10,26},{12,28},{14,30},{16,0},... | collective-permute-start | bytes 393224 | tf_op jit(solution)/shard_map/ppermute | solution.py:11
  94.6 26.7 %collective-permute-start.11 = (bf16[32,2048]{1,0:T(8,128)(2,1)S(1)}, bf16[32,2048]{1,0:T(8,128)(2,1)S(1)}, u32[]{:S(2)}, u32[]{:S(2)}) collective-permute-start(bf16[32,2048]{1,0:T(8,128)(2,1)S(1)} %get-tuple-element.24), channel_id=1, source_target_pairs={{0,24},{2,26},{4,28},{6,30},{8,16},{10,18},{12,20},{14,22},{16,8},... | collective-permute-start | bytes 393224 | tf_op jit(solution)/shard_map/ppermute | solution.py:11
  96.7 12.7 %collective-permute-start.8 = (bf16[64,2048]{1,0:T(8,128)(2,1)S(1)}, bf16[64,2048]{1,0:T(8,128)(2,1)S(1)}, u32[]{:S(2)}, u32[]{:S(2)}) collective-permute-start(bf16[64,2048]{1,0:T(8,128)(2,1)S(1)} %get-tuple-element.16), channel_id=1, source_target_pairs={{0,8},{2,10},{4,12},{6,14},{8,0},{10,2},{12,4},{14,6},{16,24},{18,... | collective-permute-start | bytes 786440 | tf_op jit(solution)/shard_map/ppermute | solution.py:11
  98.2 27.5 %collective-permute-start.23 = (bf16[32,2048]{1,0:T(8,128)(2,1)S(1)}, bf16[32,2048]{1,0:T(8,128)(2,1)S(1)}, u32[]{:S(2)}, u32[]{:S(2)}) collective-permute-start(bf16[32,2048]{1,0:T(8,128)(2,1)S(1)} %get-tuple-element.21), channel_id=1, source_target_pairs={{0,16},{2,18},{4,20},{6,22},{8,24},{10,26},{12,28},{14,30},{16,0},... | collective-permute-start | bytes 393224 | tf_op jit(solution)/shard_map/ppermute | solution.py:11
  99.2 26.5 %collective-permute-start.24 = (bf16[32,2048]{1,0:T(8,128)(2,1)S(1)}, bf16[32,2048]{1,0:T(8,128)(2,1)S(1)}, u32[]{:S(2)}, u32[]{:S(2)}) collective-permute-start(bf16[32,2048]{1,0:T(8,128)(2,1)S(1)} %get-tuple-element.22), channel_id=1, source_target_pairs={{0,24},{2,26},{4,28},{6,30},{8,16},{10,18},{12,20},{14,22},{16,8},... | collective-permute-start | bytes 393224 | tf_op jit(solution)/shard_map/ppermute | solution.py:11
  109.3 9.9 %collective-permute-start.21 = (bf16[64,2048]{1,0:T(8,128)(2,1)S(1)}, bf16[64,2048]{1,0:T(8,128)(2,1)S(1)}, u32[]{:S(2)}, u32[]{:S(2)}) collective-permute-start(bf16[64,2048]{1,0:T(8,128)(2,1)S(1)} %get-tuple-element.14), channel_id=1, source_target_pairs={{0,8},{2,10},{4,12},{6,14},{8,0},{10,2},{12,4},{14,6},{16,24},{18,... | collective-permute-start | bytes 786440 | tf_op jit(solution)/shard_map/ppermute | solution.py:11
  119.2 5.7 %collective-permute-start.12 = (bf16[32,2048]{1,0:T(8,128)(2,1)S(1)}, bf16[32,2048]{1,0:T(8,128)(2,1)S(1)}, u32[]{:S(2)}, u32[]{:S(2)}) collective-permute-start(bf16[32,2048]{1,0:T(8,128)(2,1)S(1)} %slice_add_fusion.5), channel_id=1, source_target_pairs={{0,4},{2,6},{4,0},{6,2},{8,12},{10,14},{12,8},{14,10},{16,20},{18,... | collective-permute-start | bytes 393224 | tf_op jit(solution)/shard_map/ppermute | solution.py:11
  119.9 6.5 %collective-permute-start.25 = (bf16[32,2048]{1,0:T(8,128)(2,1)S(1)}, bf16[32,2048]{1,0:T(8,128)(2,1)S(1)}, u32[]{:S(2)}, u32[]{:S(2)}) collective-permute-start(bf16[32,2048]{1,0:T(8,128)(2,1)S(1)} %slice_add_fusion.4), channel_id=1, source_target_pairs={{0,4},{2,6},{4,0},{6,2},{8,12},{10,14},{12,8},{14,10},{16,20},{18,... | collective-permute-start | bytes 393224 | tf_op jit(solution)/shard_map/ppermute | solution.py:11

commit v2 on v1

v2 whole, which is shorter than its diff:
```python
import functools

import jax
import jax.numpy as jnp
from jax import lax
from jax.experimental import pallas as pl
from jax.experimental.pallas import tpu as pltpu
from jax.sharding import PartitionSpec as P

LANES = 128
SHARE_TILE = 256


def swap(value, axis, distance):
    size = lax.axis_size(axis)
    return lax.ppermute(value, axis, [(i, i ^ distance) for i in range(size)])


def after(value, *earlier):
    return lax.optimization_barrier((value,) + earlier)[0]


def far_steps(n_expert):
    return list(range(8, n_expert, 4))


def join(*blocks):
    return jnp.concatenate(blocks, axis=0)


def after_all(values, *earlier):
    return lax.optimization_barrier(tuple(values) + earlier)[:len(values)]


class Near:
    def __init__(self, partial):
        self.half, self.rows = partial.shape[0] // 2, partial.shape[0] // 8
        self.kept = partial[:self.half]
        self.sent = swap(partial[self.half:], "expert", 1)

    def core(self, *earlier):
        kept, sent = after_all([self.kept, self.sent], *earlier)
        self.even = kept + sent
        self.from_near = swap(self.even[2 * self.rows:], "expert", 4)

    def pair(self, *earlier):
        even, from_near = after_all([self.even, self.from_near], *earlier)
        self.ready = even[self.rows:2 * self.rows] + from_near[self.rows:]
        self.beside = swap(self.ready, "expert", 2)

    def total(self):
        own, near = self.even[:self.rows], self.from_near[:self.rows]
        return own.astype(jnp.float32) + near.astype(jnp.float32) + self.beside.astype(jnp.float32)


class Far:
    def __init__(self, partial, n_expert):
        self.steps = far_steps(n_expert)
        self.half, self.quarter = partial.shape[0] // 2, partial.shape[0] // 4
        self.kept = partial[:self.half]
        self.sent = swap(partial[self.half:], "expert", 1)

    def core(self, *earlier):
        kept, sent = after_all([self.kept, self.sent], *earlier)
        self.even = kept + sent
        self.crossed = swap(self.even[self.quarter:], "expert", 2)

    def across(self, *earlier):
        even, crossed = after_all([self.even, self.crossed], *earlier)
        self.ready = even[:self.quarter] + crossed
        rows = self.quarter // len(self.steps)
        self.straight = [swap(self.ready[i * rows:(i + 1) * rows], "expert", step) for i, step in enumerate(self.steps)]

    def total(self):
        return sum(part.astype(jnp.float32) for part in self.straight)


def gate_lanes(routes, gate_codes, n_expert):
    experts = jnp.arange(n_expert, dtype=jnp.int32)
    chosen = routes[:, :, None] == experts[None, None, :]
    codes = jnp.sum(jnp.where(chosen, gate_codes[:, :, None], 0), axis=1)
    total = jnp.sum(gate_codes, axis=1, keepdims=True)
    digits = jnp.concatenate([codes // 64, codes % 64, total // 256, total % 256], axis=1)
    return jnp.pad(digits, ((0, 0), (0, LANES - digits.shape[1]))).astype(jnp.bfloat16)


def gate_of_expert(lanes, expert, n_expert):
    values = lanes.astype(jnp.float32)
    index = lax.broadcasted_iota(jnp.int32, values.shape, 1)
    pick = lambda at: jnp.sum(jnp.where(index == at, values, 0.0), axis=1, keepdims=True)
    code = pick(expert) * 64.0 + pick(expert + n_expert)
    total = pick(2 * n_expert) * 256.0 + pick(2 * n_expert + 1)
    return code / total


def dot(left, right, contract):
    return lax.dot_general(left, right, (contract, ((), ())), preferred_element_type=jnp.float32)


def forward(piece, width, expert, n_expert, gate_mat, up_mat, down_mat):
    rows_in, lanes_in = piece[:, :width], piece[:, width:]
    gate = gate_of_expert(lanes_in, expert, n_expert)
    gate_pre = dot(rows_in, gate_mat, ((1,), (0,)))
    up_pre = dot(rows_in, up_mat, ((1,), (0,)))
    sig_gate = jax.nn.sigmoid(gate_pre)
    act_gate = gate_pre * sig_gate * gate
    hidden = (act_gate * up_pre).astype(jnp.bfloat16)
    slope = gate * up_pre * sig_gate * (1.0 + gate_pre * (1.0 - sig_gate))
    out = dot(hidden, down_mat, ((1,), (0,))).astype(jnp.bfloat16)
    return hidden, act_gate, slope, out


def backward(grads_in, act_gate, slope, gate_mat, up_mat, down_mat):
    grad_hidden = dot(grads_in, down_mat, ((1,), (1,)))
    grad_gate_pre = (grad_hidden * slope).astype(jnp.bfloat16)
    grad_up_pre = (grad_hidden * act_gate).astype(jnp.bfloat16)
    grad_rows = dot(grad_gate_pre, gate_mat, ((1,), (1,))) + dot(grad_up_pre, up_mat, ((1,), (1,)))
    return grad_rows.astype(jnp.bfloat16)


def share_kernel(count, place_ref, *refs):
    out_ref = refs[-1]
    total = None
    for index in range(count):
        grads, hidden = refs[2 * index][...], refs[2 * index + 1][...]
        term = dot(grads, hidden, ((0,), (0,)))
        total = term if total is None else total + term
    out_ref[...] = total[:, None, :]


def weight_share(place, share, own, others):
    tiles = share // SHARE_TILE
    specs, operands = [], []
    for grads, hidden in own:
        specs.append(pl.BlockSpec((grads.shape[0], SHARE_TILE), lambda i, at: (0, at[0] * tiles + i)))
        specs.append(pl.BlockSpec(hidden.shape, lambda i, at: (0, 0)))
        operands += [grads, hidden]
    for grads, hidden in others:
        specs.append(pl.BlockSpec((grads.shape[0], SHARE_TILE), lambda i, at: (0, i)))
        specs.append(pl.BlockSpec(hidden.shape, lambda i, at: (0, 0)))
        operands += [grads, hidden]
    units = operands[1].shape[1]
    rows = sum(grads.shape[0] for grads, _ in own + others)
    return pl.pallas_call(
        functools.partial(share_kernel, len(own) + len(others)),
        out_shape=jax.ShapeDtypeStruct((share, 1, units), jnp.float32),
        grid_spec=pltpu.PrefetchScalarGridSpec(
            num_scalar_prefetch=1,
            grid=(tiles,),
            in_specs=specs,
            out_specs=pl.BlockSpec((SHARE_TILE, 1, units), lambda i, at: (i, 0, 0)),
        ),
        compiler_params=pltpu.CompilerParams(vmem_limit_bytes=40 * 1024 * 1024),
        cost_estimate=pl.CostEstimate(flops=2 * share * units * rows, bytes_accessed=4 * share * units + 2 * rows * (share + units), transcendentals=0),
    )(jnp.reshape(place, (1,)).astype(jnp.int32), *operands)


def shards(tokens, out_grad, routes, gate_codes, w_gate, w_up, w_down):
    rows, width = tokens.shape
    n_expert = lax.axis_size("expert")
    n_edata = lax.axis_size("edata")
    expert = lax.axis_index("expert")
    place = lax.axis_index("edata")
    share = width // n_edata
    gate_mat, up_mat, down_mat = w_gate[0], w_up[0], w_down[0]
    steps = far_steps(n_expert)

    mats = (gate_mat, up_mat, down_mat)
    block = jnp.concatenate([tokens, gate_lanes(routes, gate_codes, n_expert)], axis=1)
    straight = [swap(block, "expert", step) for step in steps]
    pair = join(block, swap(block, "expert", 2))
    near = swap(pair, "expert", 4)
    grad_beside = swap(after(out_grad, pair), "expert", 2)
    far_straight = join(*after_all(straight, pair))
    across = swap(far_straight, "expert", 2)
    near_even = join(*after_all([pair, near], far_straight))
    near_odd = swap(near_even, "expert", 1)
    grad_block = after(out_grad, near_even)
    grad_straight = [swap(grad_block, "expert", step) for step in steps]
    grad_pair = join(*after_all([out_grad, grad_beside], near_even))
    grad_near = swap(grad_pair, "expert", 4)

    hidden_n, act_n, slope_n, out_n = forward(join(*after_all([near_even, near_odd], grad_pair)), width, expert, n_expert, *mats)
    far_even = join(*after_all([far_straight, across], out_n))
    far_odd = swap(far_even, "expert", 1)
    mixed_n = Near(out_n)
    mixed_n.core(far_even)
    hidden_f, act_f, slope_f, out_f = forward(join(*after_all([far_even, far_odd], mixed_n.even)), width, expert, n_expert, *mats)
    mixed_f = Far(out_f, n_expert)

    grad_far_straight = join(*after_all(grad_straight, out_f))
    grad_across = swap(grad_far_straight, "expert", 2)
    mixed_f.core(grad_far_straight)
    grad_near_even = join(*after_all([grad_pair, grad_near], mixed_f.even))
    grad_near_odd = swap(grad_near_even, "expert", 1)
    mixed_n.pair(grad_near_even)
    grads_n = join(*after_all([grad_near_even, grad_near_odd], mixed_n.ready))
    rows_n = backward(grads_n, act_n, slope_n, *mats)
    input_n = Near(rows_n)
    grad_far_even = join(*after_all([grad_far_straight, grad_across], rows_n))
    grad_far_odd = swap(grad_far_even, "expert", 1)
    mixed_f.across(grad_far_even)
    input_n.core(mixed_f.ready)
    grads_f = join(*after_all([grad_far_even, grad_far_odd], input_n.even))
    rows_f = backward(grads_f, act_f, slope_f, *mats)
    input_f = Far(rows_f, n_expert)
    input_n.pair(rows_f)
    input_f.core(input_n.ready)
    input_f.across(input_f.even)

    others = []
    for step in range(1, n_edata):
        there = (place ^ step) * share
        for hidden, even in ((hidden_n, grad_near_even), (hidden_f, grad_far_even)):
            hidden_other = swap(hidden, "edata", step)
            other_even = swap(lax.dynamic_slice_in_dim(even, there, share, 1), "edata", step)
            others.append((join(other_even, swap(other_even, "expert", 1)), hidden_other))
    grad_down = weight_share(place, share, [(grads_n, hidden_n), (grads_f, hidden_f)], others)
    mixed = (mixed_n.total() + mixed_f.total()).astype(jnp.bfloat16)
    input_grad = (input_n.total() + input_f.total()).astype(jnp.bfloat16)
    return mixed, input_grad, grad_down


def solution(mesh):
    by_token = P(("expert", "edata"), None)
    by_expert = P("expert", None, None)
    return jax.shard_map(
        shards,
        mesh=mesh,
        in_specs=(by_token,) * 4 + (by_expert,) * 3,
        out_specs=(by_token, by_token, P("edata", "expert", None)),
        check_vma=False,
    )
```

time: 127 us -> 112 us (0.88)
  waiting for transfers between devices: 53.1 us -> 37.1 us
  Pallas kernels: 0 us -> 4.14 us
  local copies, waits for them, and re-layouts: 12.8 us -> 9.81 us
  other arithmetic: 10.6 us -> 8.9 us
    ppermute x29 -> x34, waiting for transfers between devices: 53.1 us -> 37.1 us  [swap(): return lax.ppermute(value, axis, [(i, i ^ distance) for i in range(size)])]
    unnamed x38 -> x42, local copies, waits for them, and re-layouts: 12.4 us -> 5.12 us
    pallas_call x0 -> x1, Pallas kernels: none -> 4.14 us  [weight_share(): pl.pallas_call(functools.partial(share_kernel, len(own) + len(others)), o...]
    concatenate x9 -> x4, other arithmetic: 6.53 us -> 2.79 us  [the longest x1 1.57 us: shards(): jnp.concatenate([tokens, gate_lanes(routes, gate_codes, n_expert)], axis=1)]
    add x6 -> x8, other arithmetic: 0.35 us -> 2.6 us  [the longest x4 2.51 us: core(): self.even = kept + sent]
    slice x6 -> x10, local copies, waits for them, and re-layouts: 0.28 us -> 2.49 us  [the longest x4 1.42 us: __init__(): self.sent = swap(partial[self.half:], 'expert', 1)]
    concatenate x3 -> x11, local copies, waits for them, and re-layouts: 0.13 us -> 2.14 us  [join(): return jnp.concatenate(blocks, axis=0)]
    dot_general x8 -> x12, matrix products: 14.2 us -> 14.7 us  [dot(): lax.dot_general(left, right, (contract, ((), ())), preferred_element_type...]
  transfers between devices with their start and end apart: 29 -> 34, of which waited for: 10 -> 15; matrix products, arithmetic and copies ran while one was open for 28% -> 25% of each run, Pallas kernels for 0% -> 4%
where the time goes in v2:
time: 112 us; the launch traced here: 111 us
  waiting for transfers between devices  37.1 us (33%)
  starting transfers between devices  35.2 us (31%)
  matrix products  14.7 us (13%)
  local copies, waits for them, and re-layouts  9.81 us (9%)
  other arithmetic  8.9 us (8%)
  Pallas kernels  4.14 us (4%)
  between operations  1.25 us (1%)
    ppermute x34, waiting for transfers between devices, swap(): return lax.ppermute(value, axis, [(i, i ^ distance) for i in range(size)])  37.1 us
    ppermute x34, starting transfers between devices, swap(): return lax.ppermute(value, axis, [(i, i ^ distance) for i in range(size)])  35.2 us
    dot_general x12, matrix products, dot(): lax.dot_general(left, right, (contract, ((), ())), preferred_element_type...  14.7 us
    unnamed x42, local copies, waits for them, and re-layouts  5.12 us
    pallas_call x1, Pallas kernels, weight_share(): pl.pallas_call(functools.partial(share_kernel, len(own) + len(others)), o...  4.14 us
    add x4, other arithmetic, core(): self.even = kept + sent  2.51 us
  transfers between devices with their start and end apart: 34, of which 15 were waited for; matrix products, arithmetic and copies ran while one was open for 25% of the time, Pallas kernels for 4%

profile of v2, /device:TPU:0, one launch (start us, length us, event | category | flops | bytes accessed | tf_op | source)
XLA Modules:
  0.0 111.1 jit_solution(9967183126980925418)
XLA Ops:
  2.5 1.6 %pad_maximum_fusion.3 = bf16[32,2176]{1,0:T(8,128)(2,1)} fusion(bf16[32,128]{1,0:T(8,128)(2,1)S(1)} %pad.5.clone, bf16[32,2048]{1,0:T(8,128)(2,1)} %param.7), kind=kLoop, calls=%fused_computation.63 | loop fusion | flops 278528 | bytes 278528 | tf_op jit(solution)/shard_map/concatenate | solution.py:169
  4.0 3.0 %collective-permute-start = (bf16[32,2176]{1,0:T(8,128)(2,1)}, bf16[32,2176]{1,0:T(8,128)(2,1)}, u32[]{:S(2)}, u32[]{:S(2)}) collective-permute-start(bf16[32,2176]{1,0:T(8,128)(2,1)} %pad_maximum_fusion.3), channel_id=1, source_target_pairs={{0,4},{2,6},{4,0},{6,2},{8,12},{10,14},{12,8},{14,10},{16,20},{18,... | collective-permute-start | bytes 417800 | tf_op jit(solution)/shard_map/ppermute | solution.py:16
  7.0 2.6 %collective-permute-start.2 = (bf16[32,2176]{1,0:T(8,128)(2,1)}, bf16[32,2176]{1,0:T(8,128)(2,1)}, u32[]{:S(2)}, u32[]{:S(2)}) collective-permute-start(bf16[32,2176]{1,0:T(8,128)(2,1)} %pad_maximum_fusion.3), channel_id=1, source_target_pairs={{0,16},{2,18},{4,20},{6,22},{8,24},{10,26},{12,28},{14,30},{16,0},... | collective-permute-start | bytes 417800 | tf_op jit(solution)/shard_map/ppermute | solution.py:16
  9.6 1.3 %collective-permute-start.3 = (bf16[32,2176]{1,0:T(8,128)(2,1)}, bf16[32,2176]{1,0:T(8,128)(2,1)}, u32[]{:S(2)}, u32[]{:S(2)}) collective-permute-start(bf16[32,2176]{1,0:T(8,128)(2,1)} %pad_maximum_fusion.3), channel_id=1, source_target_pairs={{0,24},{2,26},{4,28},{6,30},{8,16},{10,18},{12,20},{14,22},{16,8},... | collective-permute-start | bytes 417800 | tf_op jit(solution)/shard_map/ppermute | solution.py:16
  11.0 1.1 %pad_maximum_fusion.2 = bf16[64,2176]{1,0:T(8,128)(2,1)S(1)} fusion(bf16[32,2176]{1,0:T(8,128)(2,1)} %collective-permute-done, bf16[32,128]{1,0:T(8,128)(2,1)S(1)} %pad.5.clone, bf16[32,2048]{1,0:T(8,128)(2,1)} %param.7), kind=kLoop, calls=%fused_computation.50 | loop fusion | flops 835584 | bytes 557056 | tf_op jit(solution)/shard_map/concatenate | solution.py:28
  12.1 1.7 %collective-permute-start.1 = (bf16[64,2176]{1,0:T(8,128)(2,1)S(1)}, bf16[64,2176]{1,0:T(8,128)(2,1)S(1)}, u32[]{:S(2)}, u32[]{:S(2)}) collective-permute-start(bf16[64,2176]{1,0:T(8,128)(2,1)S(1)} %pad_maximum_fusion.2), channel_id=1, source_target_pairs={{0,8},{2,10},{4,12},{6,14},{8,0},{10,2},{12,4},{14,6},{16,24},{18,... | collective-permute-start | bytes 835592 | tf_op jit(solution)/shard_map/ppermute | solution.py:16
  13.8 6.7 %collective-permute-done.2 = bf16[32,2176]{1,0:T(8,128)(2,1)} collective-permute-done((bf16[32,2176]{1,0:T(8,128)(2,1)}, bf16[32,2176]{1,0:T(8,128)(2,1)}, u32[]{:S(2)}, u32[]{:S(2)}) %collective-permute-start.2) | collective-permute-done | bytes 139296 | tf_op jit(solution)/shard_map/ppermute | solution.py:16
  22.0 0.9 constant_dynamic-update-slice_fusion
  22.9 1.7 %collective-permute-done.1 = bf16[64,2176]{1,0:T(8,128)(2,1)S(1)} collective-permute-done((bf16[64,2176]{1,0:T(8,128)(2,1)S(1)}, bf16[64,2176]{1,0:T(8,128)(2,1)S(1)}, u32[]{:S(2)}, u32[]{:S(2)}) %collective-permute-start.1) | collective-permute-done | bytes 278560 | tf_op jit(solution)/shard_map/ppermute | solution.py:16
  25.7 1.0 collective-permute-done.5
  27.8 1.0 fusion.22
  29.0 1.9 %multiply_convert_fusion.5 = (bf16[256,768]{1,0:T(8,128)(2,1)S(1)}, f32[256,768]{1,0:T(8,128)}) fusion(f32[256]{0:T(256)S(1)} %add_divide_fusion.3, f32[256,768]{1,0:T(8,128)S(1)} %fusion.22, bf16[1,2048,768]{2,1,0:T(8,128)(2,1)S(1)} %copy-done, bf16[256,2176]{1,0:T(8,128)(2,1)S(1)} %constant_dynamic-update-slice_fusion.6), kind=kOutput, calls=%fused_computation.41 | convolution fusion | flops 806682624 | bytes 6161408 | tf_op jit(solution)/shard_map/dot_general | solution.py:97
  31.0 1.0 fusion.36
  32.0 1.9 %collective-permute-done.7 = bf16[64,2176]{1,0:T(8,128)(2,1)S(1)} collective-permute-done((bf16[64,2176]{1,0:T(8,128)(2,1)S(1)}, bf16[64,2176]{1,0:T(8,128)(2,1)S(1)}, u32[]{:S(2)}, u32[]{:S(2)}) %collective-permute-start.7) | collective-permute-done | bytes 278560 | tf_op jit(solution)/shard_map/ppermute | solution.py:16
  34.6 4.0 %collective-permute-start.12 = (bf16[32,2048]{1,0:T(8,128)(2,1)}, bf16[32,2048]{1,0:T(8,128)(2,1)}, u32[]{:S(2)}, u32[]{:S(2)}) collective-permute-start(bf16[32,2048]{1,0:T(8,128)(2,1)} %param.8), channel_id=1, source_target_pairs={{0,16},{2,18},{4,20},{6,22},{8,24},{10,26},{12,28},{14,30},{16,0},... | collective-permute-start | bytes 393224 | tf_op jit(solution)/shard_map/ppermute | solution.py:16
  39.0 0.9 add.144
  40.1 1.0 fusion.20
  41.2 1.9 %multiply_convert_fusion.4 = (bf16[256,768]{1,0:T(8,128)(2,1)S(1)}, f32[256,768]{1,0:T(8,128)}) fusion(f32[256]{0:T(256)S(1)} %add_divide_fusion.2, f32[256,768]{1,0:T(8,128)S(1)} %fusion.20, bf16[1,2048,768]{2,1,0:T(8,128)(2,1)S(1)} %copy-done, bf16[256,2176]{1,0:T(8,128)(2,1)S(1)} %constant_dynamic-update-slice_fusion.10), kind=kOutput, calls=%fused_computation.38 | convolution fusion | flops 806682624 | bytes 6161408 | tf_op jit(solution)/shard_map/dot_general | solution.py:97
  43.1 1.0 fusion.39
  44.1 1.1 %fusion.68 = (bf16[128,2048]{1,0:T(8,128)(2,1)}, bf16[128,2048]{1,0:T(8,128)(2,1)}) fusion(bf16[256,2048]{1,0:T(8,128)(2,1)S(1)} %fusion.39), kind=kLoop, calls=%fused_computation.129 | loop fusion | bytes 2097152 | tf_op jit(solution)/shard_map/slice | solution.py:61
  45.5 1.0 slice.125
  46.4 2.0 %collective-permute-start.8 = (bf16[64,2048]{1,0:T(8,128)(2,1)S(1)}, bf16[64,2048]{1,0:T(8,128)(2,1)S(1)}, u32[]{:S(2)}, u32[]{:S(2)}) collective-permute-start(bf16[64,2048]{1,0:T(8,128)(2,1)S(1)} %slice.125), channel_id=1, source_target_pairs={{0,8},{2,10},{4,12},{6,14},{8,0},{10,2},{12,4},{14,6},{16,24},{18,... | collective-permute-start | bytes 786440 | tf_op jit(solution)/shard_map/ppermute | solution.py:16
  50.4 1.3 %add.149 = bf16[128,2048]{1,0:T(8,128)(2,1)S(1)} add(bf16[128,2048]{1,0:T(8,128)(2,1)} %get-tuple-element.61, bf16[128,2048]{1,0:T(8,128)(2,1)} %collective-permute-done.11) | non-fusion elementwise | flops 262144 | bytes 1572864 | tf_op jit(solution)/shard_map/add | solution.py:65
  51.7 3.0 %collective-permute-done.9 = bf16[64,2048]{1,0:T(8,128)(2,1)S(1)} collective-permute-done((bf16[64,2048]{1,0:T(8,128)(2,1)}, bf16[64,2048]{1,0:T(8,128)(2,1)S(1)}, u32[]{:S(2)}, u32[]{:S(2)}) %collective-permute-start.9) | collective-permute-done | bytes 262176 | tf_op jit(solution)/shard_map/ppermute | solution.py:16
  54.7 1.0 constant_dynamic-update-slice_fusion.15
  55.7 1.6 %collective-permute-start.28 = (bf16[128,1024]{1,0:T(8,128)(2,1)S(1)}, bf16[128,1024]{1,0:T(8,128)(2,1)S(1)}, u32[]{:S(2)}, u32[]{:S(2)}) collective-permute-start(bf16[128,1024]{1,0:T(8,128)(2,1)S(1)} %constant_dynamic-slice_fusion), channel_id=1, source_target_pairs={{0,1},{1,0},{2,3},{3,2},{4,5},{5,4},{6,7},{7,6},{8,9},{9,8},{10,11... | collective-permute-start | bytes 786440 | tf_op jit(solution)/shard_map/ppermute | solution.py:16
  57.6 2.2 %collective-permute-done.8 = bf16[64,2048]{1,0:T(8,128)(2,1)S(1)} collective-permute-done((bf16[64,2048]{1,0:T(8,128)(2,1)S(1)}, bf16[64,2048]{1,0:T(8,128)(2,1)S(1)}, u32[]{:S(2)}, u32[]{:S(2)}) %collective-permute-start.8) | collective-permute-done | bytes 262176 | tf_op jit(solution)/shard_map/ppermute | solution.py:16
  60.1 3.0 %collective-permute-done.28 = bf16[128,1024]{1,0:T(8,128)(2,1)S(1)} collective-permute-done((bf16[128,1024]{1,0:T(8,128)(2,1)S(1)}, bf16[128,1024]{1,0:T(8,128)(2,1)S(1)}, u32[]{:S(2)}, u32[]{:S(2)}) %collective-permute-start.28) | collective-permute-done | bytes 262176 | tf_op jit(solution)/shard_map/ppermute | solution.py:16
  63.6 1.1 %collective-permute-done.29 = bf16[128,1024]{1,0:T(8,128)(2,1)S(1)} collective-permute-done((bf16[128,1024]{1,0:T(8,128)(2,1)S(1)}, bf16[128,1024]{1,0:T(8,128)(2,1)S(1)}, u32[]{:S(2)}, u32[]{:S(2)}) %collective-permute-start.29) | collective-permute-done | bytes 262176 | tf_op jit(solution)/shard_map/ppermute | solution.py:16
  64.9 1.0 fusion.2
  65.9 1.1 %fusion.10 = f32[256,2048]{1,0:T(8,128)S(1)} fusion(bf16[1,2048,768]{2,1,0:T(8,128)(2,1)S(1)} %copy-done, f32[256,768]{1,0:T(8,128)S(1)} %fusion.2, f32[256,768]{1,0:T(8,128)S(1)} %copy-done.10, f32[256]{0:T(256)S(1)} %add_divide_fusion.3), kind=kOutput, calls=%fused_computation.10 | convolution fusion | flops 806682624 | bytes 6816768 | tf_op jit(solution)/shard_map/dot_general | solution.py:97
  68.0 1.2 %fusion.33 = bf16[256,2048]{1,0:T(8,128)(2,1)S(1)} fusion(f32[256,2048]{1,0:T(8,128)S(1)} %fusion.10, bf16[1,2048,768]{2,1,0:T(8,128)(2,1)S(1)} %copy-done.8, f32[256,768]{1,0:T(8,128)S(1)} %fusion.2, f32[256,768]{1,0:T(8,128)S(1)} %copy-done.10, f32[256,768]{1,0:T(8,128)S(1)} %copy-done.13, f32[256]{0:T(256)S(1)} %add_divide_fusion.3), kind=kOutput, calls=%fused_computation.27 | convolution fusion | flops 808517632 | bytes 8651776 | tf_op jit(solution)/shard_map/dot_general | solution.py:97
  70.1 1.3 %collective-permute-done.15 = bf16[64,2048]{1,0:T(8,128)(2,1)S(1)} collective-permute-done((bf16[64,2048]{1,0:T(8,128)(2,1)S(1)}, bf16[64,2048]{1,0:T(8,128)(2,1)S(1)}, u32[]{:S(2)}, u32[]{:S(2)}) %collective-permute-start.15) | collective-permute-done | bytes 262176 | tf_op jit(solution)/shard_map/ppermute | solution.py:16
  72.2 1.2 %fusion = f32[256,768]{1,0:T(8,128)S(1)} fusion(bf16[256,2048]{1,0:T(8,128)(2,1)S(1)} %constant_dynamic-update-slice_fusion.20.refs_2_, bf16[1,768,2048]{2,1,0:T(8,128)(2,1)S(1)} %copy-done.6), kind=kOutput, calls=%fused_computation | convolution fusion | flops 805306368 | bytes 4980736 | tf_op jit(solution)/shard_map/dot_general | solution.py:97
  73.5 1.1 %fusion.8 = f32[256,2048]{1,0:T(8,128)S(1)} fusion(bf16[1,2048,768]{2,1,0:T(8,128)(2,1)S(1)} %copy-done, f32[256,768]{1,0:T(8,128)S(1)} %fusion, f32[256,768]{1,0:T(8,128)S(1)} %copy-done.12, f32[256]{0:T(256)S(1)} %add_divide_fusion.2), kind=kOutput, calls=%fused_computation.8 | convolution fusion | flops 806682624 | bytes 6816768 | tf_op jit(solution)/shard_map/dot_general | solution.py:97
  74.6 1.0 collective-permute-start.21
  75.7 1.2 %fusion.30 = bf16[256,2048]{1,0:T(8,128)(2,1)S(1)} fusion(f32[256,2048]{1,0:T(8,128)S(1)} %fusion.8, bf16[1,2048,768]{2,1,0:T(8,128)(2,1)S(1)} %copy-done.8, f32[256,768]{1,0:T(8,128)S(1)} %fusion, f32[256,768]{1,0:T(8,128)S(1)} %copy-done.12, f32[256,768]{1,0:T(8,128)S(1)} %copy-done.14, f32[256]{0:T(256)S(1)} %add_divide_fusion.2), kind=kOutput, calls=%fused_computation.26 | convolution fusion | flops 808517632 | bytes 8651776 | tf_op jit(solution)/shard_map/dot_general | solution.py:97
  77.1 1.5 %collective-permute-start.31 = (bf16[128,1024]{1,0:T(8,128)(2,1)S(1)}, bf16[128,1024]{1,0:T(8,128)(2,1)S(1)}, u32[]{:S(2)}, u32[]{:S(2)}) collective-permute-start(bf16[128,1024]{1,0:T(8,128)(2,1)S(1)} %constant_dynamic-slice_fusion.1), channel_id=1, source_target_pairs={{0,1},{1,0},{2,3},{3,2},{4,5},{5,4},{6,7},{7,6},{8,9},{9,8},{10,11... | collective-permute-start | bytes 786440 | tf_op jit(solution)/shard_map/ppermute | solution.py:16
  78.7 3.0 %collective-permute-start.18 = (bf16[32,2048]{1,0:T(8,128)(2,1)S(1)}, bf16[32,2048]{1,0:T(8,128)(2,1)S(1)}, u32[]{:S(2)}, u32[]{:S(2)}) collective-permute-start(bf16[32,2048]{1,0:T(8,128)(2,1)S(1)} %get-tuple-element.101), channel_id=1, source_target_pairs={{0,16},{2,18},{4,20},{6,22},{8,24},{10,26},{12,28},{14,30},{16,0},... | collective-permute-start | bytes 393224 | tf_op jit(solution)/shard_map/ppermute | solution.py:16
  81.6 2.9 %collective-permute-done.21 = bf16[64,2048]{1,0:T(8,128)(2,1)S(1)} collective-permute-done((bf16[64,2048]{1,0:T(8,128)(2,1)S(1)}, bf16[64,2048]{1,0:T(8,128)(2,1)S(1)}, u32[]{:S(2)}, u32[]{:S(2)}) %collective-permute-start.21) | collective-permute-done | bytes 262176 | tf_op jit(solution)/shard_map/ppermute | solution.py:16
  84.6 2.9 %collective-permute-start.19 = (bf16[32,2048]{1,0:T(8,128)(2,1)S(1)}, bf16[32,2048]{1,0:T(8,128)(2,1)S(1)}, u32[]{:S(2)}, u32[]{:S(2)}) collective-permute-start(bf16[32,2048]{1,0:T(8,128)(2,1)S(1)} %get-tuple-element.102), channel_id=1, source_target_pairs={{0,24},{2,26},{4,28},{6,30},{8,16},{10,18},{12,20},{14,22},{16,8},... | collective-permute-start | bytes 393224 | tf_op jit(solution)/shard_map/ppermute | solution.py:16
  87.5 2.0 %collective-permute-start.30 = (bf16[256,768]{1,0:T(8,128)(2,1)S(1)}, bf16[256,768]{1,0:T(8,128)(2,1)S(1)}, u32[]{:S(2)}, u32[]{:S(2)}) collective-permute-start(bf16[256,768]{1,0:T(8,128)(2,1)S(1)} %get-tuple-element.107.refs_1_), channel_id=1, source_target_pairs={{0,1},{1,0},{2,3},{3,2},{4,5},{5,4},{6,7},{7,6},{8,9},{9,8},{10,11... | collective-permute-start | bytes 1179656 | tf_op jit(solution)/shard_map/ppermute | solution.py:16
  89.8 1.7 %collective-permute-done.18 = bf16[32,2048]{1,0:T(8,128)(2,1)S(1)} collective-permute-done((bf16[32,2048]{1,0:T(8,128)(2,1)S(1)}, bf16[32,2048]{1,0:T(8,128)(2,1)S(1)}, u32[]{:S(2)}, u32[]{:S(2)}) %collective-permute-start.18) | collective-permute-done | bytes 131104 | tf_op jit(solution)/shard_map/ppermute | solution.py:16
  92.4 2.1 %collective-permute-start.23 = (bf16[32,2048]{1,0:T(8,128)(2,1)S(1)}, bf16[32,2048]{1,0:T(8,128)(2,1)S(1)}, u32[]{:S(2)}, u32[]{:S(2)}) collective-permute-start(bf16[32,2048]{1,0:T(8,128)(2,1)S(1)} %slice_add_fusion.2), channel_id=1, source_target_pairs={{0,4},{2,6},{4,0},{6,2},{8,12},{10,14},{12,8},{14,10},{16,20},{18,... | collective-permute-start | bytes 393224 | tf_op jit(solution)/shard_map/ppermute | solution.py:16
  94.5 5.5 %collective-permute-done.25 = bf16[64,2048]{1,0:T(8,128)(2,1)S(1)} collective-permute-done((bf16[64,2048]{1,0:T(8,128)(2,1)S(1)}, bf16[64,2048]{1,0:T(8,128)(2,1)S(1)}, u32[]{:S(2)}, u32[]{:S(2)}) %collective-permute-start.25) | collective-permute-done | bytes 262176 | tf_op jit(solution)/shard_map/ppermute | solution.py:16
  100.1 1.8 %collective-permute-start.27 = (bf16[32,2048]{1,0:T(8,128)(2,1)S(1)}, bf16[32,2048]{1,0:T(8,128)(2,1)S(1)}, u32[]{:S(2)}, u32[]{:S(2)}) collective-permute-start(bf16[32,2048]{1,0:T(8,128)(2,1)S(1)} %get-tuple-element.100), channel_id=1, source_target_pairs={{0,24},{2,26},{4,28},{6,30},{8,16},{10,18},{12,20},{14,22},{16,8},... | collective-permute-start | bytes 393224 | tf_op jit(solution)/shard_map/ppermute | solution.py:16
  101.9 4.3 %collective-permute-done.33.refs_7_ = bf16[256,768]{1,0:T(8,128)(2,1)S(1)} collective-permute-done((bf16[256,768]{1,0:T(8,128)(2,1)S(1)}, bf16[256,768]{1,0:T(8,128)(2,1)S(1)}, u32[]{:S(2)}, u32[]{:S(2)}) %collective-permute-start.33) | collective-permute-done | bytes 393248 | tf_op jit(solution)/shard_map/ppermute | solution.py:16
  106.2 4.1 %shard_map.94 = f32[1024,1,768]{2,1,0:T(1,128)} custom-call(s32[1]{0:T(128)} %bitcast.4.place_ref, bf16[256,2048]{1,0:T(8,128)(2,1)S(1)} %constant_dynamic-update-slice_fusion.16.refs_0_, bf16[256,768]{1,0:T(8,128)(2,1)S(1)} %get-tuple-element.107.refs_1_, bf16[256,2048]{1,0:T(8,128)(2,1)S(1)} %constant_dynamic-update-slice_fusion.20.refs_2_, ...), custom_call_target="tpu_custom_call" | custom-call | flops 1610612736 | bytes 6815744 | tf_op jit(solution)/shard_map/pallas_call | solution.py:144
  (124 shorter events, 15.2 us)
Async XLA Ops:
  0.6 28.3 %copy-start = (bf16[1,2048,768]{2,1,0:T(8,128)(2,1)S(1)}, bf16[1,2048,768]{2,1,0:T(8,128)(2,1)}, u32[]{:S(2)}) copy-start(bf16[1,2048,768]{2,1,0:T(8,128)(2,1)} %param.12) | copy-start | bytes 9437188
  4.0 7.0 %collective-permute-start = (bf16[32,2176]{1,0:T(8,128)(2,1)}, bf16[32,2176]{1,0:T(8,128)(2,1)}, u32[]{:S(2)}, u32[]{:S(2)}) collective-permute-start(bf16[32,2176]{1,0:T(8,128)(2,1)} %pad_maximum_fusion.3), channel_id=1, source_target_pairs={{0,4},{2,6},{4,0},{6,2},{8,12},{10,14},{12,8},{14,10},{16,20},{18,... | collective-permute-start | bytes 417800 | tf_op jit(solution)/shard_map/ppermute | solution.py:16
  7.0 13.5 %collective-permute-start.2 = (bf16[32,2176]{1,0:T(8,128)(2,1)}, bf16[32,2176]{1,0:T(8,128)(2,1)}, u32[]{:S(2)}, u32[]{:S(2)}) collective-permute-start(bf16[32,2176]{1,0:T(8,128)(2,1)} %pad_maximum_fusion.3), channel_id=1, source_target_pairs={{0,16},{2,18},{4,20},{6,22},{8,24},{10,26},{12,28},{14,30},{16,0},... | collective-permute-start | bytes 417800 | tf_op jit(solution)/shard_map/ppermute | solution.py:16
  9.6 11.0 %collective-permute-start.3 = (bf16[32,2176]{1,0:T(8,128)(2,1)}, bf16[32,2176]{1,0:T(8,128)(2,1)}, u32[]{:S(2)}, u32[]{:S(2)}) collective-permute-start(bf16[32,2176]{1,0:T(8,128)(2,1)} %pad_maximum_fusion.3), channel_id=1, source_target_pairs={{0,24},{2,26},{4,28},{6,30},{8,16},{10,18},{12,20},{14,22},{16,8},... | collective-permute-start | bytes 417800 | tf_op jit(solution)/shard_map/ppermute | solution.py:16
  10.9 16.8 %copy-start.7 = (bf16[1,2048,768]{2,1,0:T(8,128)(2,1)S(1)}, bf16[1,2048,768]{2,1,0:T(8,128)(2,1)}, u32[]{:S(2)}) copy-start(bf16[1,2048,768]{2,1,0:T(8,128)(2,1)} %param.11) | copy-start | bytes 9437188
  12.1 12.5 %collective-permute-start.1 = (bf16[64,2176]{1,0:T(8,128)(2,1)S(1)}, bf16[64,2176]{1,0:T(8,128)(2,1)S(1)}, u32[]{:S(2)}, u32[]{:S(2)}) collective-permute-start(bf16[64,2176]{1,0:T(8,128)(2,1)S(1)} %pad_maximum_fusion.2), channel_id=1, source_target_pairs={{0,8},{2,10},{4,12},{6,14},{8,0},{10,2},{12,4},{14,6},{16,24},{18,... | collective-permute-start | bytes 835592 | tf_op jit(solution)/shard_map/ppermute | solution.py:16
  21.5 5.2 %collective-permute-start.5 = (bf16[32,2048]{1,0:T(8,128)(2,1)}, bf16[32,2048]{1,0:T(8,128)(2,1)S(1)}, u32[]{:S(2)}, u32[]{:S(2)}) collective-permute-start(bf16[32,2048]{1,0:T(8,128)(2,1)} %param.8), channel_id=1, source_target_pairs={{0,4},{2,6},{4,0},{6,2},{8,12},{10,14},{12,8},{14,10},{16,20},{18,... | collective-permute-start | bytes 393224 | tf_op jit(solution)/shard_map/ppermute | solution.py:16
  24.7 3.0 %collective-permute-start.4 = (bf16[128,2176]{1,0:T(8,128)(2,1)S(1)}, bf16[128,2176]{1,0:T(8,128)(2,1)S(1)}, u32[]{:S(2)}, u32[]{:S(2)}) collective-permute-start(bf16[128,2176]{1,0:T(8,128)(2,1)S(1)} %constant_dynamic-update-slice_fusion.2), channel_id=1, source_target_pairs={{0,2},{2,0},{4,6},{6,4},{8,10},{10,8},{12,14},{14,12},{16,18},{18,... | collective-permute-start | bytes 1671176 | tf_op jit(solution)/shard_map/ppermute | solution.py:16
  24.8 9.1 %collective-permute-start.7 = (bf16[64,2176]{1,0:T(8,128)(2,1)S(1)}, bf16[64,2176]{1,0:T(8,128)(2,1)S(1)}, u32[]{:S(2)}, u32[]{:S(2)}) collective-permute-start(bf16[64,2176]{1,0:T(8,128)(2,1)S(1)} %constant_dynamic-update-slice_fusion), channel_id=1, source_target_pairs={{0,4},{2,6},{4,0},{6,2},{8,12},{10,14},{12,8},{14,10},{16,20},{18,... | collective-permute-start | bytes 835592 | tf_op jit(solution)/shard_map/ppermute | solution.py:16
  28.8 2.1 %copy-start.9 = (f32[256,768]{1,0:T(8,128)}, f32[256,768]{1,0:T(8,128)S(1)}, u32[]{:S(2)}) copy-start(f32[256,768]{1,0:T(8,128)S(1)} %fusion.22) | copy-start | bytes 2359300
  29.0 2.0 %copy-start.5 = (bf16[1,768,2048]{2,1,0:T(8,128)(2,1)S(1)}, bf16[1,768,2048]{2,1,0:T(8,128)(2,1)}, u32[]{:S(2)}) copy-start(bf16[1,768,2048]{2,1,0:T(8,128)(2,1)} %param.13) | copy-start | bytes 9437188
  33.9 6.1 %collective-permute-start.10 = (bf16[128,2176]{1,0:T(8,128)(2,1)S(1)}, bf16[128,2176]{1,0:T(8,128)(2,1)S(1)}, u32[]{:S(2)}, u32[]{:S(2)}) collective-permute-start(bf16[128,2176]{1,0:T(8,128)(2,1)S(1)} %constant_dynamic-update-slice_fusion.8), channel_id=1, source_target_pairs={{0,2},{2,0},{4,6},{6,4},{8,10},{10,8},{12,14},{14,12},{16,18},{18,... | collective-permute-start | bytes 1671176 | tf_op jit(solution)/shard_map/ppermute | solution.py:16
  34.1 5.0 %collective-permute-start.6 = (bf16[128,2048]{1,0:T(8,128)(2,1)S(1)}, bf16[128,2048]{1,0:T(8,128)(2,1)S(1)}, u32[]{:S(2)}, u32[]{:S(2)}) collective-permute-start(bf16[128,2048]{1,0:T(8,128)(2,1)S(1)} %get-tuple-element.97), channel_id=1, source_target_pairs={{0,2},{2,0},{4,6},{6,4},{8,10},{10,8},{12,14},{14,12},{16,18},{18,... | collective-permute-start | bytes 1572872 | tf_op jit(solution)/shard_map/ppermute | solution.py:16
  34.6 13.9 %collective-permute-start.12 = (bf16[32,2048]{1,0:T(8,128)(2,1)}, bf16[32,2048]{1,0:T(8,128)(2,1)}, u32[]{:S(2)}, u32[]{:S(2)}) collective-permute-start(bf16[32,2048]{1,0:T(8,128)(2,1)} %param.8), channel_id=1, source_target_pairs={{0,16},{2,18},{4,20},{6,22},{8,24},{10,26},{12,28},{14,30},{16,0},... | collective-permute-start | bytes 393224 | tf_op jit(solution)/shard_map/ppermute | solution.py:16
  38.6 9.9 %collective-permute-start.13 = (bf16[32,2048]{1,0:T(8,128)(2,1)}, bf16[32,2048]{1,0:T(8,128)(2,1)}, u32[]{:S(2)}, u32[]{:S(2)}) collective-permute-start(bf16[32,2048]{1,0:T(8,128)(2,1)} %param.8), channel_id=1, source_target_pairs={{0,24},{2,26},{4,28},{6,30},{8,16},{10,18},{12,20},{14,22},{16,8},... | collective-permute-start | bytes 393224 | tf_op jit(solution)/shard_map/ppermute | solution.py:16
  41.1 2.1 %copy-start.11 = (f32[256,768]{1,0:T(8,128)}, f32[256,768]{1,0:T(8,128)S(1)}, u32[]{:S(2)}) copy-start(f32[256,768]{1,0:T(8,128)S(1)} %fusion.20) | copy-start | bytes 2359300
  43.1 2.1 %copy-start.1 = (bf16[256,768]{1,0:T(8,128)(2,1)}, bf16[256,768]{1,0:T(8,128)(2,1)S(1)}, u32[]{:S(2)}) copy-start(bf16[256,768]{1,0:T(8,128)(2,1)S(1)} %get-tuple-element.109.refs_3_) | copy-start | bytes 1179652
  45.3 5.1 %collective-permute-start.11 = (bf16[128,2048]{1,0:T(8,128)(2,1)}, bf16[128,2048]{1,0:T(8,128)(2,1)}, u32[]{:S(2)}, u32[]{:S(2)}) collective-permute-start(bf16[128,2048]{1,0:T(8,128)(2,1)} %get-tuple-element.95), channel_id=1, source_target_pairs={{0,2},{2,0},{4,6},{6,4},{8,10},{10,8},{12,14},{14,12},{16,18},{18,... | collective-permute-start | bytes 1572872 | tf_op jit(solution)/shard_map/ppermute | solution.py:16
  45.3 17.9 %copy-start.3 = (bf16[128,2048]{1,0:T(8,128)(2,1)S(1)}, bf16[128,2048]{1,0:T(8,128)(2,1)}, u32[]{:S(2)}) copy-start(bf16[128,2048]{1,0:T(8,128)(2,1)} %add.144) | copy-start | bytes 1572868
  45.3 9.4 %collective-permute-start.9 = (bf16[64,2048]{1,0:T(8,128)(2,1)}, bf16[64,2048]{1,0:T(8,128)(2,1)S(1)}, u32[]{:S(2)}, u32[]{:S(2)}) collective-permute-start(bf16[64,2048]{1,0:T(8,128)(2,1)} %copy-done.4), channel_id=1, source_target_pairs={{0,8},{2,10},{4,12},{6,14},{8,0},{10,2},{12,4},{14,6},{16,24},{18,... | collective-permute-start | bytes 786440 | tf_op jit(solution)/shard_map/ppermute | solution.py:16
  46.4 13.4 %collective-permute-start.8 = (bf16[64,2048]{1,0:T(8,128)(2,1)S(1)}, bf16[64,2048]{1,0:T(8,128)(2,1)S(1)}, u32[]{:S(2)}, u32[]{:S(2)}) collective-permute-start(bf16[64,2048]{1,0:T(8,128)(2,1)S(1)} %slice.125), channel_id=1, source_target_pairs={{0,8},{2,10},{4,12},{6,14},{8,0},{10,2},{12,4},{14,6},{16,24},{18,... | collective-permute-start | bytes 786440 | tf_op jit(solution)/shard_map/ppermute | solution.py:16
  51.7 13.2 %copy-start.6 = (bf16[1,768,2048]{2,1,0:T(8,128)(2,1)S(1)}, bf16[1,768,2048]{2,1,0:T(8,128)(2,1)}, u32[]{:S(2)}) copy-start(bf16[1,768,2048]{2,1,0:T(8,128)(2,1)} %param.13) | copy-start | bytes 9437188
  55.7 7.5 %collective-permute-start.28 = (bf16[128,1024]{1,0:T(8,128)(2,1)S(1)}, bf16[128,1024]{1,0:T(8,128)(2,1)S(1)}, u32[]{:S(2)}, u32[]{:S(2)}) collective-permute-start(bf16[128,1024]{1,0:T(8,128)(2,1)S(1)} %constant_dynamic-slice_fusion), channel_id=1, source_target_pairs={{0,1},{1,0},{2,3},{3,2},{4,5},{5,4},{6,7},{7,6},{8,9},{9,8},{10,11... | collective-permute-start | bytes 786440 | tf_op jit(solution)/shard_map/ppermute | solution.py:16
  57.3 12.1 %collective-permute-start.16 = (bf16[64,2048]{1,0:T(8,128)(2,1)S(1)}, bf16[64,2048]{1,0:T(8,128)(2,1)S(1)}, u32[]{:S(2)}, u32[]{:S(2)}) collective-permute-start(bf16[64,2048]{1,0:T(8,128)(2,1)S(1)} %constant_dynamic-update-slice_fusion.12), channel_id=1, source_target_pairs={{0,4},{2,6},{4,0},{6,2},{8,12},{10,14},{12,8},{14,10},{16,20},{18,... | collective-permute-start | bytes 786440 | tf_op jit(solution)/shard_map/ppermute | solution.py:16
  57.6 7.2 %collective-permute-start.17 = (bf16[128,2048]{1,0:T(8,128)(2,1)S(1)}, bf16[128,2048]{1,0:T(8,128)(2,1)S(1)}, u32[]{:S(2)}, u32[]{:S(2)}) collective-permute-start(bf16[128,2048]{1,0:T(8,128)(2,1)S(1)} %constant_dynamic-update-slice_fusion.14), channel_id=1, source_target_pairs={{0,2},{2,0},{4,6},{6,4},{8,10},{10,8},{12,14},{14,12},{16,18},{18,... | collective-permute-start | bytes 1572872 | tf_op jit(solution)/shard_map/ppermute | solution.py:16
  59.8 11.6 %collective-permute-start.15 = (bf16[64,2048]{1,0:T(8,128)(2,1)S(1)}, bf16[64,2048]{1,0:T(8,128)(2,1)S(1)}, u32[]{:S(2)}, u32[]{:S(2)}) collective-permute-start(bf16[64,2048]{1,0:T(8,128)(2,1)S(1)} %slice.131), channel_id=1, source_target_pairs={{0,4},{2,6},{4,0},{6,2},{8,12},{10,14},{12,8},{14,10},{16,20},{18,... | collective-permute-start | bytes 786440 | tf_op jit(solution)/shard_map/ppermute | solution.py:16
  63.2 1.5 %collective-permute-start.29 = (bf16[128,1024]{1,0:T(8,128)(2,1)S(1)}, bf16[128,1024]{1,0:T(8,128)(2,1)S(1)}, u32[]{:S(2)}, u32[]{:S(2)}) collective-permute-start(bf16[128,1024]{1,0:T(8,128)(2,1)S(1)} %collective-permute-done.28), channel_id=1, source_target_pairs={{0,2},{2,0},{4,6},{6,4},{8,10},{10,8},{12,14},{14,12},{16,18},{18,... | collective-permute-start | bytes 786440 | tf_op jit(solution)/shard_map/ppermute | solution.py:16
  63.2 26.5 %collective-permute-start.14 = (bf16[32,2048]{1,0:T(8,128)(2,1)S(1)}, bf16[32,2048]{1,0:T(8,128)(2,1)S(1)}, u32[]{:S(2)}, u32[]{:S(2)}) collective-permute-start(bf16[32,2048]{1,0:T(8,128)(2,1)S(1)} %slice_add_fusion.3), channel_id=1, source_target_pairs={{0,4},{2,6},{4,0},{6,2},{8,12},{10,14},{12,8},{14,10},{16,20},{18,... | collective-permute-start | bytes 393224 | tf_op jit(solution)/shard_map/ppermute | solution.py:16
  64.8 1.1 %copy-start.10 = (f32[256,768]{1,0:T(8,128)S(1)}, f32[256,768]{1,0:T(8,128)}, u32[]{:S(2)}) copy-start(f32[256,768]{1,0:T(8,128)} %copy-done.9) | copy-start | bytes 2359300
  65.9 1.9 %copy-start.8 = (bf16[1,2048,768]{2,1,0:T(8,128)(2,1)S(1)}, bf16[1,2048,768]{2,1,0:T(8,128)(2,1)}, u32[]{:S(2)}) copy-start(bf16[1,2048,768]{2,1,0:T(8,128)(2,1)} %param.11) | copy-start | bytes 9437188
  65.9 2.1 %copy-start.13 = (f32[256,768]{1,0:T(8,128)S(1)}, f32[256,768]{1,0:T(8,128)}, u32[]{:S(2)}) copy-start(f32[256,768]{1,0:T(8,128)} %get-tuple-element.108) | copy-start | bytes 2359300
  69.4 2.1 %collective-permute-start.20 = (bf16[128,2048]{1,0:T(8,128)(2,1)S(1)}, bf16[128,2048]{1,0:T(8,128)(2,1)S(1)}, u32[]{:S(2)}, u32[]{:S(2)}) collective-permute-start(bf16[128,2048]{1,0:T(8,128)(2,1)S(1)} %get-tuple-element.93), channel_id=1, source_target_pairs={{0,2},{2,0},{4,6},{6,4},{8,10},{10,8},{12,14},{14,12},{16,18},{18,... | collective-permute-start | bytes 1572872 | tf_op jit(solution)/shard_map/ppermute | solution.py:16
  69.6 2.5 %collective-permute-start.22 = (bf16[128,2048]{1,0:T(8,128)(2,1)S(1)}, bf16[128,2048]{1,0:T(8,128)(2,1)S(1)}, u32[]{:S(2)}, u32[]{:S(2)}) collective-permute-start(bf16[128,2048]{1,0:T(8,128)(2,1)S(1)} %constant_dynamic-update-slice_fusion.18), channel_id=1, source_target_pairs={{0,2},{2,0},{4,6},{6,4},{8,10},{10,8},{12,14},{14,12},{16,18},{18,... | collective-permute-start | bytes 1572872 | tf_op jit(solution)/shard_map/ppermute | solution.py:16
  72.2 1.3 %copy-start.12 = (f32[256,768]{1,0:T(8,128)S(1)}, f32[256,768]{1,0:T(8,128)}, u32[]{:S(2)}) copy-start(f32[256,768]{1,0:T(8,128)} %copy-done.11) | copy-start | bytes 2359300
  73.5 2.2 %copy-start.14 = (f32[256,768]{1,0:T(8,128)S(1)}, f32[256,768]{1,0:T(8,128)}, u32[]{:S(2)}) copy-start(f32[256,768]{1,0:T(8,128)} %get-tuple-element.110) | copy-start | bytes 2359300
  74.6 10.0 %collective-permute-start.21 = (bf16[64,2048]{1,0:T(8,128)(2,1)S(1)}, bf16[64,2048]{1,0:T(8,128)(2,1)S(1)}, u32[]{:S(2)}, u32[]{:S(2)}) collective-permute-start(bf16[64,2048]{1,0:T(8,128)(2,1)S(1)} %slice.137), channel_id=1, source_target_pairs={{0,8},{2,10},{4,12},{6,14},{8,0},{10,2},{12,4},{14,6},{16,24},{18,... | collective-permute-start | bytes 786440 | tf_op jit(solution)/shard_map/ppermute | solution.py:16
  76.9 12.8 %copy-start.2 = (bf16[256,768]{1,0:T(8,128)(2,1)S(1)}, bf16[256,768]{1,0:T(8,128)(2,1)}, u32[]{:S(2)}) copy-start(bf16[256,768]{1,0:T(8,128)(2,1)} %copy-done.1) | copy-start | bytes 1179652
  77.0 10.5 %collective-permute-start.24 = (bf16[128,2048]{1,0:T(8,128)(2,1)S(1)}, bf16[128,2048]{1,0:T(8,128)(2,1)S(1)}, u32[]{:S(2)}, u32[]{:S(2)}) collective-permute-start(bf16[128,2048]{1,0:T(8,128)(2,1)S(1)} %get-tuple-element.91), channel_id=1, source_target_pairs={{0,2},{2,0},{4,6},{6,4},{8,10},{10,8},{12,14},{14,12},{16,18},{18,... | collective-permute-start | bytes 1572872 | tf_op jit(solution)/shard_map/ppermute | solution.py:16
  77.1 12.7 %collective-permute-start.31 = (bf16[128,1024]{1,0:T(8,128)(2,1)S(1)}, bf16[128,1024]{1,0:T(8,128)(2,1)S(1)}, u32[]{:S(2)}, u32[]{:S(2)}) collective-permute-start(bf16[128,1024]{1,0:T(8,128)(2,1)S(1)} %constant_dynamic-slice_fusion.1), channel_id=1, source_target_pairs={{0,1},{1,0},{2,3},{3,2},{4,5},{5,4},{6,7},{7,6},{8,9},{9,8},{10,11... | collective-permute-start | bytes 786440 | tf_op jit(solution)/shard_map/ppermute | solution.py:16
  78.7 12.9 %collective-permute-start.18 = (bf16[32,2048]{1,0:T(8,128)(2,1)S(1)}, bf16[32,2048]{1,0:T(8,128)(2,1)S(1)}, u32[]{:S(2)}, u32[]{:S(2)}) collective-permute-start(bf16[32,2048]{1,0:T(8,128)(2,1)S(1)} %get-tuple-element.101), channel_id=1, source_target_pairs={{0,16},{2,18},{4,20},{6,22},{8,24},{10,26},{12,28},{14,30},{16,0},... | collective-permute-start | bytes 393224 | tf_op jit(solution)/shard_map/ppermute | solution.py:16
  84.6 7.0 %collective-permute-start.19 = (bf16[32,2048]{1,0:T(8,128)(2,1)S(1)}, bf16[32,2048]{1,0:T(8,128)(2,1)S(1)}, u32[]{:S(2)}, u32[]{:S(2)}) collective-permute-start(bf16[32,2048]{1,0:T(8,128)(2,1)S(1)} %get-tuple-element.102), channel_id=1, source_target_pairs={{0,24},{2,26},{4,28},{6,30},{8,16},{10,18},{12,20},{14,22},{16,8},... | collective-permute-start | bytes 393224 | tf_op jit(solution)/shard_map/ppermute | solution.py:16
  87.5 14.4 %collective-permute-start.30 = (bf16[256,768]{1,0:T(8,128)(2,1)S(1)}, bf16[256,768]{1,0:T(8,128)(2,1)S(1)}, u32[]{:S(2)}, u32[]{:S(2)}) collective-permute-start(bf16[256,768]{1,0:T(8,128)(2,1)S(1)} %get-tuple-element.107.refs_1_), channel_id=1, source_target_pairs={{0,1},{1,0},{2,3},{3,2},{4,5},{5,4},{6,7},{7,6},{8,9},{9,8},{10,11... | collective-permute-start | bytes 1179656 | tf_op jit(solution)/shard_map/ppermute | solution.py:16
  89.7 16.6 %collective-permute-start.33 = (bf16[256,768]{1,0:T(8,128)(2,1)S(1)}, bf16[256,768]{1,0:T(8,128)(2,1)S(1)}, u32[]{:S(2)}, u32[]{:S(2)}) collective-permute-start(bf16[256,768]{1,0:T(8,128)(2,1)S(1)} %copy-done.2), channel_id=1, source_target_pairs={{0,1},{1,0},{2,3},{3,2},{4,5},{5,4},{6,7},{7,6},{8,9},{9,8},{10,11... | collective-permute-start | bytes 1179656 | tf_op jit(solution)/shard_map/ppermute | solution.py:16
  89.8 2.5 %collective-permute-start.32 = (bf16[128,1024]{1,0:T(8,128)(2,1)S(1)}, bf16[128,1024]{1,0:T(8,128)(2,1)S(1)}, u32[]{:S(2)}, u32[]{:S(2)}) collective-permute-start(bf16[128,1024]{1,0:T(8,128)(2,1)S(1)} %collective-permute-done.31), channel_id=1, source_target_pairs={{0,2},{2,0},{4,6},{6,4},{8,10},{10,8},{12,14},{14,12},{16,18},{18,... | collective-permute-start | bytes 786440 | tf_op jit(solution)/shard_map/ppermute | solution.py:16
  91.6 8.4 %collective-permute-start.25 = (bf16[64,2048]{1,0:T(8,128)(2,1)S(1)}, bf16[64,2048]{1,0:T(8,128)(2,1)S(1)}, u32[]{:S(2)}, u32[]{:S(2)}) collective-permute-start(bf16[64,2048]{1,0:T(8,128)(2,1)S(1)} %slice.141), channel_id=1, source_target_pairs={{0,4},{2,6},{4,0},{6,2},{8,12},{10,14},{12,8},{14,10},{16,20},{18,... | collective-permute-start | bytes 786440 | tf_op jit(solution)/shard_map/ppermute | solution.py:16
  92.4 18.0 %collective-permute-start.23 = (bf16[32,2048]{1,0:T(8,128)(2,1)S(1)}, bf16[32,2048]{1,0:T(8,128)(2,1)S(1)}, u32[]{:S(2)}, u32[]{:S(2)}) collective-permute-start(bf16[32,2048]{1,0:T(8,128)(2,1)S(1)} %slice_add_fusion.2), channel_id=1, source_target_pairs={{0,4},{2,6},{4,0},{6,2},{8,12},{10,14},{12,8},{14,10},{16,20},{18,... | collective-permute-start | bytes 393224 | tf_op jit(solution)/shard_map/ppermute | solution.py:16
  100.0 10.4 %collective-permute-start.26 = (bf16[32,2048]{1,0:T(8,128)(2,1)S(1)}, bf16[32,2048]{1,0:T(8,128)(2,1)S(1)}, u32[]{:S(2)}, u32[]{:S(2)}) collective-permute-start(bf16[32,2048]{1,0:T(8,128)(2,1)S(1)} %get-tuple-element.99), channel_id=1, source_target_pairs={{0,16},{2,18},{4,20},{6,22},{8,24},{10,26},{12,28},{14,30},{16,0},... | collective-permute-start | bytes 393224 | tf_op jit(solution)/shard_map/ppermute | solution.py:16
  100.1 10.3 %collective-permute-start.27 = (bf16[32,2048]{1,0:T(8,128)(2,1)S(1)}, bf16[32,2048]{1,0:T(8,128)(2,1)S(1)}, u32[]{:S(2)}, u32[]{:S(2)}) collective-permute-start(bf16[32,2048]{1,0:T(8,128)(2,1)S(1)} %get-tuple-element.100), channel_id=1, source_target_pairs={{0,24},{2,26},{4,28},{6,30},{8,16},{10,18},{12,20},{14,22},{16,8},... | collective-permute-start | bytes 393224 | tf_op jit(solution)/shard_map/ppermute | solution.py:16
  (1 other events, 1.1 us)

commit v3 on v1

v3 whole, which is shorter than its diff:
```python
import functools

import jax
import jax.numpy as jnp
from jax import lax
from jax.experimental import pallas as pl
from jax.experimental.pallas import tpu as pltpu
from jax.sharding import PartitionSpec as P

TILE = 256
OUT_TILE = 512
SHARE_TILE = 256
LANES = 128
LIMIT = 12 * 1024 * 1024
BF16 = jnp.bfloat16
F32 = jnp.float32


def swap(value, axis, distance):
    size = lax.axis_size(axis)
    return lax.ppermute(value, axis, [(i, i ^ distance) for i in range(size)])


def after(value, *earlier):
    return lax.optimization_barrier((value,) + earlier)[0]


def after_all(values, *earlier):
    return lax.optimization_barrier(tuple(values) + earlier)[: len(values)]


def dot(left, right, contract):
    return lax.dot_general(left, right, (contract, ((), ())), preferred_element_type=F32)


class Order:
    def __init__(self, first):
        self.last = first

    def __call__(self, function, *operands):
        operands = lax.optimization_barrier((*operands, self.last))[:-1]
        result = function(*operands)
        self.last = result[0] if isinstance(result, (tuple, list)) else result
        return result


def gate_lanes(routes, gate_codes, n_expert):
    experts = jnp.arange(n_expert, dtype=jnp.int32)
    chosen = routes[:, :, None] == experts[None, None, :]
    codes = jnp.sum(jnp.where(chosen, gate_codes[:, :, None], 0), axis=1)
    total = jnp.sum(gate_codes, axis=1, keepdims=True)
    digits = jnp.concatenate([codes >> 6, codes & 63, total >> 8, total & 255], axis=1)
    return jnp.pad(digits, ((0, 0), (0, LANES - digits.shape[1]))).astype(BF16)


def block_kernel(first_ref, own_ref, got_ref, lanes_ref, out_ref):
    rows, width = own_ref.shape

    def fill(own, got):
        out_ref[own, :width] = own_ref[...]
        out_ref[got, :width] = got_ref[...]
        out_ref[own, width:] = lanes_ref[...]
        out_ref[got, width:] = jnp.zeros(lanes_ref.shape, BF16)

    choose(first_ref[0], fill, slice(0, rows), slice(rows, 2 * rows))


def make_block(first, own, got, lanes):
    rows, width = own.shape
    vmem = pl.BlockSpec(memory_space=pltpu.VMEM)
    return pl.pallas_call(
        block_kernel,
        out_shape=jax.ShapeDtypeStruct((2 * rows, width + LANES), BF16),
        in_specs=[pl.BlockSpec(memory_space=pltpu.SMEM)] + [vmem] * 3,
        out_specs=vmem,
        compiler_params=pltpu.CompilerParams(vmem_limit_bytes=4 * 1024 * 1024),
        cost_estimate=pl.CostEstimate(flops=10**6, bytes_accessed=10**6, transcendentals=0),
    )(first, own, got, lanes)


def choose(flag, function, here, there):
    pl.when(flag == 1)(lambda: function(here, there))
    pl.when(flag == 0)(lambda: function(there, here))


class Stream:
    def __init__(self, pairs, sems, ahead):
        self.copies = [pltpu.make_async_copy(source, target, sems.at[i]) for i, (source, target) in enumerate(pairs)]
        self.started = self.waited = 0
        self.ahead = ahead
        self.fill()

    def fill(self):
        while self.started < min(len(self.copies), self.waited + self.ahead):
            self.copies[self.started].start()
            self.started += 1

    def wait(self, count):
        for _ in range(count):
            self.copies[self.waited].wait()
            self.waited += 1
        self.fill()


def piece_kernel(n_expert, n_edata, count, first_ref, expert_ref, place_ref, *refs):
    mine, theirs, (gate_hbm, up_hbm, down_hbm) = refs[:count], refs[count : 2 * count], refs[2 * count : 2 * count + 3]
    kept_ref, sent_ref, scaled_ref, share_ref = refs[2 * count + 3 : -12]
    rows_ref, grads_ref, lanes_ref, hidden_ref, act_ref, slope_ref, grad_gate_ref, grad_up_ref, gate_ref, up_ref, down_ref, sems = refs[-12:]
    width, units = gate_ref.shape
    pairs = []
    for at in range(0, units, TILE):
        columns = pl.ds(at, TILE)
        pairs.append((gate_hbm.at[0, :, columns], gate_ref.at[:, columns]))
        pairs.append((up_hbm.at[0, :, columns], up_ref.at[:, columns]))
    pairs += [(down_hbm.at[0, :, pl.ds(at, OUT_TILE)], down_ref.at[:, pl.ds(at, OUT_TILE)]) for at in range(0, width, OUT_TILE)]
    stream = Stream(pairs, sems, 4)

    def unpack(tokens, grads):
        at = 0
        for token, grad in zip(tokens, grads):
            block = slice(at, at + token.shape[0])
            rows_ref[block, :] = token[:, :width]
            grads_ref[block, :] = grad[:, :width]
            lanes_ref[block, :] = token[:, width:].astype(F32) + grad[:, width:].astype(F32)
            at += token.shape[0]

    choose(first_ref[0], unpack, mine, theirs)
    values = lanes_ref[...]
    lane = lax.broadcasted_iota(jnp.int32, values.shape, 1)
    expert = expert_ref[0]
    weight = jnp.where(lane == expert, 64.0, 0.0) + jnp.where(lane == expert + n_expert, 1.0, 0.0)
    whole = jnp.where(lane == 2 * n_expert, 256.0, 0.0) + jnp.where(lane == 2 * n_expert + 1, 1.0, 0.0)
    gate = jnp.sum(values * weight, axis=1, keepdims=True) / jnp.sum(values * whole, axis=1, keepdims=True)
    share = width // n_edata
    share_ref[...] = grads_ref[:, pl.ds(pl.multiple_of(place_ref[0] * share, LANES), share)]

    for at in range(0, units, TILE):
        columns = slice(at, at + TILE)
        stream.wait(2)
        gate_pre = dot(rows_ref[...], gate_ref[:, columns], ((1,), (0,)))
        up_pre = dot(rows_ref[...], up_ref[:, columns], ((1,), (0,)))
        sig_gate = jax.nn.sigmoid(gate_pre)
        act_gate = gate_pre * sig_gate
        hidden = (act_gate * up_pre).astype(BF16)
        hidden_ref[:, columns] = hidden
        scaled_ref[:, columns] = (hidden.astype(F32) * gate).astype(BF16)
        act_ref[:, columns] = act_gate * gate
        slope_ref[:, columns] = up_pre * sig_gate * (1.0 + gate_pre * (1.0 - sig_gate)) * gate
    for at in range(0, width, OUT_TILE):
        columns = slice(at, at + OUT_TILE)
        stream.wait(1)
        rows_ref[:, columns] = (dot(hidden_ref[...], down_ref[:, columns], ((1,), (0,))) * gate).astype(BF16)
    for at in range(0, units, TILE):
        columns = slice(at, at + TILE)
        grad_hidden = dot(grads_ref[...], down_ref[columns, :], ((1,), (1,)))
        grad_gate_ref[:, columns] = (grad_hidden * slope_ref[:, columns]).astype(BF16)
        grad_up_ref[:, columns] = (grad_hidden * act_ref[:, columns]).astype(BF16)
    for at in range(0, width, OUT_TILE):
        columns = slice(at, at + OUT_TILE)
        grad = dot(grad_gate_ref[...], gate_ref[columns, :], ((1,), (1,)))
        grad = grad + dot(grad_up_ref[...], up_ref[columns, :], ((1,), (1,)))
        grads_ref[:, columns] = grad.astype(BF16)

    def give(own, other):
        own[...] = rows_ref[...]
        other[...] = grads_ref[...]

    choose(first_ref[0], give, kept_ref, sent_ref)


def piece(n_expert, n_edata, first, expert, place, mats, mine, theirs):
    width, units = mats[0].shape[1:]
    rows = sum(part.shape[0] for part in mine)
    vmem, smem, hbm = (pl.BlockSpec(memory_space=space) for space in (pltpu.VMEM, pltpu.SMEM, pltpu.HBM))
    outs = [(rows, width)] * 2 + [(rows, units), (rows, width // n_edata)]
    scratch = [((rows, width), BF16)] * 2 + [((rows, LANES), F32), ((rows, units), BF16)] + [((rows, units), F32)] * 2
    scratch += [((rows, units), BF16)] * 2 + [((width, units), BF16)] * 2 + [((units, width), BF16)]
    return pl.pallas_call(
        functools.partial(piece_kernel, n_expert, n_edata, len(mine)),
        out_shape=[jax.ShapeDtypeStruct(shape, BF16) for shape in outs],
        in_specs=[smem] * 3 + [vmem] * (2 * len(mine)) + [hbm] * 3,
        out_specs=[vmem] * len(outs),
        scratch_shapes=[pltpu.VMEM(*shape) for shape in scratch] + [pltpu.SemaphoreType.DMA((2 * units // TILE + width // OUT_TILE,))],
        compiler_params=pltpu.CompilerParams(vmem_limit_bytes=rows * 88 * 1024),
        cost_estimate=pl.CostEstimate(flops=10**6, bytes_accessed=10**5, transcendentals=0),
    )(first, expert, place, *mine, *theirs, *[pltpu.with_memory_space_constraint(mat, pltpu.HBM) for mat in mats])


def cut_kernel(n_edata, first_ref, place_ref, *refs):
    out_refs = refs[-(n_edata - 1) :]
    blocks = refs[: -(n_edata - 1)]
    share = out_refs[0].shape[1]

    def cut(blocks, _):
        for step, out_ref in enumerate(out_refs, 1):
            columns, at = pl.ds(pl.multiple_of((place_ref[0] ^ step) * share, LANES), share), 0
            for block in blocks:
                out_ref[at : at + block.shape[0], :] = block[:, columns]
                at += block.shape[0]

    choose(first_ref[0], cut, blocks[: len(blocks) // 2], blocks[len(blocks) // 2 :])


def cut_shares(n_edata, first, place, here, there):
    rows, width = sum(part.shape[0] for part in here), here[0].shape[1] - LANES
    vmem, smem = (pl.BlockSpec(memory_space=space) for space in (pltpu.VMEM, pltpu.SMEM))
    return pl.pallas_call(
        functools.partial(cut_kernel, n_edata),
        out_shape=[jax.ShapeDtypeStruct((rows, width // n_edata), BF16)] * (n_edata - 1),
        in_specs=[smem] * 2 + [vmem] * (len(here) + len(there)),
        out_specs=[vmem] * (n_edata - 1),
        compiler_params=pltpu.CompilerParams(vmem_limit_bytes=LIMIT),
        cost_estimate=pl.CostEstimate(flops=10**6, bytes_accessed=10**5, transcendentals=0),
    )(first, place, *here, *there)


def total_of(*parts):
    return sum(part.astype(F32) for part in parts)


def share_kernel(counts, continued, *refs):
    out_ref, at, total = refs[-1], 0, None
    columns = pl.ds(pl.multiple_of(pl.program_id(0) * SHARE_TILE, SHARE_TILE), SHARE_TILE)
    for count in counts:
        grads = jnp.concatenate([ref[:, columns] for ref in refs[at : at + count]], axis=0)
        term = dot(grads, refs[at + count][...], ((0,), (0,)))
        total = term if total is None else total + term
        at += count + 1
    if continued:
        out_ref[...] = (total + refs[at][...])[:, None, :]
    else:
        out_ref[...] = total


def weight_share(groups, begun):
    operands = [array for grads, hidden in groups for array in (*grads, hidden)]
    share, units = groups[0][0][0].shape[1], groups[0][1].shape[1]
    specs = [pl.BlockSpec(memory_space=pltpu.VMEM)] * len(operands)
    plain = pl.BlockSpec((SHARE_TILE, units), lambda i: (i, 0))
    continued = begun is not None
    return pl.pallas_call(
        functools.partial(share_kernel, [len(grads) for grads, _ in groups], continued),
        out_shape=jax.ShapeDtypeStruct((share, 1, units) if continued else (share, units), F32),
        grid=(share // SHARE_TILE,),
        in_specs=specs + [plain] * continued,
        out_specs=pl.BlockSpec((SHARE_TILE, 1, units), lambda i: (i, 0, 0)) if continued else plain,
        compiler_params=pltpu.CompilerParams(vmem_limit_bytes=LIMIT),
        cost_estimate=pl.CostEstimate(flops=10**6, bytes_accessed=10**5, transcendentals=0),
    )(*operands, *([begun] if continued else []))


def shards(tokens, out_grad, routes, gate_codes, w_gate, w_up, w_down):
    rows, width = tokens.shape
    n_expert = lax.axis_size("expert")
    n_edata = lax.axis_size("edata")
    expert = lax.axis_index("expert").astype(jnp.int32)
    place = lax.axis_index("edata").astype(jnp.int32)
    first = expert % 2 == 0
    pick = lambda here, there: jnp.where(first, here, there)
    flags = [value.astype(jnp.int32).reshape(1) for value in (first, expert, place)]
    firsts = list(range(8, n_expert, 8))
    n_first = len(firsts)
    core = lambda part: swap(part, "expert", 1)
    across = lambda part: swap(part, "expert", 2)

    own, sent = pick(tokens, out_grad), pick(out_grad, tokens)
    got = core(sent)
    order = Order(got)
    lanes = gate_lanes(routes, gate_codes, n_expert)
    block = order(make_block, flags[0], own, got, lanes)
    beside = across(block)
    straight_1 = [swap(block, "expert", step) for step in firsts]
    near_own = swap(block, "expert", 4)
    near_beside = swap(after(beside, *straight_1), "expert", 4)
    across_1 = [across(part) for part in straight_1]
    straight_2 = [swap(part, "expert", 4) for part in straight_1]
    near_own = after(near_own, *straight_1)
    straight_2 = after_all(straight_2, near_own)
    near_beside = after(near_beside, *straight_2)
    across_2 = [across(part) for part in straight_2]
    across_1 = after_all(across_1, *straight_2)
    across_2 = after_all(across_2, near_beside)
    pieces_1 = [block, beside, *straight_1, *across_1]
    pieces_2 = [near_own, near_beside, *straight_2, *across_2]
    got_2 = [core(part) for part in pieces_2]
    got_1 = list(after_all([core(part) for part in pieces_1], *got_2))
    run = lambda *parts: piece(n_expert, n_edata, *flags, (w_gate, w_up, w_down), parts[: len(parts) // 2], parts[len(parts) // 2 :])
    size = 2 * rows
    cuts = lambda total, count: [total[i * size : (i + 1) * size] for i in range(count)]
    add = lambda *a: tuple(a[i] + a[len(a) // 2 + i] for i in range(len(a) // 2))

    cuts_out = order(lambda *a: cut_shares(n_edata, flags[0], flags[2], a[: len(pieces_1)], a[len(pieces_1) :]), *got_1, *pieces_2)
    mine = [swap(part, "edata", step) for step, part in enumerate(cuts_out, 1)]
    kept_1, sent_1, scaled_1, share_1 = order(run, *pieces_1, *got_1)
    scaled_other_1 = [swap(scaled_1, "edata", step) for step in range(1, n_edata)]
    parts_1 = order(lambda kept, got: cuts(kept + got, 2 + 2 * n_first), kept_1, core(sent_1))
    crossed_1 = [across(part) for part in parts_1[2 + n_first :]]
    kept_2, sent_2, scaled_2, share_2 = order(run, *pieces_2, *got_2)
    scaled_other_2 = [swap(scaled_2, "edata", step) for step in range(1, n_edata)]
    mine = after_all(mine, kept_2)
    ready_1 = order(add, *after_all(parts_1[2 : 2 + n_first], *mine), *crossed_1)
    back_1 = [swap(part, "expert", step) for part, step in zip(ready_1, firsts)]
    sent_2 = core(after(sent_2, *ready_1))
    near_2, *parts_2 = order(lambda kept, got: ((kept + got)[: 2 * size], *cuts((kept + got)[2 * size :], 2 * n_first)), kept_2, sent_2)
    crossed_2 = [across(part) for part in parts_2[n_first:]]
    back_near = swap(near_2, "expert", 4)
    theirs = [core(after(part, near_2)) for part in mine]
    own_share = order(lambda *a: weight_share([([a[0]], a[1]), ([a[2]], a[3])], None), share_1, scaled_1, share_2, scaled_2)
    ready_2 = order(add, *after_all(parts_2[:n_first], *after_all(scaled_other_1, own_share), *theirs), *crossed_2)
    back_2 = [swap(part, "expert", step + 4) for part, step in zip(ready_2, firsts)]
    ready = order(lambda part, got: part + got[size:], parts_1[1], after(back_near, *back_1))
    back_pair = across(ready)
    others = []
    for step in range(1, n_edata):
        here, there = mine[step - 1], theirs[step - 1]
        others += [([pick(here, there)], scaled_other_1[step - 1]), ([pick(there, here)], after(scaled_other_2[step - 1], ready))]
    grad_down = weight_share(others, own_share)
    order.last = grad_down
    total = order(lambda own, near, *parts: total_of(own, near[:size], *parts), parts_1[0], back_near, *back_1, *back_2)
    total = order(lambda total, pair: (total + pair.astype(F32)).astype(BF16), total, back_pair)
    kept, sent = pick(total[:rows], total[rows:]), pick(total[rows:], total[:rows])
    got = core(sent)
    return pick(kept, got), pick(got, kept), grad_down


def solution(mesh):
    by_token = P(("expert", "edata"), None)
    by_expert = P("expert", None, None)
    return jax.shard_map(
        shards,
        mesh=mesh,
        in_specs=(by_token,) * 4 + (by_expert,) * 3,
        out_specs=(by_token, by_token, P("edata", "expert", None)),
        check_vma=False,
    )
```

time: 127 us -> 101 us (0.80)
  Pallas kernels: 0 us -> 24.2 us
  matrix products: 14.2 us -> 0 us
  waiting for transfers between devices: 53.1 us -> 39.3 us
  local copies, waits for them, and re-layouts: 12.8 us -> 0.45 us
  other arithmetic: 10.6 us -> 4.52 us
  starting transfers between devices: 35.3 us -> 31.3 us
    pallas_call x0 -> x6, Pallas kernels: none -> 24.2 us  [the longest x2 19.2 us: piece(): pl.pallas_call(functools.partial(piece_kernel, n_expert, n_edata, len(min...]
    dot_general x8 -> x0, matrix products: 14.2 us -> none  [dot(): lax.dot_general(left, right, (contract, ((), ())), preferred_element_type...]
    ppermute x29, waiting for transfers between devices: 53.1 us -> 39.3 us  [swap(): return lax.ppermute(value, axis, [(i, i ^ distance) for i in range(size)])]
    unnamed x38 -> x0, local copies, waits for them, and re-layouts: 12.4 us -> none
    concatenate x10 -> x1, other arithmetic: 6.54 us -> 0.08 us  [gate_lanes(): jnp.concatenate([codes >> 6, codes & 63, total >> 8, total & 255], axis=1)]
    ppermute x29, starting transfers between devices: 35.3 us -> 31.3 us  [swap(): return lax.ppermute(value, axis, [(i, i ^ distance) for i in range(size)])]
    select_n x0 -> x4, other arithmetic: none -> 1.8 us  [shards(): pick = lambda here, there: jnp.where(first, here, there)]
    convert_element_type x2 -> x1, other arithmetic: 1.48 us -> 0.06 us  [shards(): (total + pair.astype(F32)).astype(BF16)]
  transfers between devices with their start and end apart: 29 -> 29, of which waited for: 10 -> 12; matrix products, arithmetic and copies ran while one was open for 28% -> 3% of each run, Pallas kernels for 0% -> 15%
where the time goes in v3:
time: 101 us
  waiting for transfers between devices  39.3 us (39%)
  starting transfers between devices  31.3 us (31%)
  Pallas kernels  24.2 us (24%)
  other arithmetic  4.52 us (4%)
    ppermute x29, waiting for transfers between devices, swap(): return lax.ppermute(value, axis, [(i, i ^ distance) for i in range(size)])  39.3 us
    ppermute x29, starting transfers between devices, swap(): return lax.ppermute(value, axis, [(i, i ^ distance) for i in range(size)])  31.3 us
    pallas_call x2, Pallas kernels, piece(): pl.pallas_call(functools.partial(piece_kernel, n_expert, n_edata, len(min...  19.2 us
    pallas_call x2, Pallas kernels, weight_share(): pl.pallas_call(functools.partial(share_kernel, [len(grads) for grads, _ i...  4.94 us
  transfers between devices with their start and end apart: 29, of which 12 were waited for; matrix products, arithmetic and copies ran while one was open for 3% of the time, Pallas kernels for 15%

profile of v3, /device:TPU:0, one launch (start us, length us, event | category | flops | bytes accessed | tf_op | source)
XLA Modules:
  0.0 100.6 jit_solution(7034050312857192788)
XLA Ops:
  0.6 1.0 broadcast_select_fusion.6
  1.6 0.5 collective-permute-start
  2.2 0.7 reduce_sum.19
  2.9 0.7 select_reduce_fusion
  3.7 0.1 copy.22
  3.8 0.1 copy.23
  3.9 0.1 fusion.6.lanes_ref
  4.0 3.7 %collective-permute-start.2 = (bf16[64,2176]{1,0:T(8,128)(2,1)S(1)}, bf16[64,2176]{1,0:T(8,128)(2,1)S(1)}, u32[]{:S(2)}, u32[]{:S(2)}) collective-permute-start(bf16[64,2176]{1,0:T(8,128)(2,1)S(1)} %shard_map.94.refs_0_), channel_id=1, source_target_pairs={{0,16},{2,18},{4,20},{6,22},{8,24},{10,26},{12,28},{14,30},{16,0},... | collective-permute-start | bytes 835592 | tf_op jit(solution)/shard_map/ppermute | solution.py:21
  7.7 1.6 %collective-permute-start.5 = (bf16[64,2176]{1,0:T(8,128)(2,1)S(1)}, bf16[64,2176]{1,0:T(8,128)(2,1)S(1)}, u32[]{:S(2)}, u32[]{:S(2)}) collective-permute-start(bf16[64,2176]{1,0:T(8,128)(2,1)S(1)} %shard_map.94.refs_0_), channel_id=1, source_target_pairs={{0,8},{2,10},{4,12},{6,14},{8,0},{10,2},{12,4},{14,6},{16,24},{18,... | collective-permute-start | bytes 835592 | tf_op jit(solution)/shard_map/ppermute | solution.py:21
  9.3 1.5 %collective-permute-start.1 = (bf16[64,2176]{1,0:T(8,128)(2,1)S(1)}, bf16[64,2176]{1,0:T(8,128)(2,1)S(1)}, u32[]{:S(2)}, u32[]{:S(2)}) collective-permute-start(bf16[64,2176]{1,0:T(8,128)(2,1)S(1)} %shard_map.94.refs_0_), channel_id=1, source_target_pairs={{0,4},{2,6},{4,0},{6,2},{8,12},{10,14},{12,8},{14,10},{16,20},{18,... | collective-permute-start | bytes 835592 | tf_op jit(solution)/shard_map/ppermute | solution.py:21
  10.8 10.3 %collective-permute-done.2.refs_2_ = bf16[64,2176]{1,0:T(8,128)(2,1)S(1)} collective-permute-done((bf16[64,2176]{1,0:T(8,128)(2,1)S(1)}, bf16[64,2176]{1,0:T(8,128)(2,1)S(1)}, u32[]{:S(2)}, u32[]{:S(2)}) %collective-permute-start.2) | collective-permute-done | bytes 278560 | tf_op jit(solution)/shard_map/ppermute | solution.py:21
  21.1 0.6 collective-permute-start.4
  21.7 1.5 %collective-permute-start.3 = (bf16[64,2176]{1,0:T(8,128)(2,1)S(1)}, bf16[64,2176]{1,0:T(8,128)(2,1)}, u32[]{:S(2)}, u32[]{:S(2)}) collective-permute-start(bf16[64,2176]{1,0:T(8,128)(2,1)S(1)} %collective-permute-done.2.refs_2_), channel_id=1, source_target_pairs={{0,4},{2,6},{4,0},{6,2},{8,12},{10,14},{12,8},{14,10},{16,20},{18,... | collective-permute-start | bytes 835592 | tf_op jit(solution)/shard_map/ppermute | solution.py:21
  23.2 1.4 %collective-permute-start.11 = (bf16[64,2176]{1,0:T(8,128)(2,1)S(1)}, bf16[64,2176]{1,0:T(8,128)(2,1)S(1)}, u32[]{:S(2)}, u32[]{:S(2)}) collective-permute-start(bf16[64,2176]{1,0:T(8,128)(2,1)S(1)} %collective-permute-done.1.refs_1_), channel_id=1, source_target_pairs={{0,8},{2,10},{4,12},{6,14},{8,0},{10,2},{12,4},{14,6},{16,24},{18,... | collective-permute-start | bytes 835592 | tf_op jit(solution)/shard_map/ppermute | solution.py:21
  24.7 5.9 %collective-permute-done.4.refs_6_.refs_2_ = bf16[64,2176]{1,0:T(8,128)(2,1)S(1)} collective-permute-done((bf16[64,2176]{1,0:T(8,128)(2,1)S(1)}, bf16[64,2176]{1,0:T(8,128)(2,1)S(1)}, u32[]{:S(2)}, u32[]{:S(2)}) %collective-permute-start.4) | collective-permute-done | bytes 278560 | tf_op jit(solution)/shard_map/ppermute | solution.py:21
  30.6 1.6 %collective-permute-start.14 = (bf16[64,2176]{1,0:T(8,128)(2,1)S(1)}, bf16[64,2176]{1,0:T(8,128)(2,1)S(1)}, u32[]{:S(2)}, u32[]{:S(2)}) collective-permute-start(bf16[64,2176]{1,0:T(8,128)(2,1)S(1)} %collective-permute-done.4.refs_6_.refs_2_), channel_id=1, source_target_pairs={{0,4},{2,6},{4,0},{6,2},{8,12},{10,14},{12,8},{14,10},{16,20},{18,... | collective-permute-start | bytes 835592 | tf_op jit(solution)/shard_map/ppermute | solution.py:21
  32.2 0.5 collective-permute-start.10
  32.7 2.7 %collective-permute-done.11.refs_5_.refs_1_ = bf16[64,2176]{1,0:T(8,128)(2,1)S(1)} collective-permute-done((bf16[64,2176]{1,0:T(8,128)(2,1)S(1)}, bf16[64,2176]{1,0:T(8,128)(2,1)S(1)}, u32[]{:S(2)}, u32[]{:S(2)}) %collective-permute-start.11) | collective-permute-done | bytes 278560 | tf_op jit(solution)/shard_map/ppermute | solution.py:21
  35.5 1.7 %collective-permute-done.14.refs_7_.refs_3_ = bf16[64,2176]{1,0:T(8,128)(2,1)S(1)} collective-permute-done((bf16[64,2176]{1,0:T(8,128)(2,1)S(1)}, bf16[64,2176]{1,0:T(8,128)(2,1)S(1)}, u32[]{:S(2)}, u32[]{:S(2)}) %collective-permute-start.14) | collective-permute-done | bytes 278560 | tf_op jit(solution)/shard_map/ppermute | solution.py:21
  37.2 0.5 collective-permute-start.12
  37.8 0.4 collective-permute-start.15
  38.2 0.7 collective-permute-done.13.refs_6_
  38.9 1.3 %collective-permute-done.9.refs_3_.refs_7_ = bf16[64,2176]{1,0:T(8,128)(2,1)S(1)} collective-permute-done((bf16[64,2176]{1,0:T(8,128)(2,1)}, bf16[64,2176]{1,0:T(8,128)(2,1)S(1)}, u32[]{:S(2)}, u32[]{:S(2)}) %collective-permute-start.9) | collective-permute-done | bytes 278560 | tf_op jit(solution)/shard_map/ppermute | solution.py:21
  40.2 9.5 %shard_map.96 = (bf16[256,2048]{1,0:T(8,128)(2,1)S(1)}, bf16[256,2048]{1,0:T(8,128)(2,1)S(1)}, bf16[256,768]{1,0:T(8,128)(2,1)S(1)}, bf16[256,1024]{1,0:T(8,128)(2,1)S(1)}) custom-call(s32[1]{0:T(128)} %bitcast.first_ref, s32[1]{0:T(128)} %bitcast.1.expert_ref, s32[1]{0:T(128)} %bitcast.2.place_ref, bf16[64,2176]{1,0:T(8,128)(2,1)S(1)} %shard_map.94.refs_0_, ...), custom_call_target="tpu_custom_call" | custom-call | flops 1000000 | bytes 100000 | tf_op jit(solution)/shard_map/pallas_call | solution.py:178
  49.7 0.2 collective-permute-start.16
  49.9 1.6 %collective-permute-start.17 = (bf16[256,1024]{1,0:T(8,128)(2,1)S(1)}, bf16[256,1024]{1,0:T(8,128)(2,1)S(1)}, u32[]{:S(2)}, u32[]{:S(2)}) collective-permute-start(bf16[256,1024]{1,0:T(8,128)(2,1)S(1)} %shard_map.95), channel_id=1, source_target_pairs={{0,1},{1,0},{2,3},{3,2},{4,5},{5,4},{6,7},{7,6},{8,9},{9,8},{10,11... | collective-permute-start | bytes 1572872 | tf_op jit(solution)/shard_map/ppermute | solution.py:21
  51.5 0.9 collective-permute-done.16
  52.4 0.5 add.35
  52.9 0.1 fusion.7
  53.0 1.7 %collective-permute-start.18 = (bf16[64,2048]{1,0:T(8,128)(2,1)S(1)}, bf16[64,2048]{1,0:T(8,128)(2,1)S(1)}, u32[]{:S(2)}, u32[]{:S(2)}) collective-permute-start(bf16[64,2048]{1,0:T(8,128)(2,1)S(1)} %get-tuple-element.150), channel_id=1, source_target_pairs={{0,4},{2,6},{4,0},{6,2},{8,12},{10,14},{12,8},{14,10},{16,20},{18,... | collective-permute-start | bytes 786440 | tf_op jit(solution)/shard_map/ppermute | solution.py:21
  54.7 9.7 %shard_map.97 = (bf16[256,2048]{1,0:T(8,128)(2,1)S(1)}, bf16[256,2048]{1,0:T(8,128)(2,1)S(1)}, bf16[256,768]{1,0:T(8,128)(2,1)S(1)}, bf16[256,1024]{1,0:T(8,128)(2,1)S(1)}) custom-call(s32[1]{0:T(128)} %bitcast.first_ref, s32[1]{0:T(128)} %bitcast.1.expert_ref, s32[1]{0:T(128)} %bitcast.2.place_ref, ...), custom_call_target="tpu_custom_call" | custom-call | flops 1000000 | bytes 100000 | tf_op jit(solution)/shard_map/pallas_call | solution.py:178
  64.5 3.0 %collective-permute-start.21 = (bf16[64,2048]{1,0:T(8,128)(2,1)S(1)}, bf16[64,2048]{1,0:T(8,128)(2,1)S(1)}, u32[]{:S(2)}, u32[]{:S(2)}) collective-permute-start(bf16[64,2048]{1,0:T(8,128)(2,1)S(1)} %add.36), channel_id=1, source_target_pairs={{0,16},{2,18},{4,20},{6,22},{8,24},{10,26},{12,28},{14,30},{16,0},... | collective-permute-start | bytes 786440 | tf_op jit(solution)/shard_map/ppermute | solution.py:21
  67.5 0.4 add.37
  68.0 1.5 %collective-permute-start.20 = (bf16[128,2048]{1,0:T(8,128)(2,1)S(1)}, bf16[128,2048]{1,0:T(8,128)(2,1)S(1)}, u32[]{:S(2)}, u32[]{:S(2)}) collective-permute-start(bf16[128,2048]{1,0:T(8,128)(2,1)S(1)} %slice.52), channel_id=1, source_target_pairs={{0,8},{2,10},{4,12},{6,14},{8,0},{10,2},{12,4},{14,6},{16,24},{18,... | collective-permute-start | bytes 1572872 | tf_op jit(solution)/shard_map/ppermute | solution.py:21
  69.5 1.4 %collective-permute-start.23 = (bf16[64,2048]{1,0:T(8,128)(2,1)S(1)}, bf16[64,2048]{1,0:T(8,128)(2,1)S(1)}, u32[]{:S(2)}, u32[]{:S(2)}) collective-permute-start(bf16[64,2048]{1,0:T(8,128)(2,1)S(1)} %get-tuple-element.155), channel_id=1, source_target_pairs={{0,4},{2,6},{4,0},{6,2},{8,12},{10,14},{12,8},{14,10},{16,20},{18,... | collective-permute-start | bytes 786440 | tf_op jit(solution)/shard_map/ppermute | solution.py:21
  70.9 1.5 %collective-permute-start.25 = (bf16[256,768]{1,0:T(8,128)(2,1)S(1)}, bf16[256,768]{1,0:T(8,128)(2,1)S(1)}, u32[]{:S(2)}, u32[]{:S(2)}) collective-permute-start(bf16[256,768]{1,0:T(8,128)(2,1)S(1)} %get-tuple-element.134.refs_1_), channel_id=1, source_target_pairs={{0,1},{1,0},{2,3},{3,2},{4,5},{5,4},{6,7},{7,6},{8,9},{9,8},{10,11... | collective-permute-start | bytes 1179656 | tf_op jit(solution)/shard_map/ppermute | solution.py:21
  72.4 1.6 %shard_map.98.refs_4_ = f32[1024,768]{1,0:T(8,128)S(1)} custom-call(bf16[256,1024]{1,0:T(8,128)(2,1)S(1)} %get-tuple-element.133.refs_0_, bf16[256,768]{1,0:T(8,128)(2,1)S(1)} %get-tuple-element.134.refs_1_, bf16[256,1024]{1,0:T(8,128)(2,1)S(1)} %get-tuple-element.135.refs_2_, bf16[256,768]{1,0:T(8,128)(2,1)S(1)} %get-tuple-element.136.refs_3_), custom_call_target="tpu_custom_call" | custom-call | flops 1000000 | bytes 100000 | tf_op jit(solution)/shard_map/pallas_call | solution.py:241
  74.1 0.6 collective-permute-start.26
  74.7 5.5 %collective-permute-done.21 = bf16[64,2048]{1,0:T(8,128)(2,1)S(1)} collective-permute-done((bf16[64,2048]{1,0:T(8,128)(2,1)S(1)}, bf16[64,2048]{1,0:T(8,128)(2,1)S(1)}, u32[]{:S(2)}, u32[]{:S(2)}) %collective-permute-start.21) | collective-permute-done | bytes 262176 | tf_op jit(solution)/shard_map/ppermute | solution.py:21
  80.1 6.5 %collective-permute-done.20 = bf16[128,2048]{1,0:T(8,128)(2,1)S(1)} collective-permute-done((bf16[128,2048]{1,0:T(8,128)(2,1)S(1)}, bf16[128,2048]{1,0:T(8,128)(2,1)S(1)}, u32[]{:S(2)}, u32[]{:S(2)}) %collective-permute-start.20) | collective-permute-done | bytes 524320 | tf_op jit(solution)/shard_map/ppermute | solution.py:21
  86.8 4.3 %collective-permute-start.24 = (bf16[64,2048]{1,0:T(8,128)(2,1)S(1)}, bf16[64,2048]{1,0:T(8,128)(2,1)S(1)}, u32[]{:S(2)}, u32[]{:S(2)}) collective-permute-start(bf16[64,2048]{1,0:T(8,128)(2,1)S(1)} %add.38), channel_id=1, source_target_pairs={{0,24},{2,26},{4,28},{6,30},{8,16},{10,18},{12,20},{14,22},{16,8},... | collective-permute-start | bytes 786440 | tf_op jit(solution)/shard_map/ppermute | solution.py:21
  91.1 1.4 %collective-permute-start.27 = (bf16[64,2048]{1,0:T(8,128)(2,1)S(1)}, bf16[64,2048]{1,0:T(8,128)(2,1)S(1)}, u32[]{:S(2)}, u32[]{:S(2)}) collective-permute-start(bf16[64,2048]{1,0:T(8,128)(2,1)S(1)} %slice_add_fusion), channel_id=1, source_target_pairs={{0,4},{2,6},{4,0},{6,2},{8,12},{10,14},{12,8},{14,10},{16,20},{18,... | collective-permute-start | bytes 786440 | tf_op jit(solution)/shard_map/ppermute | solution.py:21
  92.6 3.3 %shard_map.99 = f32[1024,1,768]{2,1,0:T(1,128)} custom-call(bf16[256,1024]{1,0:T(8,128)(2,1)S(1)} %get-tuple-element.154.refs_0_, bf16[256,768]{1,0:T(8,128)(2,1)S(1)} %collective-permute-done.25.refs_1_, bf16[256,1024]{1,0:T(8,128)(2,1)S(1)} %get-tuple-element.153.refs_2_, bf16[256,768]{1,0:T(8,128)(2,1)S(1)} %collective-permute-done.26.refs_3_, ...), custom_call_target="tpu_custom_call" | custom-call | flops 1000000 | bytes 100000 | tf_op jit(solution)/shard_map/pallas_call | solution.py:241
  95.9 1.0 %collective-permute-done.24 = bf16[64,2048]{1,0:T(8,128)(2,1)S(1)} collective-permute-done((bf16[64,2048]{1,0:T(8,128)(2,1)S(1)}, bf16[64,2048]{1,0:T(8,128)(2,1)S(1)}, u32[]{:S(2)}, u32[]{:S(2)}) %collective-permute-start.24) | collective-permute-done | bytes 262176 | tf_op jit(solution)/shard_map/ppermute | solution.py:21
  96.9 0.1 convert_add_fusion
  97.1 1.3 %collective-permute-done.27 = bf16[64,2048]{1,0:T(8,128)(2,1)S(1)} collective-permute-done((bf16[64,2048]{1,0:T(8,128)(2,1)S(1)}, bf16[64,2048]{1,0:T(8,128)(2,1)S(1)}, u32[]{:S(2)}, u32[]{:S(2)}) %collective-permute-start.27) | collective-permute-done | bytes 262176 | tf_op jit(solution)/shard_map/ppermute | solution.py:21
  98.6 1.3 %collective-permute-done.28 = bf16[32,2048]{1,0:T(8,128)(2,1)S(1)} collective-permute-done((bf16[32,2048]{1,0:T(8,128)(2,1)S(1)}, bf16[32,2048]{1,0:T(8,128)(2,1)S(1)}, u32[]{:S(2)}, u32[]{:S(2)}) %collective-permute-start.28) | collective-permute-done | bytes 131104 | tf_op jit(solution)/shard_map/ppermute | solution.py:21
  99.9 0.7 broadcast_select_fusion.2
  (38 shorter events, 0.8 us)
Async XLA Ops:
  1.6 2.3 %collective-permute-start = (bf16[32,2048]{1,0:T(8,128)(2,1)S(1)}, bf16[32,2048]{1,0:T(8,128)(2,1)S(1)}, u32[]{:S(2)}, u32[]{:S(2)}) collective-permute-start(bf16[32,2048]{1,0:T(8,128)(2,1)S(1)} %get-tuple-element.159), channel_id=1, source_target_pairs={{0,2},{2,0},{4,6},{6,4},{8,10},{10,8},{12,14},{14,12},{16,18},{18,... | collective-permute-start | bytes 393224 | tf_op jit(solution)/shard_map/ppermute | solution.py:21
  4.0 17.1 %collective-permute-start.2 = (bf16[64,2176]{1,0:T(8,128)(2,1)S(1)}, bf16[64,2176]{1,0:T(8,128)(2,1)S(1)}, u32[]{:S(2)}, u32[]{:S(2)}) collective-permute-start(bf16[64,2176]{1,0:T(8,128)(2,1)S(1)} %shard_map.94.refs_0_), channel_id=1, source_target_pairs={{0,16},{2,18},{4,20},{6,22},{8,24},{10,26},{12,28},{14,30},{16,0},... | collective-permute-start | bytes 835592 | tf_op jit(solution)/shard_map/ppermute | solution.py:21
  7.7 15.6 %collective-permute-start.5 = (bf16[64,2176]{1,0:T(8,128)(2,1)S(1)}, bf16[64,2176]{1,0:T(8,128)(2,1)S(1)}, u32[]{:S(2)}, u32[]{:S(2)}) collective-permute-start(bf16[64,2176]{1,0:T(8,128)(2,1)S(1)} %shard_map.94.refs_0_), channel_id=1, source_target_pairs={{0,8},{2,10},{4,12},{6,14},{8,0},{10,2},{12,4},{14,6},{16,24},{18,... | collective-permute-start | bytes 835592 | tf_op jit(solution)/shard_map/ppermute | solution.py:21
  9.3 14.0 %collective-permute-start.1 = (bf16[64,2176]{1,0:T(8,128)(2,1)S(1)}, bf16[64,2176]{1,0:T(8,128)(2,1)S(1)}, u32[]{:S(2)}, u32[]{:S(2)}) collective-permute-start(bf16[64,2176]{1,0:T(8,128)(2,1)S(1)} %shard_map.94.refs_0_), channel_id=1, source_target_pairs={{0,4},{2,6},{4,0},{6,2},{8,12},{10,14},{12,8},{14,10},{16,20},{18,... | collective-permute-start | bytes 835592 | tf_op jit(solution)/shard_map/ppermute | solution.py:21
  21.1 9.5 %collective-permute-start.4 = (bf16[64,2176]{1,0:T(8,128)(2,1)S(1)}, bf16[64,2176]{1,0:T(8,128)(2,1)S(1)}, u32[]{:S(2)}, u32[]{:S(2)}) collective-permute-start(bf16[64,2176]{1,0:T(8,128)(2,1)S(1)} %collective-permute-done.2.refs_2_), channel_id=1, source_target_pairs={{0,8},{2,10},{4,12},{6,14},{8,0},{10,2},{12,4},{14,6},{16,24},{18,... | collective-permute-start | bytes 835592 | tf_op jit(solution)/shard_map/ppermute | solution.py:21
  21.7 11.0 %collective-permute-start.3 = (bf16[64,2176]{1,0:T(8,128)(2,1)S(1)}, bf16[64,2176]{1,0:T(8,128)(2,1)}, u32[]{:S(2)}, u32[]{:S(2)}) collective-permute-start(bf16[64,2176]{1,0:T(8,128)(2,1)S(1)} %collective-permute-done.2.refs_2_), channel_id=1, source_target_pairs={{0,4},{2,6},{4,0},{6,2},{8,12},{10,14},{12,8},{14,10},{16,20},{18,... | collective-permute-start | bytes 835592 | tf_op jit(solution)/shard_map/ppermute | solution.py:21
  23.2 12.2 %collective-permute-start.11 = (bf16[64,2176]{1,0:T(8,128)(2,1)S(1)}, bf16[64,2176]{1,0:T(8,128)(2,1)S(1)}, u32[]{:S(2)}, u32[]{:S(2)}) collective-permute-start(bf16[64,2176]{1,0:T(8,128)(2,1)S(1)} %collective-permute-done.1.refs_1_), channel_id=1, source_target_pairs={{0,8},{2,10},{4,12},{6,14},{8,0},{10,2},{12,4},{14,6},{16,24},{18,... | collective-permute-start | bytes 835592 | tf_op jit(solution)/shard_map/ppermute | solution.py:21
  30.6 6.5 %collective-permute-start.14 = (bf16[64,2176]{1,0:T(8,128)(2,1)S(1)}, bf16[64,2176]{1,0:T(8,128)(2,1)S(1)}, u32[]{:S(2)}, u32[]{:S(2)}) collective-permute-start(bf16[64,2176]{1,0:T(8,128)(2,1)S(1)} %collective-permute-done.4.refs_6_.refs_2_), channel_id=1, source_target_pairs={{0,4},{2,6},{4,0},{6,2},{8,12},{10,14},{12,8},{14,10},{16,20},{18,... | collective-permute-start | bytes 835592 | tf_op jit(solution)/shard_map/ppermute | solution.py:21
  32.2 5.0 %collective-permute-start.6 = (bf16[64,2176]{1,0:T(8,128)(2,1)S(1)}, bf16[64,2176]{1,0:T(8,128)(2,1)S(1)}, u32[]{:S(2)}, u32[]{:S(2)}) collective-permute-start(bf16[64,2176]{1,0:T(8,128)(2,1)S(1)} %shard_map.94.refs_0_), channel_id=1, source_target_pairs={{0,2},{2,0},{4,6},{6,4},{8,10},{10,8},{12,14},{14,12},{16,18},{18,... | collective-permute-start | bytes 835592 | tf_op jit(solution)/shard_map/ppermute | solution.py:21
  32.2 5.5 %collective-permute-start.10 = (bf16[64,2176]{1,0:T(8,128)(2,1)S(1)}, bf16[64,2176]{1,0:T(8,128)(2,1)S(1)}, u32[]{:S(2)}, u32[]{:S(2)}) collective-permute-start(bf16[64,2176]{1,0:T(8,128)(2,1)S(1)} %collective-permute-done.5.refs_4_.refs_0_), channel_id=1, source_target_pairs={{0,2},{2,0},{4,6},{6,4},{8,10},{10,8},{12,14},{14,12},{16,18},{18,... | collective-permute-start | bytes 835592 | tf_op jit(solution)/shard_map/ppermute | solution.py:21
  32.7 5.0 %collective-permute-start.8 = (bf16[64,2176]{1,0:T(8,128)(2,1)S(1)}, bf16[64,2176]{1,0:T(8,128)(2,1)S(1)}, u32[]{:S(2)}, u32[]{:S(2)}) collective-permute-start(bf16[64,2176]{1,0:T(8,128)(2,1)S(1)} %collective-permute-done.2.refs_2_), channel_id=1, source_target_pairs={{0,2},{2,0},{4,6},{6,4},{8,10},{10,8},{12,14},{14,12},{16,18},{18,... | collective-permute-start | bytes 835592 | tf_op jit(solution)/shard_map/ppermute | solution.py:21
  35.5 2.7 %collective-permute-start.7 = (bf16[64,2176]{1,0:T(8,128)(2,1)S(1)}, bf16[64,2176]{1,0:T(8,128)(2,1)S(1)}, u32[]{:S(2)}, u32[]{:S(2)}) collective-permute-start(bf16[64,2176]{1,0:T(8,128)(2,1)S(1)} %collective-permute-done.1.refs_1_), channel_id=1, source_target_pairs={{0,2},{2,0},{4,6},{6,4},{8,10},{10,8},{12,14},{14,12},{16,18},{18,... | collective-permute-start | bytes 835592 | tf_op jit(solution)/shard_map/ppermute | solution.py:21
  37.2 1.7 %collective-permute-start.13 = (bf16[64,2176]{1,0:T(8,128)(2,1)S(1)}, bf16[64,2176]{1,0:T(8,128)(2,1)}, u32[]{:S(2)}, u32[]{:S(2)}) collective-permute-start(bf16[64,2176]{1,0:T(8,128)(2,1)S(1)} %collective-permute-done.4.refs_6_.refs_2_), channel_id=1, source_target_pairs={{0,2},{2,0},{4,6},{6,4},{8,10},{10,8},{12,14},{14,12},{16,18},{18,... | collective-permute-start | bytes 835592 | tf_op jit(solution)/shard_map/ppermute | solution.py:21
  37.2 3.0 %collective-permute-start.12 = (bf16[64,2176]{1,0:T(8,128)(2,1)S(1)}, bf16[64,2176]{1,0:T(8,128)(2,1)}, u32[]{:S(2)}, u32[]{:S(2)}) collective-permute-start(bf16[64,2176]{1,0:T(8,128)(2,1)S(1)} %collective-permute-done.11.refs_5_.refs_1_), channel_id=1, source_target_pairs={{0,2},{2,0},{4,6},{6,4},{8,10},{10,8},{12,14},{14,12},{16,18},{18,... | collective-permute-start | bytes 835592 | tf_op jit(solution)/shard_map/ppermute | solution.py:21
  37.7 2.4 %collective-permute-start.9 = (bf16[64,2176]{1,0:T(8,128)(2,1)}, bf16[64,2176]{1,0:T(8,128)(2,1)S(1)}, u32[]{:S(2)}, u32[]{:S(2)}) collective-permute-start(bf16[64,2176]{1,0:T(8,128)(2,1)} %collective-permute-done.3.refs_3_), channel_id=1, source_target_pairs={{0,2},{2,0},{4,6},{6,4},{8,10},{10,8},{12,14},{14,12},{16,18},{18,... | collective-permute-start | bytes 835592 | tf_op jit(solution)/shard_map/ppermute | solution.py:21
  37.8 2.4 %collective-permute-start.15 = (bf16[64,2176]{1,0:T(8,128)(2,1)S(1)}, bf16[64,2176]{1,0:T(8,128)(2,1)}, u32[]{:S(2)}, u32[]{:S(2)}) collective-permute-start(bf16[64,2176]{1,0:T(8,128)(2,1)S(1)} %collective-permute-done.14.refs_7_.refs_3_), channel_id=1, source_target_pairs={{0,2},{2,0},{4,6},{6,4},{8,10},{10,8},{12,14},{14,12},{16,18},{18,... | collective-permute-start | bytes 835592 | tf_op jit(solution)/shard_map/ppermute | solution.py:21
  49.7 2.7 %collective-permute-start.16 = (bf16[256,2048]{1,0:T(8,128)(2,1)S(1)}, bf16[256,2048]{1,0:T(8,128)(2,1)S(1)}, u32[]{:S(2)}, u32[]{:S(2)}) collective-permute-start(bf16[256,2048]{1,0:T(8,128)(2,1)S(1)} %get-tuple-element.107), channel_id=1, source_target_pairs={{0,2},{2,0},{4,6},{6,4},{8,10},{10,8},{12,14},{14,12},{16,18},{18,... | collective-permute-start | bytes 3145736 | tf_op jit(solution)/shard_map/ppermute | solution.py:21
  49.9 14.4 %collective-permute-start.17 = (bf16[256,1024]{1,0:T(8,128)(2,1)S(1)}, bf16[256,1024]{1,0:T(8,128)(2,1)S(1)}, u32[]{:S(2)}, u32[]{:S(2)}) collective-permute-start(bf16[256,1024]{1,0:T(8,128)(2,1)S(1)} %shard_map.95), channel_id=1, source_target_pairs={{0,1},{1,0},{2,3},{3,2},{4,5},{5,4},{6,7},{7,6},{8,9},{9,8},{10,11... | collective-permute-start | bytes 1572872 | tf_op jit(solution)/shard_map/ppermute | solution.py:21
  53.0 11.4 %collective-permute-start.18 = (bf16[64,2048]{1,0:T(8,128)(2,1)S(1)}, bf16[64,2048]{1,0:T(8,128)(2,1)S(1)}, u32[]{:S(2)}, u32[]{:S(2)}) collective-permute-start(bf16[64,2048]{1,0:T(8,128)(2,1)S(1)} %get-tuple-element.150), channel_id=1, source_target_pairs={{0,4},{2,6},{4,0},{6,2},{8,12},{10,14},{12,8},{14,10},{16,20},{18,... | collective-permute-start | bytes 786440 | tf_op jit(solution)/shard_map/ppermute | solution.py:21
  64.5 3.1 %collective-permute-start.19 = (bf16[256,2048]{1,0:T(8,128)(2,1)S(1)}, bf16[256,2048]{1,0:T(8,128)(2,1)S(1)}, u32[]{:S(2)}, u32[]{:S(2)}) collective-permute-start(bf16[256,2048]{1,0:T(8,128)(2,1)S(1)} %get-tuple-element.124), channel_id=1, source_target_pairs={{0,2},{2,0},{4,6},{6,4},{8,10},{10,8},{12,14},{14,12},{16,18},{18,... | collective-permute-start | bytes 3145736 | tf_op jit(solution)/shard_map/ppermute | solution.py:21
  64.5 15.6 %collective-permute-start.21 = (bf16[64,2048]{1,0:T(8,128)(2,1)S(1)}, bf16[64,2048]{1,0:T(8,128)(2,1)S(1)}, u32[]{:S(2)}, u32[]{:S(2)}) collective-permute-start(bf16[64,2048]{1,0:T(8,128)(2,1)S(1)} %add.36), channel_id=1, source_target_pairs={{0,16},{2,18},{4,20},{6,22},{8,24},{10,26},{12,28},{14,30},{16,0},... | collective-permute-start | bytes 786440 | tf_op jit(solution)/shard_map/ppermute | solution.py:21
  68.0 18.7 %collective-permute-start.20 = (bf16[128,2048]{1,0:T(8,128)(2,1)S(1)}, bf16[128,2048]{1,0:T(8,128)(2,1)S(1)}, u32[]{:S(2)}, u32[]{:S(2)}) collective-permute-start(bf16[128,2048]{1,0:T(8,128)(2,1)S(1)} %slice.52), channel_id=1, source_target_pairs={{0,8},{2,10},{4,12},{6,14},{8,0},{10,2},{12,4},{14,6},{16,24},{18,... | collective-permute-start | bytes 1572872 | tf_op jit(solution)/shard_map/ppermute | solution.py:21
  69.5 4.6 %collective-permute-start.22 = (bf16[256,1024]{1,0:T(8,128)(2,1)S(1)}, bf16[256,1024]{1,0:T(8,128)(2,1)S(1)}, u32[]{:S(2)}, u32[]{:S(2)}) collective-permute-start(bf16[256,1024]{1,0:T(8,128)(2,1)S(1)} %collective-permute-done.17), channel_id=1, source_target_pairs={{0,2},{2,0},{4,6},{6,4},{8,10},{10,8},{12,14},{14,12},{16,18},{18,... | collective-permute-start | bytes 1572872 | tf_op jit(solution)/shard_map/ppermute | solution.py:21
  69.5 17.2 %collective-permute-start.23 = (bf16[64,2048]{1,0:T(8,128)(2,1)S(1)}, bf16[64,2048]{1,0:T(8,128)(2,1)S(1)}, u32[]{:S(2)}, u32[]{:S(2)}) collective-permute-start(bf16[64,2048]{1,0:T(8,128)(2,1)S(1)} %get-tuple-element.155), channel_id=1, source_target_pairs={{0,4},{2,6},{4,0},{6,2},{8,12},{10,14},{12,8},{14,10},{16,20},{18,... | collective-permute-start | bytes 786440 | tf_op jit(solution)/shard_map/ppermute | solution.py:21
  70.9 21.7 %collective-permute-start.25 = (bf16[256,768]{1,0:T(8,128)(2,1)S(1)}, bf16[256,768]{1,0:T(8,128)(2,1)S(1)}, u32[]{:S(2)}, u32[]{:S(2)}) collective-permute-start(bf16[256,768]{1,0:T(8,128)(2,1)S(1)} %get-tuple-element.134.refs_1_), channel_id=1, source_target_pairs={{0,1},{1,0},{2,3},{3,2},{4,5},{5,4},{6,7},{7,6},{8,9},{9,8},{10,11... | collective-permute-start | bytes 1179656 | tf_op jit(solution)/shard_map/ppermute | solution.py:21
  74.1 18.4 %collective-permute-start.26 = (bf16[256,768]{1,0:T(8,128)(2,1)S(1)}, bf16[256,768]{1,0:T(8,128)(2,1)S(1)}, u32[]{:S(2)}, u32[]{:S(2)}) collective-permute-start(bf16[256,768]{1,0:T(8,128)(2,1)S(1)} %get-tuple-element.136.refs_3_), channel_id=1, source_target_pairs={{0,1},{1,0},{2,3},{3,2},{4,5},{5,4},{6,7},{7,6},{8,9},{9,8},{10,11... | collective-permute-start | bytes 1179656 | tf_op jit(solution)/shard_map/ppermute | solution.py:21
  86.8 10.2 %collective-permute-start.24 = (bf16[64,2048]{1,0:T(8,128)(2,1)S(1)}, bf16[64,2048]{1,0:T(8,128)(2,1)S(1)}, u32[]{:S(2)}, u32[]{:S(2)}) collective-permute-start(bf16[64,2048]{1,0:T(8,128)(2,1)S(1)} %add.38), channel_id=1, source_target_pairs={{0,24},{2,26},{4,28},{6,30},{8,16},{10,18},{12,20},{14,22},{16,8},... | collective-permute-start | bytes 786440 | tf_op jit(solution)/shard_map/ppermute | solution.py:21
  91.1 7.3 %collective-permute-start.27 = (bf16[64,2048]{1,0:T(8,128)(2,1)S(1)}, bf16[64,2048]{1,0:T(8,128)(2,1)S(1)}, u32[]{:S(2)}, u32[]{:S(2)}) collective-permute-start(bf16[64,2048]{1,0:T(8,128)(2,1)S(1)} %slice_add_fusion), channel_id=1, source_target_pairs={{0,4},{2,6},{4,0},{6,2},{8,12},{10,14},{12,8},{14,10},{16,20},{18,... | collective-permute-start | bytes 786440 | tf_op jit(solution)/shard_map/ppermute | solution.py:21
  98.5 1.4 %collective-permute-start.28 = (bf16[32,2048]{1,0:T(8,128)(2,1)S(1)}, bf16[32,2048]{1,0:T(8,128)(2,1)S(1)}, u32[]{:S(2)}, u32[]{:S(2)}) collective-permute-start(bf16[32,2048]{1,0:T(8,128)(2,1)S(1)} %broadcast_select_fusion.4), channel_id=1, source_target_pairs={{0,2},{2,0},{4,6},{6,4},{8,10},{10,8},{12,14},{14,12},{16,18},{18,... | collective-permute-start | bytes 393224 | tf_op jit(solution)/shard_map/ppermute | solution.py:21

commit v4 on v3

--- a/solution.py
+++ b/solution.py
@@ -8,7 +8,7 @@
 from jax.sharding import PartitionSpec as P
 
 TILE = 256
-OUT_TILE = 512
+OUT_TILE = 1024
 SHARE_TILE = 256
 LANES = 128
 LIMIT = 12 * 1024 * 1024
@@ -104,75 +104,79 @@
 
 def piece_kernel(n_expert, n_edata, count, first_ref, expert_ref, place_ref, *refs):
     mine, theirs, (gate_hbm, up_hbm, down_hbm) = refs[:count], refs[count : 2 * count], refs[2 * count : 2 * count + 3]
-    kept_ref, sent_ref, scaled_ref, share_ref = refs[2 * count + 3 : -12]
+    kept_refs, sent_refs, scaled_refs, share_refs = (refs[2 * count + 3 + 2 * i : 2 * count + 5 + 2 * i] for i in range(4))
     rows_ref, grads_ref, lanes_ref, hidden_ref, act_ref, slope_ref, grad_gate_ref, grad_up_ref, gate_ref, up_ref, down_ref, sems = refs[-12:]
     width, units = gate_ref.shape
+    half = rows_ref.shape[0] // 2
     pairs = []
     for at in range(0, units, TILE):
         columns = pl.ds(at, TILE)
         pairs.append((gate_hbm.at[0, :, columns], gate_ref.at[:, columns]))
         pairs.append((up_hbm.at[0, :, columns], up_ref.at[:, columns]))
     pairs += [(down_hbm.at[0, :, pl.ds(at, OUT_TILE)], down_ref.at[:, pl.ds(at, OUT_TILE)]) for at in range(0, width, OUT_TILE)]
-    stream = Stream(pairs, sems, 4)
-
-    def unpack(tokens, grads):
+
+    def body(sources, targets):
+        out_refs, grad_refs = targets
+        stream = Stream(pairs, sems, 6)
         at = 0
-        for token, grad in zip(tokens, grads):
+        for token, grad in zip(*sources):
             block = slice(at, at + token.shape[0])
             rows_ref[block, :] = token[:, :width]
             grads_ref[block, :] = grad[:, :width]
             lanes_ref[block, :] = token[:, width:].astype(F32) + grad[:, width:].astype(F32)
             at += token.shape[0]
-
-    choose(first_ref[0], unpack, mine, theirs)
-    values = lanes_ref[...]
-    lane = lax.broadcasted_iota(jnp.int32, values.shape, 1)
-    expert = expert_ref[0]
-    weight = jnp.where(lane == expert, 64.0, 0.0) + jnp.where(lane == expert + n_expert, 1.0, 0.0)
-    whole = jnp.where(lane == 2 * n_expert, 256.0, 0.0) + jnp.where(lane == 2 * n_expert + 1, 1.0, 0.0)
-    gate = jnp.sum(values * weight, axis=1, keepdims=True) / jnp.sum(values * whole, axis=1, keepdims=True)
-    share = width // n_edata
-    share_ref[...] = grads_ref[:, pl.ds(pl.multiple_of(place_ref[0] * share, LANES), share)]
-
-    for at in range(0, units, TILE):
-        columns = slice(at, at + TILE)
-        stream.wait(2)
-        gate_pre = dot(rows_ref[...], gate_ref[:, columns], ((1,), (0,)))
-        up_pre = dot(rows_ref[...], up_ref[:, columns], ((1,), (0,)))
-        sig_gate = jax.nn.sigmoid(gate_pre)
-        act_gate = gate_pre * sig_gate
-        hidden = (act_gate * up_pre).astype(BF16)
-        hidden_ref[:, columns] = hidden
-        scaled_ref[:, columns] = (hidden.astype(F32) * gate).astype(BF16)
-        act_ref[:, columns] = act_gate * gate
-        slope_ref[:, columns] = up_pre * sig_gate * (1.0 + gate_pre * (1.0 - sig_gate)) * gate
-    for at in range(0, width, OUT_TILE):
-        columns = slice(at, at + OUT_TILE)
-        stream.wait(1)
-        rows_ref[:, columns] = (dot(hidden_ref[...], down_ref[:, columns], ((1,), (0,))) * gate).astype(BF16)
-    for at in range(0, units, TILE):
-        columns = slice(at, at + TILE)
-        grad_hidden = dot(grads_ref[...], down_ref[columns, :], ((1,), (1,)))
-        grad_gate_ref[:, columns] = (grad_hidden * slope_ref[:, columns]).astype(BF16)
-        grad_up_ref[:, columns] = (grad_hidden * act_ref[:, columns]).astype(BF16)
-    for at in range(0, width, OUT_TILE):
-        columns = slice(at, at + OUT_TILE)
-        grad = dot(grad_gate_ref[...], gate_ref[columns, :], ((1,), (1,)))
-        grad = grad + dot(grad_up_ref[...], up_ref[columns, :], ((1,), (1,)))
-        grads_ref[:, columns] = grad.astype(BF16)
-
-    def give(own, other):
-        own[...] = rows_ref[...]
-        other[...] = grads_ref[...]
-
-    choose(first_ref[0], give, kept_ref, sent_ref)
+        values = lanes_ref[...]
+        lane = lax.broadcasted_iota(jnp.int32, values.shape, 1)
+        expert = expert_ref[0]
+        weight = jnp.where(lane == expert, 64.0, 0.0) + jnp.where(lane == expert + n_expert, 1.0, 0.0)
+        whole = jnp.where(lane == 2 * n_expert, 256.0, 0.0) + jnp.where(lane == 2 * n_expert + 1, 1.0, 0.0)
+        gate = jnp.sum(values * weight, axis=1, keepdims=True) / jnp.sum(values * whole, axis=1, keepdims=True)
+        share = share_refs[0].shape[1]
+        columns = pl.ds(pl.multiple_of(place_ref[0] * share, LANES), share)
+        share_refs[0][...] = grads_ref[:half, columns]
+        share_refs[1][...] = grads_ref[half:, columns]
+
+        for at in range(0, units, TILE):
+            columns = slice(at, at + TILE)
+            stream.wait(2)
+            gate_pre = dot(rows_ref[...], gate_ref[:, columns], ((1,), (0,)))
+            up_pre = dot(rows_ref[...], up_ref[:, columns], ((1,), (0,)))
+            sig_gate = jax.nn.sigmoid(gate_pre)
+            act_gate = gate_pre * sig_gate
+            hidden = (act_gate * up_pre).astype(BF16)
+            hidden_ref[:, columns] = hidden
+            scaled = (hidden.astype(F32) * gate).astype(BF16)
+            scaled_refs[0][:, columns] = scaled[:half]
+            scaled_refs[1][:, columns] = scaled[half:]
+            act_ref[:, columns] = act_gate * gate
+            slope_ref[:, columns] = up_pre * sig_gate * (1.0 + gate_pre * (1.0 - sig_gate)) * gate
+        for at in range(0, width, OUT_TILE):
+            columns = slice(at, at + OUT_TILE)
+            stream.wait(1)
+            out = (dot(hidden_ref[...], down_ref[:, columns], ((1,), (0,))) * gate).astype(BF16)
+            out_refs[0][:, columns] = out[:half]
+            out_refs[1][:, columns] = out[half:]
+        for at in range(0, units, TILE):
+            columns = slice(at, at + TILE)
+            grad_hidden = dot(grads_ref[...], down_ref[columns, :], ((1,), (1,)))
+            grad_gate_ref[:, columns] = (grad_hidden * slope_ref[:, columns]).astype(BF16)
+            grad_up_ref[:, columns] = (grad_hidden * act_ref[:, columns]).astype(BF16)
+        for at in range(0, width, OUT_TILE):
+            columns = slice(at, at + OUT_TILE)
+            grad = dot(grad_gate_ref[...], gate_ref[columns, :], ((1,), (1,)))
+            grad = (grad + dot(grad_up_ref[...], up_ref[columns, :], ((1,), (1,)))).astype(BF16)
+            grad_refs[0][:, columns] = grad[:half]
+            grad_refs[1][:, columns] = grad[half:]
+
+    pl.when(first_ref[0] == 1)(lambda: body((mine, theirs), (kept_refs, sent_refs)))
+    pl.when(first_ref[0] == 0)(lambda: body((theirs, mine), (sent_refs, kept_refs)))
 
 
 def piece(n_expert, n_edata, first, expert, place, mats, mine, theirs):
     width, units = mats[0].shape[1:]
     rows = sum(part.shape[0] for part in mine)
     vmem, smem, hbm = (pl.BlockSpec(memory_space=space) for space in (pltpu.VMEM, pltpu.SMEM, pltpu.HBM))
-    outs = [(rows, width)] * 2 + [(rows, units), (rows, width // n_edata)]
+    outs = [(rows // 2, size) for size in (width, width, units, width // n_edata) for _ in range(2)]
     scratch = [((rows, width), BF16)] * 2 + [((rows, LANES), F32), ((rows, units), BF16)] + [((rows, units), F32)] * 2
     scratch += [((rows, units), BF16)] * 2 + [((width, units), BF16)] * 2 + [((units, width), BF16)]
     return pl.pallas_call(
@@ -181,7 +185,7 @@
         in_specs=[smem] * 3 + [vmem] * (2 * len(mine)) + [hbm] * 3,
         out_specs=[vmem] * len(outs),
         scratch_shapes=[pltpu.VMEM(*shape) for shape in scratch] + [pltpu.SemaphoreType.DMA((2 * units // TILE + width // OUT_TILE,))],
-        compiler_params=pltpu.CompilerParams(vmem_limit_bytes=rows * 88 * 1024),
+        compiler_params=pltpu.CompilerParams(vmem_limit_bytes=(16 + 42 * rows // 1024) * 1024 * 1024),
         cost_estimate=pl.CostEstimate(flops=10**6, bytes_accessed=10**5, transcendentals=0),
     )(first, expert, place, *mine, *theirs, *[pltpu.with_memory_space_constraint(mat, pltpu.HBM) for mat in mats])
 
@@ -218,7 +222,7 @@
     return sum(part.astype(F32) for part in parts)
 
 
-def share_kernel(counts, continued, *refs):
+def share_kernel(counts, *refs):
     out_ref, at, total = refs[-1], 0, None
     columns = pl.ds(pl.multiple_of(pl.program_id(0) * SHARE_TILE, SHARE_TILE), SHARE_TILE)
     for count in counts:
@@ -226,27 +230,22 @@
         term = dot(grads, refs[at + count][...], ((0,), (0,)))
         total = term if total is None else total + term
         at += count + 1
-    if continued:
-        out_ref[...] = (total + refs[at][...])[:, None, :]
-    else:
-        out_ref[...] = total
-
-
-def weight_share(groups, begun):
+    out_ref[...] = total[:, None, :]
+
+
+def weight_share(groups):
     operands = [array for grads, hidden in groups for array in (*grads, hidden)]
     share, units = groups[0][0][0].shape[1], groups[0][1].shape[1]
     specs = [pl.BlockSpec(memory_space=pltpu.VMEM)] * len(operands)
-    plain = pl.BlockSpec((SHARE_TILE, units), lambda i: (i, 0))
-    continued = begun is not None
     return pl.pallas_call(
-        functools.partial(share_kernel, [len(grads) for grads, _ in groups], continued),
-        out_shape=jax.ShapeDtypeStruct((share, 1, units) if continued else (share, units), F32),
+        functools.partial(share_kernel, [len(grads) for grads, _ in groups]),
+        out_shape=jax.ShapeDtypeStruct((share, 1, units), F32),
         grid=(share // SHARE_TILE,),
-        in_specs=specs + [plain] * continued,
-        out_specs=pl.BlockSpec((SHARE_TILE, 1, units), lambda i: (i, 0, 0)) if continued else plain,
+        in_specs=specs,
+        out_specs=pl.BlockSpec((SHARE_TILE, 1, units), lambda i: (i, 0, 0)),
         compiler_params=pltpu.CompilerParams(vmem_limit_bytes=LIMIT),
         cost_estimate=pl.CostEstimate(flops=10**6, bytes_accessed=10**5, transcendentals=0),
-    )(*operands, *([begun] if continued else []))
+    )(*operands)
 
 
 def shards(tokens, out_grad, routes, gate_codes, w_gate, w_up, w_down):
@@ -283,7 +282,7 @@
     pieces_1 = [block, beside, *straight_1, *across_1]
     pieces_2 = [near_own, near_beside, *straight_2, *across_2]
     got_2 = [core(part) for part in pieces_2]
-    got_1 = list(after_all([core(part) for part in pieces_1], *got_2))
+    got_1 = [core(part) for part in pieces_1]
     run = lambda *parts: piece(n_expert, n_edata, *flags, (w_gate, w_up, w_down), parts[: len(parts) // 2], parts[len(parts) // 2 :])
     size = 2 * rows
     cuts = lambda total, count: [total[i * size : (i + 1) * size] for i in range(count)]
@@ -291,33 +290,32 @@
 
     cuts_out = order(lambda *a: cut_shares(n_edata, flags[0], flags[2], a[: len(pieces_1)], a[len(pieces_1) :]), *got_1, *pieces_2)
     mine = [swap(part, "edata", step) for step, part in enumerate(cuts_out, 1)]
-    kept_1, sent_1, scaled_1, share_1 = order(run, *pieces_1, *got_1)
-    scaled_other_1 = [swap(scaled_1, "edata", step) for step in range(1, n_edata)]
-    parts_1 = order(lambda kept, got: cuts(kept + got, 2 + 2 * n_first), kept_1, core(sent_1))
-    crossed_1 = [across(part) for part in parts_1[2 + n_first :]]
-    kept_2, sent_2, scaled_2, share_2 = order(run, *pieces_2, *got_2)
-    scaled_other_2 = [swap(scaled_2, "edata", step) for step in range(1, n_edata)]
-    mine = after_all(mine, kept_2)
-    ready_1 = order(add, *after_all(parts_1[2 : 2 + n_first], *mine), *crossed_1)
+    kept_1, kept_2, sent_1, sent_2, scaled_1, scaled_2, share_1, share_2 = order(run, *pieces_1, *pieces_2, *got_1, *got_2)
+    scaled_other_1, scaled_other_2 = ([swap(scaled, "edata", step) for step in range(1, n_edata)] for scaled in (scaled_1, scaled_2))
+    sums = lambda kept, got: cuts(kept + got, 2 + 2 * n_first)
+    sent_1, sent_2 = after_all([sent_1, sent_2], *mine)
+    got_2, got_1 = core(sent_2), core(sent_1)
+    near_own, near_beside, *parts_2 = order(sums, kept_2, got_2)
+    crossed_2 = [across(part) for part in parts_2[n_first:]]
+    back_beside = swap(near_beside, "expert", 4)
+    own, beside, *parts_1 = order(sums, kept_1, got_1)
+    crossed_1 = [across(part) for part in parts_1[n_first:]]
+    theirs = [core(part) for part in mine]
+    ready_2 = order(add, *after_all(parts_2[:n_first], *theirs), *crossed_2)
+    back_2 = [swap(part, "expert", 4) for part in ready_2]
+    ready = order(lambda part, got: part + got, beside, back_beside)
+    back_pair = across(ready)
+    add_three = lambda *a: tuple(a[i] + a[n_first + i] + a[2 * n_first + i] for i in range(n_first))
+    ready_1 = order(add_three, *after_all(parts_1[:n_first], *scaled_other_1), *crossed_1, *back_2)
     back_1 = [swap(part, "expert", step) for part, step in zip(ready_1, firsts)]
-    sent_2 = core(after(sent_2, *ready_1))
-    near_2, *parts_2 = order(lambda kept, got: ((kept + got)[: 2 * size], *cuts((kept + got)[2 * size :], 2 * n_first)), kept_2, sent_2)
-    crossed_2 = [across(part) for part in parts_2[n_first:]]
-    back_near = swap(near_2, "expert", 4)
-    theirs = [core(after(part, near_2)) for part in mine]
-    own_share = order(lambda *a: weight_share([([a[0]], a[1]), ([a[2]], a[3])], None), share_1, scaled_1, share_2, scaled_2)
-    ready_2 = order(add, *after_all(parts_2[:n_first], *after_all(scaled_other_1, own_share), *theirs), *crossed_2)
-    back_2 = [swap(part, "expert", step + 4) for part, step in zip(ready_2, firsts)]
-    ready = order(lambda part, got: part + got[size:], parts_1[1], after(back_near, *back_1))
-    back_pair = across(ready)
-    others = []
-    for step in range(1, n_edata):
-        here, there = mine[step - 1], theirs[step - 1]
-        others += [([pick(here, there)], scaled_other_1[step - 1]), ([pick(there, here)], after(scaled_other_2[step - 1], ready))]
-    grad_down = weight_share(others, own_share)
+    back_own = swap(after(near_own, *ready_1), "expert", 4)
+    groups = [([share_1], scaled_1), ([share_2], scaled_2)]
+    for here, there, hidden_1, hidden_2 in zip(mine, theirs, scaled_other_1, scaled_other_2):
+        groups += [([pick(here, there)], hidden_1), ([pick(there, here)], hidden_2)]
+    grad_down = weight_share([(after_all(grads, *ready_1), hidden) for grads, hidden in groups])
     order.last = grad_down
-    total = order(lambda own, near, *parts: total_of(own, near[:size], *parts), parts_1[0], back_near, *back_1, *back_2)
-    total = order(lambda total, pair: (total + pair.astype(F32)).astype(BF16), total, back_pair)
+    total = order(total_of, own, back_pair, *back_1)
+    total = order(lambda *parts: total_of(*parts).astype(BF16), total, back_own)
     kept, sent = pick(total[:rows], total[rows:]), pick(total[rows:], total[:rows])
     got = core(sent)
     return pick(kept, got), pick(got, kept), grad_down

time: 101 us -> 91.4 us (0.905)
  Pallas kernels: 24.2 us -> 17.8 us
  starting transfers between devices: 31.3 us -> 27.1 us
  waiting for transfers between devices: 39.3 us -> 40.5 us
    pallas_call x2 -> x1, Pallas kernels: 19.2 us -> 13.8 us  [piece(): pl.pallas_call(functools.partial(piece_kernel, n_expert, n_edata, len(min...]
    ppermute x29 -> x30, starting transfers between devices: 31.3 us -> 27.1 us  [swap(): return lax.ppermute(value, axis, [(i, i ^ distance) for i in range(size)])]
    ppermute x29 -> x30, waiting for transfers between devices: 39.3 us -> 40.5 us  [swap(): return lax.ppermute(value, axis, [(i, i ^ distance) for i in range(size)])]
    pallas_call x2 -> x1, Pallas kernels: 4.94 us -> 3.92 us  [weight_share(): pl.pallas_call(functools.partial(share_kernel, [len(grads) for grads, _ i...]
  transfers between devices with their start and end apart: 29 -> 30, of which waited for: 12 -> 16; matrix products, arithmetic and copies ran while one was open for 3% -> 3% of each run, Pallas kernels for 15% -> 19%
where the time goes in v4:
time: 91.4 us; the launch traced here: 91.2 us
  waiting for transfers between devices  40.5 us (44%)
  starting transfers between devices  27.1 us (30%)
  Pallas kernels  17.8 us (19%)
  other arithmetic  4.43 us (5%)
    ppermute x30, waiting for transfers between devices, swap(): return lax.ppermute(value, axis, [(i, i ^ distance) for i in range(size)])  40.5 us
    ppermute x30, starting transfers between devices, swap(): return lax.ppermute(value, axis, [(i, i ^ distance) for i in range(size)])  27.1 us
    pallas_call x1, Pallas kernels, piece(): pl.pallas_call(functools.partial(piece_kernel, n_expert, n_edata, len(min...  13.8 us
    pallas_call x1, Pallas kernels, weight_share(): pl.pallas_call(functools.partial(share_kernel, [len(grads) for grads, _ i...  3.92 us
  transfers between devices with their start and end apart: 30, of which 16 were waited for; matrix products, arithmetic and copies ran while one was open for 3% of the time, Pallas kernels for 19%

profile of v4, /device:TPU:0, one launch (start us, length us, event | category | flops | bytes accessed | tf_op | source)
XLA Modules:
  0.0 91.2 jit_solution(6205324471717024400)
XLA Ops:
  0.6 1.0 %broadcast_select_fusion.6 = (bf16[32,2048]{1,0:T(8,128)(2,1)S(1)}, bf16[32,2048]{1,0:T(8,128)(2,1)S(1)}) fusion(bf16[32,2048]{1,0:T(8,128)(2,1)} %param.8, bf16[32,2048]{1,0:T(8,128)(2,1)} %param.7, pred[]{:T(512)S(6)} %eq.18), kind=kLoop, calls=%fused_computation.9 | loop fusion | flops 131072 | bytes 524289 | tf_op jit(solution)/shard_map/jit(_where)/select_n | solution.py:258
  1.6 0.5 collective-permute-start
  2.2 0.7 reduce_sum.19
  2.9 0.7 select_reduce_fusion
  3.7 0.1 copy.22
  4.0 3.7 %collective-permute-start.2 = (bf16[64,2176]{1,0:T(8,128)(2,1)S(1)}, bf16[64,2176]{1,0:T(8,128)(2,1)S(1)}, u32[]{:S(2)}, u32[]{:S(2)}) collective-permute-start(bf16[64,2176]{1,0:T(8,128)(2,1)S(1)} %shard_map.94.refs_0_), channel_id=1, source_target_pairs={{0,16},{2,18},{4,20},{6,22},{8,24},{10,26},{12,28},{14,30},{16,0},... | collective-permute-start | bytes 835592 | tf_op jit(solution)/shard_map/ppermute | solution.py:21
  7.7 1.5 %collective-permute-start.1 = (bf16[64,2176]{1,0:T(8,128)(2,1)S(1)}, bf16[64,2176]{1,0:T(8,128)(2,1)S(1)}, u32[]{:S(2)}, u32[]{:S(2)}) collective-permute-start(bf16[64,2176]{1,0:T(8,128)(2,1)S(1)} %shard_map.94.refs_0_), channel_id=1, source_target_pairs={{0,4},{2,6},{4,0},{6,2},{8,12},{10,14},{12,8},{14,10},{16,20},{18,... | collective-permute-start | bytes 835592 | tf_op jit(solution)/shard_map/ppermute | solution.py:21
  9.2 1.6 %collective-permute-start.5 = (bf16[64,2176]{1,0:T(8,128)(2,1)S(1)}, bf16[64,2176]{1,0:T(8,128)(2,1)S(1)}, u32[]{:S(2)}, u32[]{:S(2)}) collective-permute-start(bf16[64,2176]{1,0:T(8,128)(2,1)S(1)} %shard_map.94.refs_0_), channel_id=1, source_target_pairs={{0,8},{2,10},{4,12},{6,14},{8,0},{10,2},{12,4},{14,6},{16,24},{18,... | collective-permute-start | bytes 835592 | tf_op jit(solution)/shard_map/ppermute | solution.py:21
  10.8 10.3 %collective-permute-done.2.refs_2_ = bf16[64,2176]{1,0:T(8,128)(2,1)S(1)} collective-permute-done((bf16[64,2176]{1,0:T(8,128)(2,1)S(1)}, bf16[64,2176]{1,0:T(8,128)(2,1)S(1)}, u32[]{:S(2)}, u32[]{:S(2)}) %collective-permute-start.2) | collective-permute-done | bytes 278560 | tf_op jit(solution)/shard_map/ppermute | solution.py:21
  21.1 0.7 collective-permute-start.4
  21.8 1.5 %collective-permute-start.3 = (bf16[64,2176]{1,0:T(8,128)(2,1)S(1)}, bf16[64,2176]{1,0:T(8,128)(2,1)S(1)}, u32[]{:S(2)}, u32[]{:S(2)}) collective-permute-start(bf16[64,2176]{1,0:T(8,128)(2,1)S(1)} %collective-permute-done.2.refs_2_), channel_id=1, source_target_pairs={{0,4},{2,6},{4,0},{6,2},{8,12},{10,14},{12,8},{14,10},{16,20},{18,... | collective-permute-start | bytes 835592 | tf_op jit(solution)/shard_map/ppermute | solution.py:21
  23.2 1.4 %collective-permute-start.6 = (bf16[64,2176]{1,0:T(8,128)(2,1)S(1)}, bf16[64,2176]{1,0:T(8,128)(2,1)S(1)}, u32[]{:S(2)}, u32[]{:S(2)}) collective-permute-start(bf16[64,2176]{1,0:T(8,128)(2,1)S(1)} %collective-permute-done.1.refs_1_), channel_id=1, source_target_pairs={{0,8},{2,10},{4,12},{6,14},{8,0},{10,2},{12,4},{14,6},{16,24},{18,... | collective-permute-start | bytes 835592 | tf_op jit(solution)/shard_map/ppermute | solution.py:21
  24.7 0.5 collective-permute-start.10
  25.2 5.4 %collective-permute-done.4.refs_6_ = bf16[64,2176]{1,0:T(8,128)(2,1)S(1)} collective-permute-done((bf16[64,2176]{1,0:T(8,128)(2,1)S(1)}, bf16[64,2176]{1,0:T(8,128)(2,1)S(1)}, u32[]{:S(2)}, u32[]{:S(2)}) %collective-permute-start.4) | collective-permute-done | bytes 278560 | tf_op jit(solution)/shard_map/ppermute | solution.py:21
  30.6 1.6 %collective-permute-start.7 = (bf16[64,2176]{1,0:T(8,128)(2,1)S(1)}, bf16[64,2176]{1,0:T(8,128)(2,1)S(1)}, u32[]{:S(2)}, u32[]{:S(2)}) collective-permute-start(bf16[64,2176]{1,0:T(8,128)(2,1)S(1)} %collective-permute-done.4.refs_6_), channel_id=1, source_target_pairs={{0,4},{2,6},{4,0},{6,2},{8,12},{10,14},{12,8},{14,10},{16,20},{18,... | collective-permute-start | bytes 835592 | tf_op jit(solution)/shard_map/ppermute | solution.py:21
  32.2 3.2 %collective-permute-done.6.refs_5_ = bf16[64,2176]{1,0:T(8,128)(2,1)S(1)} collective-permute-done((bf16[64,2176]{1,0:T(8,128)(2,1)S(1)}, bf16[64,2176]{1,0:T(8,128)(2,1)S(1)}, u32[]{:S(2)}, u32[]{:S(2)}) %collective-permute-start.6) | collective-permute-done | bytes 278560 | tf_op jit(solution)/shard_map/ppermute | solution.py:21
  35.5 1.7 %collective-permute-done.7.refs_7_ = bf16[64,2176]{1,0:T(8,128)(2,1)S(1)} collective-permute-done((bf16[64,2176]{1,0:T(8,128)(2,1)S(1)}, bf16[64,2176]{1,0:T(8,128)(2,1)S(1)}, u32[]{:S(2)}, u32[]{:S(2)}) %collective-permute-start.7) | collective-permute-done | bytes 278560 | tf_op jit(solution)/shard_map/ppermute | solution.py:21
  37.3 1.6 %collective-permute-start.16 = (bf16[256,1024]{1,0:T(8,128)(2,1)S(1)}, bf16[256,1024]{1,0:T(8,128)(2,1)S(1)}, u32[]{:S(2)}, u32[]{:S(2)}) collective-permute-start(bf16[256,1024]{1,0:T(8,128)(2,1)S(1)} %shard_map.95), channel_id=1, source_target_pairs={{0,1},{1,0},{2,3},{3,2},{4,5},{5,4},{6,7},{7,6},{8,9},{9,8},{10,11... | collective-permute-start | bytes 1572872 | tf_op jit(solution)/shard_map/ppermute | solution.py:21
  38.9 0.5 collective-permute-start.13
  39.4 0.5 collective-permute-start.15
  39.9 0.5 collective-permute-done.12.refs_12_
  40.4 0.4 collective-permute-done.13.refs_13_
  40.8 0.4 collective-permute-done.14.refs_14_
  41.2 0.4 collective-permute-done.15.refs_15_
  41.6 13.8 %shard_map.96 = (bf16[256,2048]{1,0:T(8,128)(2,1)S(1)}, bf16[256,2048]{1,0:T(8,128)(2,1)S(1)}, bf16[256,2048]{1,0:T(8,128)(2,1)S(1)}, bf16[256,2048]{1,0:T(8,128...) custom-call(s32[1]{0:T(128)} %bitcast.first_ref, ...), custom_call_target="tpu_custom_call" | custom-call | flops 1000000 | bytes 100000 | tf_op jit(solution)/shard_map/pallas_call | solution.py:182
  55.6 0.5 collective-permute-start.17
  56.1 0.5 collective-permute-start.23
  56.5 1.7 %collective-permute-done.18 = bf16[256,2048]{1,0:T(8,128)(2,1)S(1)} collective-permute-done((bf16[256,2048]{1,0:T(8,128)(2,1)S(1)}, bf16[256,2048]{1,0:T(8,128)(2,1)S(1)}, u32[]{:S(2)}, u32[]{:S(2)}) %collective-permute-start.18) | collective-permute-done | bytes 1048608 | tf_op jit(solution)/shard_map/ppermute | solution.py:21
  58.2 0.4 add.34
  58.6 0.1 fusion.8
  58.7 1.0 %collective-permute-done.17 = bf16[256,2048]{1,0:T(8,128)(2,1)S(1)} collective-permute-done((bf16[256,2048]{1,0:T(8,128)(2,1)S(1)}, bf16[256,2048]{1,0:T(8,128)(2,1)S(1)}, u32[]{:S(2)}, u32[]{:S(2)}) %collective-permute-start.17) | collective-permute-done | bytes 1048608 | tf_op jit(solution)/shard_map/ppermute | solution.py:21
  59.7 1.5 %collective-permute-start.21 = (bf16[64,2048]{1,0:T(8,128)(2,1)S(1)}, bf16[64,2048]{1,0:T(8,128)(2,1)S(1)}, u32[]{:S(2)}, u32[]{:S(2)}) collective-permute-start(bf16[64,2048]{1,0:T(8,128)(2,1)S(1)} %get-tuple-element.143), channel_id=1, source_target_pairs={{0,4},{2,6},{4,0},{6,2},{8,12},{10,14},{12,8},{14,10},{16,20},{18,... | collective-permute-start | bytes 786440 | tf_op jit(solution)/shard_map/ppermute | solution.py:21
  61.2 0.4 add.35
  61.8 0.9 collective-permute-start.19
  62.7 0.5 collective-permute-start.24
  63.2 5.7 %collective-permute-done.21 = bf16[64,2048]{1,0:T(8,128)(2,1)S(1)} collective-permute-done((bf16[64,2048]{1,0:T(8,128)(2,1)S(1)}, bf16[64,2048]{1,0:T(8,128)(2,1)S(1)}, u32[]{:S(2)}, u32[]{:S(2)}) %collective-permute-start.21) | collective-permute-done | bytes 262176 | tf_op jit(solution)/shard_map/ppermute | solution.py:21
  68.9 1.0 %collective-permute-start.25 = (bf16[64,2048]{1,0:T(8,128)(2,1)S(1)}, bf16[64,2048]{1,0:T(8,128)(2,1)S(1)}, u32[]{:S(2)}, u32[]{:S(2)}) collective-permute-start(bf16[64,2048]{1,0:T(8,128)(2,1)S(1)} %add.36), channel_id=1, source_target_pairs={{0,8},{2,10},{4,12},{6,14},{8,0},{10,2},{12,4},{14,6},{16,24},{18,... | collective-permute-start | bytes 786440 | tf_op jit(solution)/shard_map/ppermute | solution.py:21
  69.9 0.5 collective-permute-start.27
  70.5 1.5 %collective-permute-start.22 = (bf16[64,2048]{1,0:T(8,128)(2,1)S(1)}, bf16[64,2048]{1,0:T(8,128)(2,1)S(1)}, u32[]{:S(2)}, u32[]{:S(2)}) collective-permute-start(bf16[64,2048]{1,0:T(8,128)(2,1)S(1)} %add.37), channel_id=1, source_target_pairs={{0,4},{2,6},{4,0},{6,2},{8,12},{10,14},{12,8},{14,10},{16,20},{18,... | collective-permute-start | bytes 786440 | tf_op jit(solution)/shard_map/ppermute | solution.py:21
  72.0 2.4 %collective-permute-done.24 = bf16[64,2048]{1,0:T(8,128)(2,1)S(1)} collective-permute-done((bf16[64,2048]{1,0:T(8,128)(2,1)S(1)}, bf16[64,2048]{1,0:T(8,128)(2,1)S(1)}, u32[]{:S(2)}, u32[]{:S(2)}) %collective-permute-start.24) | collective-permute-done | bytes 262176 | tf_op jit(solution)/shard_map/ppermute | solution.py:21
  74.5 1.2 %collective-permute-done.25 = bf16[64,2048]{1,0:T(8,128)(2,1)S(1)} collective-permute-done((bf16[64,2048]{1,0:T(8,128)(2,1)S(1)}, bf16[64,2048]{1,0:T(8,128)(2,1)S(1)}, u32[]{:S(2)}, u32[]{:S(2)}) %collective-permute-start.25) | collective-permute-done | bytes 262176 | tf_op jit(solution)/shard_map/ppermute | solution.py:21
  75.8 2.9 %collective-permute-start.26 = (bf16[64,2048]{1,0:T(8,128)(2,1)S(1)}, bf16[64,2048]{1,0:T(8,128)(2,1)S(1)}, u32[]{:S(2)}, u32[]{:S(2)}) collective-permute-start(bf16[64,2048]{1,0:T(8,128)(2,1)S(1)} %add_add_fusion), channel_id=1, source_target_pairs={{0,16},{2,18},{4,20},{6,22},{8,24},{10,26},{12,28},{14,30},{16,0},... | collective-permute-start | bytes 786440 | tf_op jit(solution)/shard_map/ppermute | solution.py:21
  78.7 1.5 %collective-permute-start.28 = (bf16[64,2048]{1,0:T(8,128)(2,1)S(1)}, bf16[64,2048]{1,0:T(8,128)(2,1)S(1)}, u32[]{:S(2)}, u32[]{:S(2)}) collective-permute-start(bf16[64,2048]{1,0:T(8,128)(2,1)S(1)} %get-tuple-element.134), channel_id=1, source_target_pairs={{0,8},{2,10},{4,12},{6,14},{8,0},{10,2},{12,4},{14,6},{16,24},{18,... | collective-permute-start | bytes 786440 | tf_op jit(solution)/shard_map/ppermute | solution.py:21
  80.2 3.9 %shard_map.97 = f32[1024,1,768]{2,1,0:T(1,128)} custom-call(bf16[256,1024]{1,0:T(8,128)(2,1)S(1)} %get-tuple-element.125.refs_0_, bf16[256,768]{1,0:T(8,128)(2,1)S(1)} %get-tuple-element.119.refs_1_, bf16[256,1024]{1,0:T(8,128)(2,1)S(1)} %get-tuple-element.127.refs_2_, bf16[256,768]{1,0:T(8,128)(2,1)S(1)} %get-tuple-element.128.refs_3_, ...), custom_call_target="tpu_custom_call" | custom-call | flops 1000000 | bytes 100000 | tf_op jit(solution)/shard_map/pallas_call | solution.py:240
  84.1 4.2 %collective-permute-done.26 = bf16[64,2048]{1,0:T(8,128)(2,1)S(1)} collective-permute-done((bf16[64,2048]{1,0:T(8,128)(2,1)S(1)}, bf16[64,2048]{1,0:T(8,128)(2,1)S(1)}, u32[]{:S(2)}, u32[]{:S(2)}) %collective-permute-start.26) | collective-permute-done | bytes 262176 | tf_op jit(solution)/shard_map/ppermute | solution.py:21
  88.5 0.5 collective-permute-done.28
  89.1 1.3 %collective-permute-done.29 = bf16[32,2048]{1,0:T(8,128)(2,1)S(1)} collective-permute-done((bf16[32,2048]{1,0:T(8,128)(2,1)S(1)}, bf16[32,2048]{1,0:T(8,128)(2,1)S(1)}, u32[]{:S(2)}, u32[]{:S(2)}) %collective-permute-start.29) | collective-permute-done | bytes 131104 | tf_op jit(solution)/shard_map/ppermute | solution.py:21
  90.4 0.7 broadcast_select_fusion.2
  (37 shorter events, 1.1 us)
Async XLA Ops:
  1.6 2.3 %collective-permute-start = (bf16[32,2048]{1,0:T(8,128)(2,1)S(1)}, bf16[32,2048]{1,0:T(8,128)(2,1)S(1)}, u32[]{:S(2)}, u32[]{:S(2)}) collective-permute-start(bf16[32,2048]{1,0:T(8,128)(2,1)S(1)} %get-tuple-element.149), channel_id=1, source_target_pairs={{0,2},{2,0},{4,6},{6,4},{8,10},{10,8},{12,14},{14,12},{16,18},{18,... | collective-permute-start | bytes 393224 | tf_op jit(solution)/shard_map/ppermute | solution.py:21
  4.0 17.1 %collective-permute-start.2 = (bf16[64,2176]{1,0:T(8,128)(2,1)S(1)}, bf16[64,2176]{1,0:T(8,128)(2,1)S(1)}, u32[]{:S(2)}, u32[]{:S(2)}) collective-permute-start(bf16[64,2176]{1,0:T(8,128)(2,1)S(1)} %shard_map.94.refs_0_), channel_id=1, source_target_pairs={{0,16},{2,18},{4,20},{6,22},{8,24},{10,26},{12,28},{14,30},{16,0},... | collective-permute-start | bytes 835592 | tf_op jit(solution)/shard_map/ppermute | solution.py:21
  7.7 15.6 %collective-permute-start.1 = (bf16[64,2176]{1,0:T(8,128)(2,1)S(1)}, bf16[64,2176]{1,0:T(8,128)(2,1)S(1)}, u32[]{:S(2)}, u32[]{:S(2)}) collective-permute-start(bf16[64,2176]{1,0:T(8,128)(2,1)S(1)} %shard_map.94.refs_0_), channel_id=1, source_target_pairs={{0,4},{2,6},{4,0},{6,2},{8,12},{10,14},{12,8},{14,10},{16,20},{18,... | collective-permute-start | bytes 835592 | tf_op jit(solution)/shard_map/ppermute | solution.py:21
  9.2 15.5 %collective-permute-start.5 = (bf16[64,2176]{1,0:T(8,128)(2,1)S(1)}, bf16[64,2176]{1,0:T(8,128)(2,1)S(1)}, u32[]{:S(2)}, u32[]{:S(2)}) collective-permute-start(bf16[64,2176]{1,0:T(8,128)(2,1)S(1)} %shard_map.94.refs_0_), channel_id=1, source_target_pairs={{0,8},{2,10},{4,12},{6,14},{8,0},{10,2},{12,4},{14,6},{16,24},{18,... | collective-permute-start | bytes 835592 | tf_op jit(solution)/shard_map/ppermute | solution.py:21
  21.1 9.5 %collective-permute-start.4 = (bf16[64,2176]{1,0:T(8,128)(2,1)S(1)}, bf16[64,2176]{1,0:T(8,128)(2,1)S(1)}, u32[]{:S(2)}, u32[]{:S(2)}) collective-permute-start(bf16[64,2176]{1,0:T(8,128)(2,1)S(1)} %collective-permute-done.2.refs_2_), channel_id=1, source_target_pairs={{0,8},{2,10},{4,12},{6,14},{8,0},{10,2},{12,4},{14,6},{16,24},{18,... | collective-permute-start | bytes 835592 | tf_op jit(solution)/shard_map/ppermute | solution.py:21
  21.8 10.5 %collective-permute-start.3 = (bf16[64,2176]{1,0:T(8,128)(2,1)S(1)}, bf16[64,2176]{1,0:T(8,128)(2,1)S(1)}, u32[]{:S(2)}, u32[]{:S(2)}) collective-permute-start(bf16[64,2176]{1,0:T(8,128)(2,1)S(1)} %collective-permute-done.2.refs_2_), channel_id=1, source_target_pairs={{0,4},{2,6},{4,0},{6,2},{8,12},{10,14},{12,8},{14,10},{16,20},{18,... | collective-permute-start | bytes 835592 | tf_op jit(solution)/shard_map/ppermute | solution.py:21
  23.2 12.2 %collective-permute-start.6 = (bf16[64,2176]{1,0:T(8,128)(2,1)S(1)}, bf16[64,2176]{1,0:T(8,128)(2,1)S(1)}, u32[]{:S(2)}, u32[]{:S(2)}) collective-permute-start(bf16[64,2176]{1,0:T(8,128)(2,1)S(1)} %collective-permute-done.1.refs_1_), channel_id=1, source_target_pairs={{0,8},{2,10},{4,12},{6,14},{8,0},{10,2},{12,4},{14,6},{16,24},{18,... | collective-permute-start | bytes 835592 | tf_op jit(solution)/shard_map/ppermute | solution.py:21
  24.7 12.5 %collective-permute-start.8 = (bf16[64,2176]{1,0:T(8,128)(2,1)S(1)}, bf16[64,2176]{1,0:T(8,128)(2,1)S(1)}, u32[]{:S(2)}, u32[]{:S(2)}) collective-permute-start(bf16[64,2176]{1,0:T(8,128)(2,1)S(1)} %shard_map.94.refs_0_), channel_id=1, source_target_pairs={{0,2},{2,0},{4,6},{6,4},{8,10},{10,8},{12,14},{14,12},{16,18},{18,... | collective-permute-start | bytes 835592 | tf_op jit(solution)/shard_map/ppermute | solution.py:21
  24.7 12.5 %collective-permute-start.10 = (bf16[64,2176]{1,0:T(8,128)(2,1)S(1)}, bf16[64,2176]{1,0:T(8,128)(2,1)S(1)}, u32[]{:S(2)}, u32[]{:S(2)}) collective-permute-start(bf16[64,2176]{1,0:T(8,128)(2,1)S(1)} %collective-permute-done.2.refs_2_), channel_id=1, source_target_pairs={{0,2},{2,0},{4,6},{6,4},{8,10},{10,8},{12,14},{14,12},{16,18},{18,... | collective-permute-start | bytes 835592 | tf_op jit(solution)/shard_map/ppermute | solution.py:21
  30.6 6.5 %collective-permute-start.7 = (bf16[64,2176]{1,0:T(8,128)(2,1)S(1)}, bf16[64,2176]{1,0:T(8,128)(2,1)S(1)}, u32[]{:S(2)}, u32[]{:S(2)}) collective-permute-start(bf16[64,2176]{1,0:T(8,128)(2,1)S(1)} %collective-permute-done.4.refs_6_), channel_id=1, source_target_pairs={{0,4},{2,6},{4,0},{6,2},{8,12},{10,14},{12,8},{14,10},{16,20},{18,... | collective-permute-start | bytes 835592 | tf_op jit(solution)/shard_map/ppermute | solution.py:21
  32.2 5.0 %collective-permute-start.9 = (bf16[64,2176]{1,0:T(8,128)(2,1)S(1)}, bf16[64,2176]{1,0:T(8,128)(2,1)S(1)}, u32[]{:S(2)}, u32[]{:S(2)}) collective-permute-start(bf16[64,2176]{1,0:T(8,128)(2,1)S(1)} %collective-permute-done.1.refs_1_), channel_id=1, source_target_pairs={{0,2},{2,0},{4,6},{6,4},{8,10},{10,8},{12,14},{14,12},{16,18},{18,... | collective-permute-start | bytes 835592 | tf_op jit(solution)/shard_map/ppermute | solution.py:21
  35.5 1.7 %collective-permute-start.11 = (bf16[64,2176]{1,0:T(8,128)(2,1)S(1)}, bf16[64,2176]{1,0:T(8,128)(2,1)S(1)}, u32[]{:S(2)}, u32[]{:S(2)}) collective-permute-start(bf16[64,2176]{1,0:T(8,128)(2,1)S(1)} %collective-permute-done.3.refs_3_), channel_id=1, source_target_pairs={{0,2},{2,0},{4,6},{6,4},{8,10},{10,8},{12,14},{14,12},{16,18},{18,... | collective-permute-start | bytes 835592 | tf_op jit(solution)/shard_map/ppermute | solution.py:21
  37.3 18.2 %collective-permute-start.16 = (bf16[256,1024]{1,0:T(8,128)(2,1)S(1)}, bf16[256,1024]{1,0:T(8,128)(2,1)S(1)}, u32[]{:S(2)}, u32[]{:S(2)}) collective-permute-start(bf16[256,1024]{1,0:T(8,128)(2,1)S(1)} %shard_map.95), channel_id=1, source_target_pairs={{0,1},{1,0},{2,3},{3,2},{4,5},{5,4},{6,7},{7,6},{8,9},{9,8},{10,11... | collective-permute-start | bytes 1572872 | tf_op jit(solution)/shard_map/ppermute | solution.py:21
  38.9 1.6 %collective-permute-start.12 = (bf16[64,2176]{1,0:T(8,128)(2,1)S(1)}, bf16[64,2176]{1,0:T(8,128)(2,1)S(1)}, u32[]{:S(2)}, u32[]{:S(2)}) collective-permute-start(bf16[64,2176]{1,0:T(8,128)(2,1)S(1)} %collective-permute-done.5.refs_4_), channel_id=1, source_target_pairs={{0,2},{2,0},{4,6},{6,4},{8,10},{10,8},{12,14},{14,12},{16,18},{18,... | collective-permute-start | bytes 835592 | tf_op jit(solution)/shard_map/ppermute | solution.py:21
  38.9 2.0 %collective-permute-start.13 = (bf16[64,2176]{1,0:T(8,128)(2,1)S(1)}, bf16[64,2176]{1,0:T(8,128)(2,1)S(1)}, u32[]{:S(2)}, u32[]{:S(2)}) collective-permute-start(bf16[64,2176]{1,0:T(8,128)(2,1)S(1)} %collective-permute-done.6.refs_5_), channel_id=1, source_target_pairs={{0,2},{2,0},{4,6},{6,4},{8,10},{10,8},{12,14},{14,12},{16,18},{18,... | collective-permute-start | bytes 835592 | tf_op jit(solution)/shard_map/ppermute | solution.py:21
  39.4 1.8 %collective-permute-start.14 = (bf16[64,2176]{1,0:T(8,128)(2,1)S(1)}, bf16[64,2176]{1,0:T(8,128)(2,1)S(1)}, u32[]{:S(2)}, u32[]{:S(2)}) collective-permute-start(bf16[64,2176]{1,0:T(8,128)(2,1)S(1)} %collective-permute-done.4.refs_6_), channel_id=1, source_target_pairs={{0,2},{2,0},{4,6},{6,4},{8,10},{10,8},{12,14},{14,12},{16,18},{18,... | collective-permute-start | bytes 835592 | tf_op jit(solution)/shard_map/ppermute | solution.py:21
  39.4 2.2 %collective-permute-start.15 = (bf16[64,2176]{1,0:T(8,128)(2,1)S(1)}, bf16[64,2176]{1,0:T(8,128)(2,1)S(1)}, u32[]{:S(2)}, u32[]{:S(2)}) collective-permute-start(bf16[64,2176]{1,0:T(8,128)(2,1)S(1)} %collective-permute-done.7.refs_7_), channel_id=1, source_target_pairs={{0,2},{2,0},{4,6},{6,4},{8,10},{10,8},{12,14},{14,12},{16,18},{18,... | collective-permute-start | bytes 835592 | tf_op jit(solution)/shard_map/ppermute | solution.py:21
  55.5 2.7 %collective-permute-start.18 = (bf16[256,2048]{1,0:T(8,128)(2,1)S(1)}, bf16[256,2048]{1,0:T(8,128)(2,1)S(1)}, u32[]{:S(2)}, u32[]{:S(2)}) collective-permute-start(bf16[256,2048]{1,0:T(8,128)(2,1)S(1)} %get-tuple-element.109), channel_id=1, source_target_pairs={{0,2},{2,0},{4,6},{6,4},{8,10},{10,8},{12,14},{14,12},{16,18},{18,... | collective-permute-start | bytes 3145736 | tf_op jit(solution)/shard_map/ppermute | solution.py:21
  55.6 4.1 %collective-permute-start.17 = (bf16[256,2048]{1,0:T(8,128)(2,1)S(1)}, bf16[256,2048]{1,0:T(8,128)(2,1)S(1)}, u32[]{:S(2)}, u32[]{:S(2)}) collective-permute-start(bf16[256,2048]{1,0:T(8,128)(2,1)S(1)} %get-tuple-element.107), channel_id=1, source_target_pairs={{0,2},{2,0},{4,6},{6,4},{8,10},{10,8},{12,14},{14,12},{16,18},{18,... | collective-permute-start | bytes 3145736 | tf_op jit(solution)/shard_map/ppermute | solution.py:21
  56.1 14.4 %collective-permute-start.23 = (bf16[256,768]{1,0:T(8,128)(2,1)S(1)}, bf16[256,768]{1,0:T(8,128)(2,1)S(1)}, u32[]{:S(2)}, u32[]{:S(2)}) collective-permute-start(bf16[256,768]{1,0:T(8,128)(2,1)S(1)} %get-tuple-element.119.refs_1_), channel_id=1, source_target_pairs={{0,1},{1,0},{2,3},{3,2},{4,5},{5,4},{6,7},{7,6},{8,9},{9,8},{10,11... | collective-permute-start | bytes 1179656 | tf_op jit(solution)/shard_map/ppermute | solution.py:21
  56.5 5.2 %collective-permute-start.20 = (bf16[256,1024]{1,0:T(8,128)(2,1)S(1)}, bf16[256,1024]{1,0:T(8,128)(2,1)S(1)}, u32[]{:S(2)}, u32[]{:S(2)}) collective-permute-start(bf16[256,1024]{1,0:T(8,128)(2,1)S(1)} %collective-permute-done.16), channel_id=1, source_target_pairs={{0,2},{2,0},{4,6},{6,4},{8,10},{10,8},{12,14},{14,12},{16,18},{18,... | collective-permute-start | bytes 1572872 | tf_op jit(solution)/shard_map/ppermute | solution.py:21
  59.7 9.1 %collective-permute-start.21 = (bf16[64,2048]{1,0:T(8,128)(2,1)S(1)}, bf16[64,2048]{1,0:T(8,128)(2,1)S(1)}, u32[]{:S(2)}, u32[]{:S(2)}) collective-permute-start(bf16[64,2048]{1,0:T(8,128)(2,1)S(1)} %get-tuple-element.143), channel_id=1, source_target_pairs={{0,4},{2,6},{4,0},{6,2},{8,12},{10,14},{12,8},{14,10},{16,20},{18,... | collective-permute-start | bytes 786440 | tf_op jit(solution)/shard_map/ppermute | solution.py:21
  61.8 8.7 %collective-permute-start.19 = (bf16[64,2048]{1,0:T(8,128)(2,1)S(1)}, bf16[64,2048]{1,0:T(8,128)(2,1)S(1)}, u32[]{:S(2)}, u32[]{:S(2)}) collective-permute-start(bf16[64,2048]{1,0:T(8,128)(2,1)S(1)} %get-tuple-element.145), channel_id=1, source_target_pairs={{0,8},{2,10},{4,12},{6,14},{8,0},{10,2},{12,4},{14,6},{16,24},{18,... | collective-permute-start | bytes 786440 | tf_op jit(solution)/shard_map/ppermute | solution.py:21
  62.7 11.8 %collective-permute-start.24 = (bf16[64,2048]{1,0:T(8,128)(2,1)S(1)}, bf16[64,2048]{1,0:T(8,128)(2,1)S(1)}, u32[]{:S(2)}, u32[]{:S(2)}) collective-permute-start(bf16[64,2048]{1,0:T(8,128)(2,1)S(1)} %get-tuple-element.139), channel_id=1, source_target_pairs={{0,4},{2,6},{4,0},{6,2},{8,12},{10,14},{12,8},{14,10},{16,20},{18,... | collective-permute-start | bytes 786440 | tf_op jit(solution)/shard_map/ppermute | solution.py:21
  68.9 6.8 %collective-permute-start.25 = (bf16[64,2048]{1,0:T(8,128)(2,1)S(1)}, bf16[64,2048]{1,0:T(8,128)(2,1)S(1)}, u32[]{:S(2)}, u32[]{:S(2)}) collective-permute-start(bf16[64,2048]{1,0:T(8,128)(2,1)S(1)} %add.36), channel_id=1, source_target_pairs={{0,8},{2,10},{4,12},{6,14},{8,0},{10,2},{12,4},{14,6},{16,24},{18,... | collective-permute-start | bytes 786440 | tf_op jit(solution)/shard_map/ppermute | solution.py:21
  69.9 10.3 %collective-permute-start.27 = (bf16[256,768]{1,0:T(8,128)(2,1)S(1)}, bf16[256,768]{1,0:T(8,128)(2,1)S(1)}, u32[]{:S(2)}, u32[]{:S(2)}) collective-permute-start(bf16[256,768]{1,0:T(8,128)(2,1)S(1)} %get-tuple-element.128.refs_3_), channel_id=1, source_target_pairs={{0,1},{1,0},{2,3},{3,2},{4,5},{5,4},{6,7},{7,6},{8,9},{9,8},{10,11... | collective-permute-start | bytes 1179656 | tf_op jit(solution)/shard_map/ppermute | solution.py:21
  70.5 13.6 %collective-permute-start.22 = (bf16[64,2048]{1,0:T(8,128)(2,1)S(1)}, bf16[64,2048]{1,0:T(8,128)(2,1)S(1)}, u32[]{:S(2)}, u32[]{:S(2)}) collective-permute-start(bf16[64,2048]{1,0:T(8,128)(2,1)S(1)} %add.37), channel_id=1, source_target_pairs={{0,4},{2,6},{4,0},{6,2},{8,12},{10,14},{12,8},{14,10},{16,20},{18,... | collective-permute-start | bytes 786440 | tf_op jit(solution)/shard_map/ppermute | solution.py:21
  75.8 12.6 %collective-permute-start.26 = (bf16[64,2048]{1,0:T(8,128)(2,1)S(1)}, bf16[64,2048]{1,0:T(8,128)(2,1)S(1)}, u32[]{:S(2)}, u32[]{:S(2)}) collective-permute-start(bf16[64,2048]{1,0:T(8,128)(2,1)S(1)} %add_add_fusion), channel_id=1, source_target_pairs={{0,16},{2,18},{4,20},{6,22},{8,24},{10,26},{12,28},{14,30},{16,0},... | collective-permute-start | bytes 786440 | tf_op jit(solution)/shard_map/ppermute | solution.py:21
  78.7 10.2 %collective-permute-start.28 = (bf16[64,2048]{1,0:T(8,128)(2,1)S(1)}, bf16[64,2048]{1,0:T(8,128)(2,1)S(1)}, u32[]{:S(2)}, u32[]{:S(2)}) collective-permute-start(bf16[64,2048]{1,0:T(8,128)(2,1)S(1)} %get-tuple-element.134), channel_id=1, source_target_pairs={{0,8},{2,10},{4,12},{6,14},{8,0},{10,2},{12,4},{14,6},{16,24},{18,... | collective-permute-start | bytes 786440 | tf_op jit(solution)/shard_map/ppermute | solution.py:21
  89.0 1.4 %collective-permute-start.29 = (bf16[32,2048]{1,0:T(8,128)(2,1)S(1)}, bf16[32,2048]{1,0:T(8,128)(2,1)S(1)}, u32[]{:S(2)}, u32[]{:S(2)}) collective-permute-start(bf16[32,2048]{1,0:T(8,128)(2,1)S(1)} %broadcast_select_fusion.4), channel_id=1, source_target_pairs={{0,2},{2,0},{4,6},{6,4},{8,10},{10,8},{12,14},{14,12},{16,18},{18,... | collective-permute-start | bytes 393224 | tf_op jit(solution)/shard_map/ppermute | solution.py:21

commit v5 on v4

--- a/solution.py
+++ b/solution.py
@@ -104,10 +104,15 @@
 
 def piece_kernel(n_expert, n_edata, count, first_ref, expert_ref, place_ref, *refs):
     mine, theirs, (gate_hbm, up_hbm, down_hbm) = refs[:count], refs[count : 2 * count], refs[2 * count : 2 * count + 3]
-    kept_refs, sent_refs, scaled_refs, share_refs = (refs[2 * count + 3 + 2 * i : 2 * count + 5 + 2 * i] for i in range(4))
+    outs = refs[2 * count + 3 : -12]
+    kept_refs, sent_refs, scaled_refs, share_refs = outs[:4], outs[4:8], outs[8:10], outs[10:]
     rows_ref, grads_ref, lanes_ref, hidden_ref, act_ref, slope_ref, grad_gate_ref, grad_up_ref, gate_ref, up_ref, down_ref, sems = refs[-12:]
     width, units = gate_ref.shape
     half = rows_ref.shape[0] // 2
+    ranges, at = [], 0
+    for ref in kept_refs:
+        ranges.append(slice(at, at + ref.shape[0]))
+        at += ref.shape[0]
     pairs = []
     for at in range(0, units, TILE):
         columns = pl.ds(at, TILE)
@@ -117,7 +122,7 @@
 
     def body(sources, targets):
         out_refs, grad_refs = targets
-        stream = Stream(pairs, sems, 6)
+        stream = Stream(pairs, sems, 10)
         at = 0
         for token, grad in zip(*sources):
             block = slice(at, at + token.shape[0])
@@ -154,8 +159,8 @@
             columns = slice(at, at + OUT_TILE)
             stream.wait(1)
             out = (dot(hidden_ref[...], down_ref[:, columns], ((1,), (0,))) * gate).astype(BF16)
-            out_refs[0][:, columns] = out[:half]
-            out_refs[1][:, columns] = out[half:]
+            for ref, block in zip(out_refs, ranges):
+                ref[:, columns] = out[block]
         for at in range(0, units, TILE):
             columns = slice(at, at + TILE)
             grad_hidden = dot(grads_ref[...], down_ref[columns, :], ((1,), (1,)))
@@ -165,8 +170,8 @@
             columns = slice(at, at + OUT_TILE)
             grad = dot(grad_gate_ref[...], gate_ref[columns, :], ((1,), (1,)))
             grad = (grad + dot(grad_up_ref[...], up_ref[columns, :], ((1,), (1,)))).astype(BF16)
-            grad_refs[0][:, columns] = grad[:half]
-            grad_refs[1][:, columns] = grad[half:]
+            for ref, block in zip(grad_refs, ranges):
+                ref[:, columns] = grad[block]
 
     pl.when(first_ref[0] == 1)(lambda: body((mine, theirs), (kept_refs, sent_refs)))
     pl.when(first_ref[0] == 0)(lambda: body((theirs, mine), (sent_refs, kept_refs)))
@@ -176,7 +181,9 @@
     width, units = mats[0].shape[1:]
     rows = sum(part.shape[0] for part in mine)
     vmem, smem, hbm = (pl.BlockSpec(memory_space=space) for space in (pltpu.VMEM, pltpu.SMEM, pltpu.HBM))
-    outs = [(rows // 2, size) for size in (width, width, units, width // n_edata) for _ in range(2)]
+    first_two = 2 * mine[0].shape[0]
+    parts = [(first_two, width), (rows // 2 - first_two, width)] * 2
+    outs = parts * 2 + [(rows // 2, size) for size in (units, width // n_edata) for _ in range(2)]
     scratch = [((rows, width), BF16)] * 2 + [((rows, LANES), F32), ((rows, units), BF16)] + [((rows, units), F32)] * 2
     scratch += [((rows, units), BF16)] * 2 + [((width, units), BF16)] * 2 + [((units, width), BF16)]
     return pl.pallas_call(
@@ -290,32 +297,35 @@
 
     cuts_out = order(lambda *a: cut_shares(n_edata, flags[0], flags[2], a[: len(pieces_1)], a[len(pieces_1) :]), *got_1, *pieces_2)
     mine = [swap(part, "edata", step) for step, part in enumerate(cuts_out, 1)]
-    kept_1, kept_2, sent_1, sent_2, scaled_1, scaled_2, share_1, share_2 = order(run, *pieces_1, *pieces_2, *got_1, *got_2)
+    *sums_of, scaled_1, scaled_2, share_1, share_2 = order(run, *pieces_1, *pieces_2, *got_1, *got_2)
     scaled_other_1, scaled_other_2 = ([swap(scaled, "edata", step) for step in range(1, n_edata)] for scaled in (scaled_1, scaled_2))
-    sums = lambda kept, got: cuts(kept + got, 2 + 2 * n_first)
-    sent_1, sent_2 = after_all([sent_1, sent_2], *mine)
-    got_2, got_1 = core(sent_2), core(sent_1)
-    near_own, near_beside, *parts_2 = order(sums, kept_2, got_2)
+    kept, sent = sums_of[:4], after_all(sums_of[4:], *mine)
+    got_last, got_near = core(sent[3]), core(sent[2])
+    sums = lambda kept, got: cuts(kept + got, kept.shape[0] // size)
+    parts_2 = order(sums, kept[3], got_last)
+    got_first, got_own = (core(part) for part in after_all([sent[1], sent[0]], *parts_2))
     crossed_2 = [across(part) for part in parts_2[n_first:]]
+    near_own, near_beside = order(sums, kept[2], got_near)
     back_beside = swap(near_beside, "expert", 4)
-    own, beside, *parts_1 = order(sums, kept_1, got_1)
+    parts_1 = order(sums, kept[1], got_first)
     crossed_1 = [across(part) for part in parts_1[n_first:]]
+    own, beside = order(sums, kept[0], got_own)
     theirs = [core(part) for part in mine]
     ready_2 = order(add, *after_all(parts_2[:n_first], *theirs), *crossed_2)
     back_2 = [swap(part, "expert", 4) for part in ready_2]
     ready = order(lambda part, got: part + got, beside, back_beside)
-    back_pair = across(ready)
     add_three = lambda *a: tuple(a[i] + a[n_first + i] + a[2 * n_first + i] for i in range(n_first))
     ready_1 = order(add_three, *after_all(parts_1[:n_first], *scaled_other_1), *crossed_1, *back_2)
     back_1 = [swap(part, "expert", step) for part, step in zip(ready_1, firsts)]
+    back_pair = across(after(ready, *ready_1))
     back_own = swap(after(near_own, *ready_1), "expert", 4)
     groups = [([share_1], scaled_1), ([share_2], scaled_2)]
     for here, there, hidden_1, hidden_2 in zip(mine, theirs, scaled_other_1, scaled_other_2):
         groups += [([pick(here, there)], hidden_1), ([pick(there, here)], hidden_2)]
     grad_down = weight_share([(after_all(grads, *ready_1), hidden) for grads, hidden in groups])
     order.last = grad_down
-    total = order(total_of, own, back_pair, *back_1)
-    total = order(lambda *parts: total_of(*parts).astype(BF16), total, back_own)
+    total = order(total_of, own, back_own)
+    total = order(lambda *parts: total_of(*parts).astype(BF16), total, back_pair, *back_1)
     kept, sent = pick(total[:rows], total[rows:]), pick(total[rows:], total[:rows])
     got = core(sent)
     return pick(kept, got), pick(got, kept), grad_down

time: 91.4 us -> 90.2 us (0.987)
  waiting for transfers between devices: 40.5 us -> 37 us
  starting transfers between devices: 27.1 us -> 29.2 us
    ppermute x30 -> x32, waiting for transfers between devices: 40.5 us -> 37 us  [swap(): return lax.ppermute(value, axis, [(i, i ^ distance) for i in range(size)])]
    ppermute x30 -> x32, starting transfers between devices: 27.1 us -> 29.2 us  [swap(): return lax.ppermute(value, axis, [(i, i ^ distance) for i in range(size)])]
  transfers between devices with their start and end apart: 30 -> 32, of which waited for: 16 -> 15; matrix products, arithmetic and copies ran while one was open for 3% -> 3% of each run, Pallas kernels for 19% -> 20%
where the time goes in v5:
time: 90.2 us; the launch traced here: 89.5 us
  waiting for transfers between devices  37 us (41%)
  starting transfers between devices  29.2 us (32%)
  Pallas kernels  17.8 us (20%)
  other arithmetic  4.15 us (5%)
    ppermute x32, waiting for transfers between devices, swap(): return lax.ppermute(value, axis, [(i, i ^ distance) for i in range(size)])  37 us
    ppermute x32, starting transfers between devices, swap(): return lax.ppermute(value, axis, [(i, i ^ distance) for i in range(size)])  29.2 us
    pallas_call x1, Pallas kernels, piece(): pl.pallas_call(functools.partial(piece_kernel, n_expert, n_edata, len(min...  13.8 us
    pallas_call x1, Pallas kernels, weight_share(): pl.pallas_call(functools.partial(share_kernel, [len(grads) for grads, _ i...  3.93 us
  transfers between devices with their start and end apart: 32, of which 15 were waited for; matrix products, arithmetic and copies ran while one was open for 3% of the time, Pallas kernels for 20%

profile of v5, /device:TPU:0, one launch (start us, length us, event | category | flops | bytes accessed | tf_op | source)
XLA Modules:
  0.0 89.5 jit_solution(6830363823968782419)
XLA Ops:
  0.6 1.0 %broadcast_select_fusion.6 = (bf16[32,2048]{1,0:T(8,128)(2,1)S(1)}, bf16[32,2048]{1,0:T(8,128)(2,1)S(1)}) fusion(bf16[32,2048]{1,0:T(8,128)(2,1)} %param.8, bf16[32,2048]{1,0:T(8,128)(2,1)} %param.7, pred[]{:T(512)S(6)} %eq.18), kind=kLoop, calls=%fused_computation.9 | loop fusion | flops 131072 | bytes 524289 | tf_op jit(solution)/shard_map/jit(_where)/select_n | solution.py:265
  1.6 0.5 collective-permute-start
  2.2 0.7 reduce_sum.19
  2.9 0.7 select_reduce_fusion
  4.0 3.7 %collective-permute-start.2 = (bf16[64,2176]{1,0:T(8,128)(2,1)S(1)}, bf16[64,2176]{1,0:T(8,128)(2,1)S(1)}, u32[]{:S(2)}, u32[]{:S(2)}) collective-permute-start(bf16[64,2176]{1,0:T(8,128)(2,1)S(1)} %shard_map.94.refs_0_), channel_id=1, source_target_pairs={{0,16},{2,18},{4,20},{6,22},{8,24},{10,26},{12,28},{14,30},{16,0},... | collective-permute-start | bytes 835592 | tf_op jit(solution)/shard_map/ppermute | solution.py:21
  7.7 1.5 %collective-permute-start.1 = (bf16[64,2176]{1,0:T(8,128)(2,1)S(1)}, bf16[64,2176]{1,0:T(8,128)(2,1)S(1)}, u32[]{:S(2)}, u32[]{:S(2)}) collective-permute-start(bf16[64,2176]{1,0:T(8,128)(2,1)S(1)} %shard_map.94.refs_0_), channel_id=1, source_target_pairs={{0,4},{2,6},{4,0},{6,2},{8,12},{10,14},{12,8},{14,10},{16,20},{18,... | collective-permute-start | bytes 835592 | tf_op jit(solution)/shard_map/ppermute | solution.py:21
  9.2 1.6 %collective-permute-start.5 = (bf16[64,2176]{1,0:T(8,128)(2,1)S(1)}, bf16[64,2176]{1,0:T(8,128)(2,1)S(1)}, u32[]{:S(2)}, u32[]{:S(2)}) collective-permute-start(bf16[64,2176]{1,0:T(8,128)(2,1)S(1)} %shard_map.94.refs_0_), channel_id=1, source_target_pairs={{0,8},{2,10},{4,12},{6,14},{8,0},{10,2},{12,4},{14,6},{16,24},{18,... | collective-permute-start | bytes 835592 | tf_op jit(solution)/shard_map/ppermute | solution.py:21
  10.8 10.3 %collective-permute-done.2.refs_2_ = bf16[64,2176]{1,0:T(8,128)(2,1)S(1)} collective-permute-done((bf16[64,2176]{1,0:T(8,128)(2,1)S(1)}, bf16[64,2176]{1,0:T(8,128)(2,1)S(1)}, u32[]{:S(2)}, u32[]{:S(2)}) %collective-permute-start.2) | collective-permute-done | bytes 278560 | tf_op jit(solution)/shard_map/ppermute | solution.py:21
  21.1 0.7 collective-permute-start.4
  21.8 1.5 %collective-permute-start.3 = (bf16[64,2176]{1,0:T(8,128)(2,1)S(1)}, bf16[64,2176]{1,0:T(8,128)(2,1)S(1)}, u32[]{:S(2)}, u32[]{:S(2)}) collective-permute-start(bf16[64,2176]{1,0:T(8,128)(2,1)S(1)} %collective-permute-done.2.refs_2_), channel_id=1, source_target_pairs={{0,4},{2,6},{4,0},{6,2},{8,12},{10,14},{12,8},{14,10},{16,20},{18,... | collective-permute-start | bytes 835592 | tf_op jit(solution)/shard_map/ppermute | solution.py:21
  23.2 1.4 %collective-permute-start.6 = (bf16[64,2176]{1,0:T(8,128)(2,1)S(1)}, bf16[64,2176]{1,0:T(8,128)(2,1)S(1)}, u32[]{:S(2)}, u32[]{:S(2)}) collective-permute-start(bf16[64,2176]{1,0:T(8,128)(2,1)S(1)} %collective-permute-done.1.refs_1_), channel_id=1, source_target_pairs={{0,8},{2,10},{4,12},{6,14},{8,0},{10,2},{12,4},{14,6},{16,24},{18,... | collective-permute-start | bytes 835592 | tf_op jit(solution)/shard_map/ppermute | solution.py:21
  24.7 0.5 collective-permute-start.10
  25.2 5.4 %collective-permute-done.4.refs_6_ = bf16[64,2176]{1,0:T(8,128)(2,1)S(1)} collective-permute-done((bf16[64,2176]{1,0:T(8,128)(2,1)S(1)}, bf16[64,2176]{1,0:T(8,128)(2,1)S(1)}, u32[]{:S(2)}, u32[]{:S(2)}) %collective-permute-start.4) | collective-permute-done | bytes 278560 | tf_op jit(solution)/shard_map/ppermute | solution.py:21
  30.6 1.6 %collective-permute-start.7 = (bf16[64,2176]{1,0:T(8,128)(2,1)S(1)}, bf16[64,2176]{1,0:T(8,128)(2,1)S(1)}, u32[]{:S(2)}, u32[]{:S(2)}) collective-permute-start(bf16[64,2176]{1,0:T(8,128)(2,1)S(1)} %collective-permute-done.4.refs_6_), channel_id=1, source_target_pairs={{0,4},{2,6},{4,0},{6,2},{8,12},{10,14},{12,8},{14,10},{16,20},{18,... | collective-permute-start | bytes 835592 | tf_op jit(solution)/shard_map/ppermute | solution.py:21
  32.2 3.2 %collective-permute-done.6.refs_5_ = bf16[64,2176]{1,0:T(8,128)(2,1)S(1)} collective-permute-done((bf16[64,2176]{1,0:T(8,128)(2,1)S(1)}, bf16[64,2176]{1,0:T(8,128)(2,1)S(1)}, u32[]{:S(2)}, u32[]{:S(2)}) %collective-permute-start.6) | collective-permute-done | bytes 278560 | tf_op jit(solution)/shard_map/ppermute | solution.py:21
  35.5 1.7 %collective-permute-done.7.refs_7_ = bf16[64,2176]{1,0:T(8,128)(2,1)S(1)} collective-permute-done((bf16[64,2176]{1,0:T(8,128)(2,1)S(1)}, bf16[64,2176]{1,0:T(8,128)(2,1)S(1)}, u32[]{:S(2)}, u32[]{:S(2)}) %collective-permute-start.7) | collective-permute-done | bytes 278560 | tf_op jit(solution)/shard_map/ppermute | solution.py:21
  37.3 1.6 %collective-permute-start.16 = (bf16[256,1024]{1,0:T(8,128)(2,1)S(1)}, bf16[256,1024]{1,0:T(8,128)(2,1)S(1)}, u32[]{:S(2)}, u32[]{:S(2)}) collective-permute-start(bf16[256,1024]{1,0:T(8,128)(2,1)S(1)} %shard_map.95), channel_id=1, source_target_pairs={{0,1},{1,0},{2,3},{3,2},{4,5},{5,4},{6,7},{7,6},{8,9},{9,8},{10,11... | collective-permute-start | bytes 1572872 | tf_op jit(solution)/shard_map/ppermute | solution.py:21
  38.9 0.5 collective-permute-start.13
  39.4 0.5 collective-permute-start.15
  39.9 0.5 collective-permute-done.12.refs_12_
  40.4 0.4 collective-permute-done.13.refs_13_
  40.8 0.4 collective-permute-done.14.refs_14_
  41.2 0.4 collective-permute-done.15.refs_15_
  41.6 13.8 %shard_map.96 = (bf16[128,2048]{1,0:T(8,128)(2,1)S(1)}, bf16[128,2048]{1,0:T(8,128)(2,1)S(1)}, bf16[128,2048]{1,0:T(8,128)(2,1)S(1)}, bf16[128,2048]{1,0:T(8,128...) custom-call(s32[1]{0:T(128)} %bitcast.first_ref, ...), custom_call_target="tpu_custom_call" | custom-call | flops 1000000 | bytes 100000 | tf_op jit(solution)/shard_map/pallas_call | solution.py:189
  55.6 0.5 collective-permute-start.20
  56.1 1.3 %collective-permute-done.17 = bf16[128,2048]{1,0:T(8,128)(2,1)S(1)} collective-permute-done((bf16[128,2048]{1,0:T(8,128)(2,1)S(1)}, bf16[128,2048]{1,0:T(8,128)(2,1)S(1)}, u32[]{:S(2)}, u32[]{:S(2)}) %collective-permute-start.17) | collective-permute-done | bytes 524320 | tf_op jit(solution)/shard_map/ppermute | solution.py:21
  57.5 0.1 add.40
  57.7 0.2 collective-permute-start.19
  57.9 0.5 collective-permute-start.21
  58.3 1.6 %collective-permute-start.24 = (bf16[64,2048]{1,0:T(8,128)(2,1)S(1)}, bf16[64,2048]{1,0:T(8,128)(2,1)S(1)}, u32[]{:S(2)}, u32[]{:S(2)}) collective-permute-start(bf16[64,2048]{1,0:T(8,128)(2,1)S(1)} %get-tuple-element.171), channel_id=1, source_target_pairs={{0,4},{2,6},{4,0},{6,2},{8,12},{10,14},{12,8},{14,10},{16,20},{18,... | collective-permute-start | bytes 786440 | tf_op jit(solution)/shard_map/ppermute | solution.py:21
  59.9 0.1 add.41
  60.1 0.9 %collective-permute-start.26 = (bf16[64,2048]{1,0:T(8,128)(2,1)S(1)}, bf16[64,2048]{1,0:T(8,128)(2,1)S(1)}, u32[]{:S(2)}, u32[]{:S(2)}) collective-permute-start(bf16[64,2048]{1,0:T(8,128)(2,1)S(1)} %get-tuple-element.165), channel_id=1, source_target_pairs={{0,8},{2,10},{4,12},{6,14},{8,0},{10,2},{12,4},{14,6},{16,24},{18,... | collective-permute-start | bytes 786440 | tf_op jit(solution)/shard_map/ppermute | solution.py:21
  61.0 0.1 add.42
  61.2 0.6 collective-permute-done.18
  61.9 0.1 add.43
  62.0 4.6 %collective-permute-done.24 = bf16[64,2048]{1,0:T(8,128)(2,1)S(1)} collective-permute-done((bf16[64,2048]{1,0:T(8,128)(2,1)S(1)}, bf16[64,2048]{1,0:T(8,128)(2,1)S(1)}, u32[]{:S(2)}, u32[]{:S(2)}) %collective-permute-start.24) | collective-permute-done | bytes 262176 | tf_op jit(solution)/shard_map/ppermute | solution.py:21
  66.7 1.0 %collective-permute-start.25 = (bf16[64,2048]{1,0:T(8,128)(2,1)S(1)}, bf16[64,2048]{1,0:T(8,128)(2,1)S(1)}, u32[]{:S(2)}, u32[]{:S(2)}) collective-permute-start(bf16[64,2048]{1,0:T(8,128)(2,1)S(1)} %add.44), channel_id=1, source_target_pairs={{0,8},{2,10},{4,12},{6,14},{8,0},{10,2},{12,4},{14,6},{16,24},{18,... | collective-permute-start | bytes 786440 | tf_op jit(solution)/shard_map/ppermute | solution.py:21
  67.7 1.5 %collective-permute-start.22 = (bf16[64,2048]{1,0:T(8,128)(2,1)S(1)}, bf16[64,2048]{1,0:T(8,128)(2,1)S(1)}, u32[]{:S(2)}, u32[]{:S(2)}) collective-permute-start(bf16[64,2048]{1,0:T(8,128)(2,1)S(1)} %get-tuple-element.169), channel_id=1, source_target_pairs={{0,4},{2,6},{4,0},{6,2},{8,12},{10,14},{12,8},{14,10},{16,20},{18,... | collective-permute-start | bytes 786440 | tf_op jit(solution)/shard_map/ppermute | solution.py:21
  69.2 1.5 %collective-permute-start.28 = (bf16[256,768]{1,0:T(8,128)(2,1)S(1)}, bf16[256,768]{1,0:T(8,128)(2,1)S(1)}, u32[]{:S(2)}, u32[]{:S(2)}) collective-permute-start(bf16[256,768]{1,0:T(8,128)(2,1)S(1)} %get-tuple-element.154.refs_3_), channel_id=1, source_target_pairs={{0,1},{1,0},{2,3},{3,2},{4,5},{5,4},{6,7},{7,6},{8,9},{9,8},{10,11... | collective-permute-start | bytes 1179656 | tf_op jit(solution)/shard_map/ppermute | solution.py:21
  70.8 3.8 %collective-permute-done.25 = bf16[64,2048]{1,0:T(8,128)(2,1)S(1)} collective-permute-done((bf16[64,2048]{1,0:T(8,128)(2,1)S(1)}, bf16[64,2048]{1,0:T(8,128)(2,1)S(1)}, u32[]{:S(2)}, u32[]{:S(2)}) %collective-permute-start.25) | collective-permute-done | bytes 262176 | tf_op jit(solution)/shard_map/ppermute | solution.py:21
  74.5 0.4 collective-permute-done.22
  74.9 1.1 %collective-permute-start.27 = (bf16[64,2048]{1,0:T(8,128)(2,1)S(1)}, bf16[64,2048]{1,0:T(8,128)(2,1)S(1)}, u32[]{:S(2)}, u32[]{:S(2)}) collective-permute-start(bf16[64,2048]{1,0:T(8,128)(2,1)S(1)} %get-tuple-element.149), channel_id=1, source_target_pairs={{0,8},{2,10},{4,12},{6,14},{8,0},{10,2},{12,4},{14,6},{16,24},{18,... | collective-permute-start | bytes 786440 | tf_op jit(solution)/shard_map/ppermute | solution.py:21
  76.2 2.9 %collective-permute-start.30 = (bf16[64,2048]{1,0:T(8,128)(2,1)S(1)}, bf16[64,2048]{1,0:T(8,128)(2,1)S(1)}, u32[]{:S(2)}, u32[]{:S(2)}) collective-permute-start(bf16[64,2048]{1,0:T(8,128)(2,1)S(1)} %add_add_fusion), channel_id=1, source_target_pairs={{0,16},{2,18},{4,20},{6,22},{8,24},{10,26},{12,28},{14,30},{16,0},... | collective-permute-start | bytes 786440 | tf_op jit(solution)/shard_map/ppermute | solution.py:21
  79.1 1.5 %collective-permute-start.29 = (bf16[64,2048]{1,0:T(8,128)(2,1)S(1)}, bf16[64,2048]{1,0:T(8,128)(2,1)S(1)}, u32[]{:S(2)}, u32[]{:S(2)}) collective-permute-start(bf16[64,2048]{1,0:T(8,128)(2,1)S(1)} %add.45), channel_id=1, source_target_pairs={{0,4},{2,6},{4,0},{6,2},{8,12},{10,14},{12,8},{14,10},{16,20},{18,... | collective-permute-start | bytes 786440 | tf_op jit(solution)/shard_map/ppermute | solution.py:21
  80.6 3.9 %shard_map.97 = f32[1024,1,768]{2,1,0:T(1,128)} custom-call(bf16[256,1024]{1,0:T(8,128)(2,1)S(1)} %get-tuple-element.151.refs_0_, bf16[256,768]{1,0:T(8,128)(2,1)S(1)} %get-tuple-element.139.refs_1_, bf16[256,1024]{1,0:T(8,128)(2,1)S(1)} %get-tuple-element.153.refs_2_, bf16[256,768]{1,0:T(8,128)(2,1)S(1)} %get-tuple-element.154.refs_3_, ...), custom_call_target="tpu_custom_call" | custom-call | flops 1000000 | bytes 100000 | tf_op jit(solution)/shard_map/pallas_call | solution.py:247
  84.6 2.5 %collective-permute-done.27 = bf16[64,2048]{1,0:T(8,128)(2,1)S(1)} collective-permute-done((bf16[64,2048]{1,0:T(8,128)(2,1)S(1)}, bf16[64,2048]{1,0:T(8,128)(2,1)S(1)}, u32[]{:S(2)}, u32[]{:S(2)}) %collective-permute-start.27) | collective-permute-done | bytes 262176 | tf_op jit(solution)/shard_map/ppermute | solution.py:21
  87.4 1.3 %collective-permute-done.31 = bf16[32,2048]{1,0:T(8,128)(2,1)S(1)} collective-permute-done((bf16[32,2048]{1,0:T(8,128)(2,1)S(1)}, bf16[32,2048]{1,0:T(8,128)(2,1)S(1)}, u32[]{:S(2)}, u32[]{:S(2)}) %collective-permute-start.31) | collective-permute-done | bytes 131104 | tf_op jit(solution)/shard_map/ppermute | solution.py:21
  88.7 0.7 broadcast_select_fusion.2
  (45 shorter events, 1.3 us)
Async XLA Ops:
  1.6 2.3 %collective-permute-start = (bf16[32,2048]{1,0:T(8,128)(2,1)S(1)}, bf16[32,2048]{1,0:T(8,128)(2,1)S(1)}, u32[]{:S(2)}, u32[]{:S(2)}) collective-permute-start(bf16[32,2048]{1,0:T(8,128)(2,1)S(1)} %get-tuple-element.175), channel_id=1, source_target_pairs={{0,2},{2,0},{4,6},{6,4},{8,10},{10,8},{12,14},{14,12},{16,18},{18,... | collective-permute-start | bytes 393224 | tf_op jit(solution)/shard_map/ppermute | solution.py:21
  4.0 17.1 %collective-permute-start.2 = (bf16[64,2176]{1,0:T(8,128)(2,1)S(1)}, bf16[64,2176]{1,0:T(8,128)(2,1)S(1)}, u32[]{:S(2)}, u32[]{:S(2)}) collective-permute-start(bf16[64,2176]{1,0:T(8,128)(2,1)S(1)} %shard_map.94.refs_0_), channel_id=1, source_target_pairs={{0,16},{2,18},{4,20},{6,22},{8,24},{10,26},{12,28},{14,30},{16,0},... | collective-permute-start | bytes 835592 | tf_op jit(solution)/shard_map/ppermute | solution.py:21
  7.7 15.6 %collective-permute-start.1 = (bf16[64,2176]{1,0:T(8,128)(2,1)S(1)}, bf16[64,2176]{1,0:T(8,128)(2,1)S(1)}, u32[]{:S(2)}, u32[]{:S(2)}) collective-permute-start(bf16[64,2176]{1,0:T(8,128)(2,1)S(1)} %shard_map.94.refs_0_), channel_id=1, source_target_pairs={{0,4},{2,6},{4,0},{6,2},{8,12},{10,14},{12,8},{14,10},{16,20},{18,... | collective-permute-start | bytes 835592 | tf_op jit(solution)/shard_map/ppermute | solution.py:21
  9.2 15.5 %collective-permute-start.5 = (bf16[64,2176]{1,0:T(8,128)(2,1)S(1)}, bf16[64,2176]{1,0:T(8,128)(2,1)S(1)}, u32[]{:S(2)}, u32[]{:S(2)}) collective-permute-start(bf16[64,2176]{1,0:T(8,128)(2,1)S(1)} %shard_map.94.refs_0_), channel_id=1, source_target_pairs={{0,8},{2,10},{4,12},{6,14},{8,0},{10,2},{12,4},{14,6},{16,24},{18,... | collective-permute-start | bytes 835592 | tf_op jit(solution)/shard_map/ppermute | solution.py:21
  21.1 9.5 %collective-permute-start.4 = (bf16[64,2176]{1,0:T(8,128)(2,1)S(1)}, bf16[64,2176]{1,0:T(8,128)(2,1)S(1)}, u32[]{:S(2)}, u32[]{:S(2)}) collective-permute-start(bf16[64,2176]{1,0:T(8,128)(2,1)S(1)} %collective-permute-done.2.refs_2_), channel_id=1, source_target_pairs={{0,8},{2,10},{4,12},{6,14},{8,0},{10,2},{12,4},{14,6},{16,24},{18,... | collective-permute-start | bytes 835592 | tf_op jit(solution)/shard_map/ppermute | solution.py:21
  21.8 10.5 %collective-permute-start.3 = (bf16[64,2176]{1,0:T(8,128)(2,1)S(1)}, bf16[64,2176]{1,0:T(8,128)(2,1)S(1)}, u32[]{:S(2)}, u32[]{:S(2)}) collective-permute-start(bf16[64,2176]{1,0:T(8,128)(2,1)S(1)} %collective-permute-done.2.refs_2_), channel_id=1, source_target_pairs={{0,4},{2,6},{4,0},{6,2},{8,12},{10,14},{12,8},{14,10},{16,20},{18,... | collective-permute-start | bytes 835592 | tf_op jit(solution)/shard_map/ppermute | solution.py:21
  23.2 12.2 %collective-permute-start.6 = (bf16[64,2176]{1,0:T(8,128)(2,1)S(1)}, bf16[64,2176]{1,0:T(8,128)(2,1)S(1)}, u32[]{:S(2)}, u32[]{:S(2)}) collective-permute-start(bf16[64,2176]{1,0:T(8,128)(2,1)S(1)} %collective-permute-done.1.refs_1_), channel_id=1, source_target_pairs={{0,8},{2,10},{4,12},{6,14},{8,0},{10,2},{12,4},{14,6},{16,24},{18,... | collective-permute-start | bytes 835592 | tf_op jit(solution)/shard_map/ppermute | solution.py:21
  24.7 12.5 %collective-permute-start.8 = (bf16[64,2176]{1,0:T(8,128)(2,1)S(1)}, bf16[64,2176]{1,0:T(8,128)(2,1)S(1)}, u32[]{:S(2)}, u32[]{:S(2)}) collective-permute-start(bf16[64,2176]{1,0:T(8,128)(2,1)S(1)} %shard_map.94.refs_0_), channel_id=1, source_target_pairs={{0,2},{2,0},{4,6},{6,4},{8,10},{10,8},{12,14},{14,12},{16,18},{18,... | collective-permute-start | bytes 835592 | tf_op jit(solution)/shard_map/ppermute | solution.py:21
  24.7 12.5 %collective-permute-start.10 = (bf16[64,2176]{1,0:T(8,128)(2,1)S(1)}, bf16[64,2176]{1,0:T(8,128)(2,1)S(1)}, u32[]{:S(2)}, u32[]{:S(2)}) collective-permute-start(bf16[64,2176]{1,0:T(8,128)(2,1)S(1)} %collective-permute-done.2.refs_2_), channel_id=1, source_target_pairs={{0,2},{2,0},{4,6},{6,4},{8,10},{10,8},{12,14},{14,12},{16,18},{18,... | collective-permute-start | bytes 835592 | tf_op jit(solution)/shard_map/ppermute | solution.py:21
  30.6 6.5 %collective-permute-start.7 = (bf16[64,2176]{1,0:T(8,128)(2,1)S(1)}, bf16[64,2176]{1,0:T(8,128)(2,1)S(1)}, u32[]{:S(2)}, u32[]{:S(2)}) collective-permute-start(bf16[64,2176]{1,0:T(8,128)(2,1)S(1)} %collective-permute-done.4.refs_6_), channel_id=1, source_target_pairs={{0,4},{2,6},{4,0},{6,2},{8,12},{10,14},{12,8},{14,10},{16,20},{18,... | collective-permute-start | bytes 835592 | tf_op jit(solution)/shard_map/ppermute | solution.py:21
  32.2 5.0 %collective-permute-start.9 = (bf16[64,2176]{1,0:T(8,128)(2,1)S(1)}, bf16[64,2176]{1,0:T(8,128)(2,1)S(1)}, u32[]{:S(2)}, u32[]{:S(2)}) collective-permute-start(bf16[64,2176]{1,0:T(8,128)(2,1)S(1)} %collective-permute-done.1.refs_1_), channel_id=1, source_target_pairs={{0,2},{2,0},{4,6},{6,4},{8,10},{10,8},{12,14},{14,12},{16,18},{18,... | collective-permute-start | bytes 835592 | tf_op jit(solution)/shard_map/ppermute | solution.py:21
  35.5 1.7 %collective-permute-start.11 = (bf16[64,2176]{1,0:T(8,128)(2,1)S(1)}, bf16[64,2176]{1,0:T(8,128)(2,1)S(1)}, u32[]{:S(2)}, u32[]{:S(2)}) collective-permute-start(bf16[64,2176]{1,0:T(8,128)(2,1)S(1)} %collective-permute-done.3.refs_3_), channel_id=1, source_target_pairs={{0,2},{2,0},{4,6},{6,4},{8,10},{10,8},{12,14},{14,12},{16,18},{18,... | collective-permute-start | bytes 835592 | tf_op jit(solution)/shard_map/ppermute | solution.py:21
  37.3 18.2 %collective-permute-start.16 = (bf16[256,1024]{1,0:T(8,128)(2,1)S(1)}, bf16[256,1024]{1,0:T(8,128)(2,1)S(1)}, u32[]{:S(2)}, u32[]{:S(2)}) collective-permute-start(bf16[256,1024]{1,0:T(8,128)(2,1)S(1)} %shard_map.95), channel_id=1, source_target_pairs={{0,1},{1,0},{2,3},{3,2},{4,5},{5,4},{6,7},{7,6},{8,9},{9,8},{10,11... | collective-permute-start | bytes 1572872 | tf_op jit(solution)/shard_map/ppermute | solution.py:21
  38.9 1.6 %collective-permute-start.12 = (bf16[64,2176]{1,0:T(8,128)(2,1)S(1)}, bf16[64,2176]{1,0:T(8,128)(2,1)S(1)}, u32[]{:S(2)}, u32[]{:S(2)}) collective-permute-start(bf16[64,2176]{1,0:T(8,128)(2,1)S(1)} %collective-permute-done.5.refs_4_), channel_id=1, source_target_pairs={{0,2},{2,0},{4,6},{6,4},{8,10},{10,8},{12,14},{14,12},{16,18},{18,... | collective-permute-start | bytes 835592 | tf_op jit(solution)/shard_map/ppermute | solution.py:21
  38.9 2.0 %collective-permute-start.13 = (bf16[64,2176]{1,0:T(8,128)(2,1)S(1)}, bf16[64,2176]{1,0:T(8,128)(2,1)S(1)}, u32[]{:S(2)}, u32[]{:S(2)}) collective-permute-start(bf16[64,2176]{1,0:T(8,128)(2,1)S(1)} %collective-permute-done.6.refs_5_), channel_id=1, source_target_pairs={{0,2},{2,0},{4,6},{6,4},{8,10},{10,8},{12,14},{14,12},{16,18},{18,... | collective-permute-start | bytes 835592 | tf_op jit(solution)/shard_map/ppermute | solution.py:21
  39.4 1.8 %collective-permute-start.14 = (bf16[64,2176]{1,0:T(8,128)(2,1)S(1)}, bf16[64,2176]{1,0:T(8,128)(2,1)S(1)}, u32[]{:S(2)}, u32[]{:S(2)}) collective-permute-start(bf16[64,2176]{1,0:T(8,128)(2,1)S(1)} %collective-permute-done.4.refs_6_), channel_id=1, source_target_pairs={{0,2},{2,0},{4,6},{6,4},{8,10},{10,8},{12,14},{14,12},{16,18},{18,... | collective-permute-start | bytes 835592 | tf_op jit(solution)/shard_map/ppermute | solution.py:21
  39.4 2.2 %collective-permute-start.15 = (bf16[64,2176]{1,0:T(8,128)(2,1)S(1)}, bf16[64,2176]{1,0:T(8,128)(2,1)S(1)}, u32[]{:S(2)}, u32[]{:S(2)}) collective-permute-start(bf16[64,2176]{1,0:T(8,128)(2,1)S(1)} %collective-permute-done.7.refs_7_), channel_id=1, source_target_pairs={{0,2},{2,0},{4,6},{6,4},{8,10},{10,8},{12,14},{14,12},{16,18},{18,... | collective-permute-start | bytes 835592 | tf_op jit(solution)/shard_map/ppermute | solution.py:21
  55.5 2.0 %collective-permute-start.17 = (bf16[128,2048]{1,0:T(8,128)(2,1)S(1)}, bf16[128,2048]{1,0:T(8,128)(2,1)S(1)}, u32[]{:S(2)}, u32[]{:S(2)}) collective-permute-start(bf16[128,2048]{1,0:T(8,128)(2,1)S(1)} %get-tuple-element.125), channel_id=1, source_target_pairs={{0,2},{2,0},{4,6},{6,4},{8,10},{10,8},{12,14},{14,12},{16,18},{18,... | collective-permute-start | bytes 1572872 | tf_op jit(solution)/shard_map/ppermute | solution.py:21
  55.6 4.4 %collective-permute-start.20 = (bf16[128,2048]{1,0:T(8,128)(2,1)S(1)}, bf16[128,2048]{1,0:T(8,128)(2,1)S(1)}, u32[]{:S(2)}, u32[]{:S(2)}) collective-permute-start(bf16[128,2048]{1,0:T(8,128)(2,1)S(1)} %get-tuple-element.132), channel_id=1, source_target_pairs={{0,2},{2,0},{4,6},{6,4},{8,10},{10,8},{12,14},{14,12},{16,18},{18,... | collective-permute-start | bytes 1572872 | tf_op jit(solution)/shard_map/ppermute | solution.py:21
  56.1 4.1 %collective-permute-start.23 = (bf16[256,1024]{1,0:T(8,128)(2,1)S(1)}, bf16[256,1024]{1,0:T(8,128)(2,1)S(1)}, u32[]{:S(2)}, u32[]{:S(2)}) collective-permute-start(bf16[256,1024]{1,0:T(8,128)(2,1)S(1)} %collective-permute-done.16), channel_id=1, source_target_pairs={{0,2},{2,0},{4,6},{6,4},{8,10},{10,8},{12,14},{14,12},{16,18},{18,... | collective-permute-start | bytes 1572872 | tf_op jit(solution)/shard_map/ppermute | solution.py:21
  57.7 3.4 %collective-permute-start.19 = (bf16[128,2048]{1,0:T(8,128)(2,1)S(1)}, bf16[128,2048]{1,0:T(8,128)(2,1)S(1)}, u32[]{:S(2)}, u32[]{:S(2)}) collective-permute-start(bf16[128,2048]{1,0:T(8,128)(2,1)S(1)} %get-tuple-element.130), channel_id=1, source_target_pairs={{0,2},{2,0},{4,6},{6,4},{8,10},{10,8},{12,14},{14,12},{16,18},{18,... | collective-permute-start | bytes 1572872 | tf_op jit(solution)/shard_map/ppermute | solution.py:21
  57.9 12.9 %collective-permute-start.21 = (bf16[256,768]{1,0:T(8,128)(2,1)S(1)}, bf16[256,768]{1,0:T(8,128)(2,1)S(1)}, u32[]{:S(2)}, u32[]{:S(2)}) collective-permute-start(bf16[256,768]{1,0:T(8,128)(2,1)S(1)} %get-tuple-element.139.refs_1_), channel_id=1, source_target_pairs={{0,1},{1,0},{2,3},{3,2},{4,5},{5,4},{6,7},{7,6},{8,9},{9,8},{10,11... | collective-permute-start | bytes 1179656 | tf_op jit(solution)/shard_map/ppermute | solution.py:21
  58.3 8.3 %collective-permute-start.24 = (bf16[64,2048]{1,0:T(8,128)(2,1)S(1)}, bf16[64,2048]{1,0:T(8,128)(2,1)S(1)}, u32[]{:S(2)}, u32[]{:S(2)}) collective-permute-start(bf16[64,2048]{1,0:T(8,128)(2,1)S(1)} %get-tuple-element.171), channel_id=1, source_target_pairs={{0,4},{2,6},{4,0},{6,2},{8,12},{10,14},{12,8},{14,10},{16,20},{18,... | collective-permute-start | bytes 786440 | tf_op jit(solution)/shard_map/ppermute | solution.py:21
  59.9 1.9 %collective-permute-start.18 = (bf16[128,2048]{1,0:T(8,128)(2,1)S(1)}, bf16[128,2048]{1,0:T(8,128)(2,1)S(1)}, u32[]{:S(2)}, u32[]{:S(2)}) collective-permute-start(bf16[128,2048]{1,0:T(8,128)(2,1)S(1)} %get-tuple-element.128), channel_id=1, source_target_pairs={{0,2},{2,0},{4,6},{6,4},{8,10},{10,8},{12,14},{14,12},{16,18},{18,... | collective-permute-start | bytes 1572872 | tf_op jit(solution)/shard_map/ppermute | solution.py:21
  60.1 10.6 %collective-permute-start.26 = (bf16[64,2048]{1,0:T(8,128)(2,1)S(1)}, bf16[64,2048]{1,0:T(8,128)(2,1)S(1)}, u32[]{:S(2)}, u32[]{:S(2)}) collective-permute-start(bf16[64,2048]{1,0:T(8,128)(2,1)S(1)} %get-tuple-element.165), channel_id=1, source_target_pairs={{0,8},{2,10},{4,12},{6,14},{8,0},{10,2},{12,4},{14,6},{16,24},{18,... | collective-permute-start | bytes 786440 | tf_op jit(solution)/shard_map/ppermute | solution.py:21
  66.7 7.8 %collective-permute-start.25 = (bf16[64,2048]{1,0:T(8,128)(2,1)S(1)}, bf16[64,2048]{1,0:T(8,128)(2,1)S(1)}, u32[]{:S(2)}, u32[]{:S(2)}) collective-permute-start(bf16[64,2048]{1,0:T(8,128)(2,1)S(1)} %add.44), channel_id=1, source_target_pairs={{0,8},{2,10},{4,12},{6,14},{8,0},{10,2},{12,4},{14,6},{16,24},{18,... | collective-permute-start | bytes 786440 | tf_op jit(solution)/shard_map/ppermute | solution.py:21
  67.7 7.2 %collective-permute-start.22 = (bf16[64,2048]{1,0:T(8,128)(2,1)S(1)}, bf16[64,2048]{1,0:T(8,128)(2,1)S(1)}, u32[]{:S(2)}, u32[]{:S(2)}) collective-permute-start(bf16[64,2048]{1,0:T(8,128)(2,1)S(1)} %get-tuple-element.169), channel_id=1, source_target_pairs={{0,4},{2,6},{4,0},{6,2},{8,12},{10,14},{12,8},{14,10},{16,20},{18,... | collective-permute-start | bytes 786440 | tf_op jit(solution)/shard_map/ppermute | solution.py:21
  69.2 11.4 %collective-permute-start.28 = (bf16[256,768]{1,0:T(8,128)(2,1)S(1)}, bf16[256,768]{1,0:T(8,128)(2,1)S(1)}, u32[]{:S(2)}, u32[]{:S(2)}) collective-permute-start(bf16[256,768]{1,0:T(8,128)(2,1)S(1)} %get-tuple-element.154.refs_3_), channel_id=1, source_target_pairs={{0,1},{1,0},{2,3},{3,2},{4,5},{5,4},{6,7},{7,6},{8,9},{9,8},{10,11... | collective-permute-start | bytes 1179656 | tf_op jit(solution)/shard_map/ppermute | solution.py:21
  74.9 12.2 %collective-permute-start.27 = (bf16[64,2048]{1,0:T(8,128)(2,1)S(1)}, bf16[64,2048]{1,0:T(8,128)(2,1)S(1)}, u32[]{:S(2)}, u32[]{:S(2)}) collective-permute-start(bf16[64,2048]{1,0:T(8,128)(2,1)S(1)} %get-tuple-element.149), channel_id=1, source_target_pairs={{0,8},{2,10},{4,12},{6,14},{8,0},{10,2},{12,4},{14,6},{16,24},{18,... | collective-permute-start | bytes 786440 | tf_op jit(solution)/shard_map/ppermute | solution.py:21
  76.2 11.0 %collective-permute-start.30 = (bf16[64,2048]{1,0:T(8,128)(2,1)S(1)}, bf16[64,2048]{1,0:T(8,128)(2,1)S(1)}, u32[]{:S(2)}, u32[]{:S(2)}) collective-permute-start(bf16[64,2048]{1,0:T(8,128)(2,1)S(1)} %add_add_fusion), channel_id=1, source_target_pairs={{0,16},{2,18},{4,20},{6,22},{8,24},{10,26},{12,28},{14,30},{16,0},... | collective-permute-start | bytes 786440 | tf_op jit(solution)/shard_map/ppermute | solution.py:21
  79.1 8.1 %collective-permute-start.29 = (bf16[64,2048]{1,0:T(8,128)(2,1)S(1)}, bf16[64,2048]{1,0:T(8,128)(2,1)S(1)}, u32[]{:S(2)}, u32[]{:S(2)}) collective-permute-start(bf16[64,2048]{1,0:T(8,128)(2,1)S(1)} %add.45), channel_id=1, source_target_pairs={{0,4},{2,6},{4,0},{6,2},{8,12},{10,14},{12,8},{14,10},{16,20},{18,... | collective-permute-start | bytes 786440 | tf_op jit(solution)/shard_map/ppermute | solution.py:21
  87.3 1.4 %collective-permute-start.31 = (bf16[32,2048]{1,0:T(8,128)(2,1)S(1)}, bf16[32,2048]{1,0:T(8,128)(2,1)S(1)}, u32[]{:S(2)}, u32[]{:S(2)}) collective-permute-start(bf16[32,2048]{1,0:T(8,128)(2,1)S(1)} %broadcast_select_fusion.4), channel_id=1, source_target_pairs={{0,2},{2,0},{4,6},{6,4},{8,10},{10,8},{12,14},{14,12},{16,18},{18,... | collective-permute-start | bytes 393224 | tf_op jit(solution)/shard_map/ppermute | solution.py:21
